TPU v7x, 32 devices: a whole 2x2x4 slice. The times are simulated.
32 devices in a mesh: gx: 4 (over y, x), gy: 4 (over z), gz: 2 (over core).
Axes of the slice: x: 2, y: 2, z: 4, core: 2. Of those that a mesh axis runs over, the one named last changes fastest.
Arguments:
- displacement: float32 [3, 4096], P(None, ('gx', 'gy', 'gz')), may hold values from -6 to 6
- reference_image: bfloat16 [4096, 512], P(('gx', 'gy', 'gz')), may hold values from -6 to 6
- image_gradient: bfloat16 [3, 4096, 512], P(None, ('gx', 'gy', 'gz')), may hold values from -6 to 6
- deformed_blocks: bfloat16 [4096, 4096], P(('gx', 'gy', 'gz')), may hold values from -6 to 6
- fractions: bfloat16 [24, 4096], P(None, ('gx', 'gy', 'gz')), may hold values from 0 to 1
- offsets: int32 [3, 4096], P(None, ('gx', 'gy', 'gz')), may hold values from 0 to 7
- send_list: int32 [16384], P(('gx', 'gy', 'gz')), may hold values from 0 to 127, as said below
- recv_slot: int32 [4096], P(('gx', 'gy', 'gz')), may hold values from 0 to 511, as said below
Outputs:
- gradient: float32 [3, 4096], P(None, ('gx', 'gy', 'gz'))
Inputs may be any that keep to these rules, and one draw needn't show every extreme that they name: `recv_slot`: within one device the 128 entries are distinct slots; slot s is served by the device with the same gx index whose gy+gz index is s // 64. `send_list`: entry p * 64 + k of a device is the block, among that device's 128 rows of deformed_blocks, read by the device of the same gx index with gy+gz index p through its slot (this device's gy+gz index) * 64 + k; entries that no slot reads name arbitrary blocks.
All inputs are finite; a program needn't handle non-finite values.
Results may differ from a plain program's by a relative error of at most 0.00039.
Values may be sent and summed in bfloat16 or wider, within the bound.
No kernel may reach another device: no remote copies, remote signals or barrier semaphores. Data moves between devices by JAX's collectives and lax.ppermute only.
A program may use at most 64 MiB of HBM per device.

v0:
```python
import jax
import jax.numpy as jnp
from jax import lax
from jax.sharding import PartitionSpec as P

CX = 2
CY = 8
CZ = 8


shear_modulus = 0.05
lame_first = 1.0
data_weight = 0.0625
highest = lax.Precision.HIGHEST


def padded_2(cells, sides, width):
    for axis, dim in sides:
        count = lax.axis_size(axis)
        ends = count - 1
        head = lax.slice_in_dim(cells, 0, width, axis=dim)
        tail = lax.slice_in_dim(cells, cells.shape[dim] - width, cells.shape[dim], axis=dim)
        cells = jnp.concatenate(
            [
                lax.ppermute(tail, axis, [(i, (i + 1) % count) for i in range(ends)]),
                cells,
                lax.ppermute(head, axis, [((i + 1) % count, i) for i in range(ends)]),
            ],
            axis=dim,
        )
    return cells


def from_behind(block, axis, distance):
    devices = range(lax.axis_size(axis))
    route = [(i - distance, i) for i in devices if i - distance in devices]
    return lax.ppermute(block, axis, route)


def shape_table():
    centres = (jnp.arange(8, dtype=jnp.float32) + 0.5) / 8.0
    weights = jnp.stack([1.0 - centres, centres], axis=1)
    values = (
        weights[:, None, None, :, None, None]
        * weights[None, :, None, None, :, None]
        * weights[None, None, :, None, None, :]
    )
    return values.reshape(512, 8)


def interpolate(voxels, fraction, offset):
    number = voxels.shape[0]
    volume = voxels.astype(jnp.float32).reshape(number, 16, 16, 16)
    starts = offset[:, :, None] + jnp.arange(8, dtype=jnp.int32)[None, None, :]
    columns = jnp.arange(16, dtype=jnp.int32)
    upper_weight = jnp.swapaxes(fraction.astype(jnp.float32), 1, 2)[..., None]
    lower_hit = (columns == starts[..., None]).astype(jnp.float32)
    upper_hit = (columns == starts[..., None] + 1).astype(jnp.float32)
    matrices = (1.0 - upper_weight) * lower_hit + upper_weight * upper_hit
    partial_z = jnp.einsum("nkc,nabc->nabk", matrices[2], volume, precision=highest)
    partial_y = jnp.einsum("njb,nabk->najk", matrices[1], partial_z, precision=highest)
    result = jnp.einsum("nia,najk->nijk", matrices[0], partial_y, precision=highest)
    return result.reshape(number, 512).astype(jnp.bfloat16)


def element_forces(samples, image, slopes, shape_values):
    difference = image.astype(jnp.float32) - samples.astype(jnp.float32)
    weighted = slopes.astype(jnp.float32) * difference[None]
    number = image.shape[0]
    return jnp.dot(weighted.reshape(3 * number, 512), shape_values, precision=highest).reshape(
        3, number, 8
    )


def displaced(padded, vector):
    return padded[
        :,
        1 + vector[0] : padded.shape[1] - 1 + vector[0],
        1 + vector[1] : padded.shape[2] - 1 + vector[1],
        1 + vector[2] : padded.shape[3] - 1 + vector[2],
    ]


def combined(outer_step, inner_step, sign_outer, sign_inner):
    return tuple(
        (
            sign_outer * outer_step[position] + sign_inner * inner_step[position]
            for position in range(3)
        )
    )


def navier(padded):
    unit_steps = ((1, 0, 0), (0, 1, 0), (0, 0, 1))
    centre = displaced(padded, (0, 0, 0))
    laplace = -6.0 * centre
    for unit_step in unit_steps:
        laplace = (
            laplace
            + displaced(padded, unit_step)
            + displaced(padded, combined(unit_step, unit_step, -1, 0))
        )
    gathered_rows = []
    for outer_axis in range(3):
        accumulated = jnp.zeros_like(centre[0])
        for inner_axis in range(3):
            outer_step = unit_steps[outer_axis]
            inner_step = unit_steps[inner_axis]
            if outer_axis == inner_axis:
                element_term = (
                    displaced(padded, outer_step)[inner_axis]
                    + displaced(padded, combined(outer_step, outer_step, -1, 0))[inner_axis]
                    - 2.0 * centre[inner_axis]
                )
            else:
                element_term = 0.25 * (
                    displaced(padded, combined(outer_step, inner_step, 1, 1))[inner_axis]
                    - displaced(padded, combined(outer_step, inner_step, 1, -1))[inner_axis]
                    - displaced(padded, combined(outer_step, inner_step, -1, 1))[inner_axis]
                    + displaced(padded, combined(outer_step, inner_step, -1, -1))[inner_axis]
                )
            accumulated = accumulated + element_term
        gathered_rows.append(accumulated)
    divergence_grad = jnp.stack(gathered_rows)
    return -(shear_modulus * laplace + (lame_first + shear_modulus) * divergence_grad)


def to_peers(payload):
    return lax.all_to_all(payload, ("gy", "gz"), split_axis=0, concat_axis=0, tiled=True)


def shifted_layer(upper_part, arriving, axis):
    length = upper_part.shape[axis]
    return jnp.concatenate(
        [jnp.expand_dims(arriving, axis), lax.slice_in_dim(upper_part, 0, length - 1, axis=axis)],
        axis=axis,
    )


def local(
    displacement,
    reference_image,
    image_gradient,
    deformed_blocks,
    fractions,
    offsets,
    send_list,
    recv_slot,
):
    per_device = reference_image.shape[0]
    shape_values = shape_table()
    grid = displacement.reshape(3, CX, CY, CZ)
    padded = padded_2(grid, (("gx", 1), ("gy", 2), ("gz", 3)), 1)
    stiffness = navier(padded)
    outgoing = jnp.take(deformed_blocks, send_list, axis=0)
    arrived = to_peers(outgoing)
    samples = interpolate(
        jnp.take(arrived, recv_slot, axis=0), fractions.reshape(3, 8, per_device), offsets
    )
    forces = element_forces(samples, reference_image, image_gradient, shape_values)
    corners = forces.reshape(3, CX, CY, CZ, 2, 2, 2).transpose(0, 4, 5, 6, 1, 2, 3)
    carried = corners[:, 1]
    arriving = from_behind(lax.index_in_dim(carried, CX - 1, 3, keepdims=False), "gx", 1)
    after_x = corners[:, 0] + shifted_layer(carried, arriving, 3)
    carried = after_x[:, 1]
    arriving = from_behind(lax.index_in_dim(carried, CY - 1, 3, keepdims=False), "gy", 1)
    after_y = after_x[:, 0] + shifted_layer(carried, arriving, 3)
    carried = after_y[:, 1]
    arriving = from_behind(lax.index_in_dim(carried, CZ - 1, 3, keepdims=False), "gz", 1)
    data_force = after_y[:, 0] + shifted_layer(carried, arriving, 3)
    return (data_force * data_weight + stiffness).reshape(3, per_device)


def solution(mesh):
    in_specs = (
        P(None, ("gx", "gy", "gz")),
        P(("gx", "gy", "gz"), None),
        P(None, ("gx", "gy", "gz"), None),
        P(("gx", "gy", "gz"), None),
        P(None, ("gx", "gy", "gz")),
        P(None, ("gx", "gy", "gz")),
        P(("gx", "gy", "gz")),
        P(("gx", "gy", "gz")),
    )
    out_specs = P(None, ("gx", "gy", "gz"))
    return jax.shard_map(local, mesh=mesh, in_specs=in_specs, out_specs=out_specs, check_vma=False)
```

profile of v0, /device:TPU:13, one launch (start us, length us, event | category | flops | bytes accessed | tf_op | source)
XLA Modules:
  0.0 314.6 jit_solution(12539835171433226531)
XLA Ops:
  0.0 0.8 compare_select_fusion
  0.8 0.7 compare_and_fusion
  1.6 4.3 %gather_fusion = bf16[512,4096]{1,0:T(8,128)(2,1)} fusion(bf16[128,4096]{1,0:T(8,128)(2,1)S(1)} %copy-done, s32[1024]{0:T(1024)S(1)} %pad_clamp_fusion.1), kind=kCustom, calls=%fused_computation | custom fusion | bytes 8390656 | tf_op jit(solution)/shard_map/jit(_take)/gather | solution.py:155
  5.9 4.6 %broadcast_select_fusion = bf16[8,64,4096]{2,1,0:T(8,128)(2,1)} fusion(bf16[8,64,4096]{2,1,0:T(8,128)(2,1)} %bitcast.83, pred[8,64]{1,0:T(8,128)(4,1)S(1)} %broadcast_in_dim.47), kind=kLoop, calls=%fused_computation.2 | loop fusion | flops 2097152 | bytes 8389120 | tf_op jit(solution)/shard_map/jit(_take)/select_n | solution.py:155
  10.6 5.8 %all-to-all-start = ((bf16[8,64,4096]{2,1,0:T(8,128)(2,1)}), bf16[8,64,4096]{2,1,0:T(8,128)(2,1)}, u32[]{:S(2)}, u32[]{:S(2)}) async-start(bf16[8,64,4096]{2,1,0:T(8,128)(2,1)} %broadcast_select_fusion), calls=%async_computation | async-start | bytes 8388608 | tf_op jit(solution)/shard_map/all_to_all | solution.py:129
  16.5 3.1 collective-permute-start.4
  19.6 3.1 collective-permute-start.3
  22.7 0.1 copy.44
  23.0 0.1 broadcast_multiply_fusion
  23.1 0.1 iota_add_fusion
  23.2 1.7 select_add_fusion
  25.0 2.0 collective-permute-start.5
  27.0 3.3 %collective-permute-start.6 = (f32[3,4,1,8]{3,2,1,0:T(1,128)S(1)}, f32[3,4,1,8]{3,2,1,0:T(1,128)S(1)}, u32[]{:S(2)}, u32[]{:S(2)}) collective-permute-start(f32[3,4,1,8]{3,2,1,0:T(1,128)S(1)} %get-tuple-element.17), channel_id=1, source_target_pairs={{0,2},{2,4},{4,6},{1,3},{3,5},{5,7},{8,10},{10,12},{12,14},{9,11},... | collective-permute-start | bytes 1160 | tf_op jit(solution)/shard_map/ppermute | solution.py:25
  30.4 0.8 copy.43
  31.1 0.2 mul.154
  31.3 77.0 %collective-permute-done.5 = f32[3,4,1,8]{3,2,1,0:T(1,128)S(1)} collective-permute-done((f32[3,4,1,8]{3,2,1,0:T(1,128)S(1)}, f32[3,4,1,8]{3,2,1,0:T(1,128)S(1)}, u32[]{:S(2)}, u32[]{:S(2)}) %collective-permute-start.5) | collective-permute-done | bytes 416 | tf_op jit(solution)/shard_map/ppermute | solution.py:27
  108.4 3.1 collective-permute-start.7
  111.5 1.3 collective-permute-start.8
  112.8 0.6 reshape.148
  113.4 0.7 mul.167
  114.1 0.7 mul.171
  114.8 1.4 fusion.27
  116.2 5.9 %gather_fusion.1 = bf16[128,4096]{1,0:T(8,128)(2,1)} fusion(bf16[512,4096]{1,0:T(8,128)(2,1)} %bitcast.6, s32[1024]{0:T(1024)S(1)} %pad_clamp_fusion), kind=kCustom, calls=%fused_computation.1 | custom fusion | bytes 2097664 | tf_op jit(solution)/shard_map/jit(_take)/gather | solution.py:158
  122.1 13.8 %copy.45 = bf16[128,4096]{0,1:T(8,128)(2,1)} copy(bf16[128,4096]{1,0:T(8,128)(2,1)} %gather_fusion.1) | data formatting | bytes 2097152 | tf_op jit(solution)/shard_map/jit(_take)/gather | solution.py:158
  135.9 2.4 broadcast_select_fusion.1
  138.3 12.6 %copy.46 = bf16[128,16,16,16]{3,2,1,0:T(8,128)(2,1)} copy(bf16[128,16,16,16]{0,3,2,1:T(8,128)(2,1)} %broadcast_select_fusion.1) | data formatting | bytes 2097152 | tf_op jit(solution)/shard_map/jit(_take)/select_n | solution.py:158
  150.9 60.8 %fusion = f32[128,16,16,8]{2,3,1,0:T(8,128)S(1)} fusion(bf16[128,16,16,16]{3,2,1,0:T(8,128)(2,1)} %copy.46, f32[3,128,8,16]{3,2,1,0:T(8,128)S(1)} %select_add_fusion), kind=kOutput, calls=%fused_computation.12 | convolution fusion | flops 50331648 | bytes 2621440 | tf_op jit(solution)/shard_map/nkc,nabc->nabk/dot_general | solution.py:60
  211.7 9.5 %convolution_bitcast_fusion = f32[128,16,8,8]{2,3,1,0:T(8,128)} fusion(f32[128,16,16,8]{2,3,1,0:T(8,128)S(1)} %fusion, f32[3,128,8,16]{3,2,1,0:T(8,128)S(1)} %select_add_fusion), kind=kOutput, calls=%fused_computation.3 | convolution fusion | flops 25165824 | bytes 9437184 | tf_op jit(solution)/shard_map/njb,nabk->najk/dot_general | solution.py:61
  221.2 7.2 %copy.47 = f32[128,16,8,8]{1,3,2,0:T(8,128)} copy(f32[128,16,8,8]{2,3,1,0:T(8,128)} %convolution_bitcast_fusion) | data formatting | bytes 1048576 | tf_op jit(solution)/shard_map/njb,nabk->najk/transpose | solution.py:61
  228.5 57.7 %fusion.1 = bf16[128,8,8,8]{3,1,2,0:T(8,128)(2,1)S(1)} fusion(f32[128,16,8,8]{1,3,2,0:T(8,128)} %copy.47, f32[3,128,8,16]{3,2,1,0:T(8,128)} %copy-done.1), kind=kOutput, calls=%fused_computation.14 | convolution fusion | flops 12582912 | bytes 4849664 | tf_op jit(solution)/shard_map/nia,najk->nijk/dot_general | solution.py:62
  286.2 2.2 copy.48
  288.5 1.0 convert_subtract_fusion
  289.4 0.1 copy.49
  289.6 1.1 convert_multiply_fusion
  290.7 6.9 %convolution_bitcast_fusion.1 = f32[3,2,2,2,2,8,8]{6,3,2,1,5,4,0:T(2,128)S(1)} fusion(f32[3,2,8,8,512,1,1]{4,3,6,5,2,1,0:T(8,128)S(1)} %bitcast.86, f32[2,2,2,512,1,1,1]{3,2,1,0,4,5,6:T(2,128)} %reshape.148), kind=kOutput, calls=%fused_computation.7 | convolution fusion | flops 18874368 | bytes 815104 | tf_op jit(solution)/shard_map/dot_general | solution.py:70
  297.6 3.1 collective-permute-start
  300.8 0.9 fusion.20
  301.7 1.7 collective-permute-done
  303.5 2.0 collective-permute-start.1
  305.5 0.1 fusion.37
  305.6 2.2 collective-permute-done.1
  308.0 0.2 slice_reduce_fusion
  308.1 1.3 collective-permute-start.2
  309.4 0.1 pad_maximum_fusion.1
  309.6 3.9 %collective-permute-done.2 = f32[3,2,8]{2,1,0:T(2,128)S(1)} collective-permute-done((f32[3,2,8]{2,1,0:T(2,128)S(1)}, f32[3,2,8]{2,1,0:T(2,128)S(1)}, u32[]{:S(2)}, u32[]{:S(2)}) %collective-permute-start.2) | collective-permute-done | bytes 224 | tf_op jit(solution)/shard_map/ppermute | solution.py:37
  313.5 0.1 copy.56
  313.6 0.1 fusion.11
  313.7 0.7 reshape.123
  (66 shorter events, 0.8 us)
Async XLA Ops:
  0.0 1.6 copy-start
  10.6 5.8 %copy-start.11 = (f32[3,128]{1,0:T(4,128)S(1)}, f32[3,128]{1,0:T(4,128)}, u32[]{:S(2)}) copy-start(f32[3,128]{1,0:T(4,128)} %param.8) | copy-start | bytes 4612
  10.6 12.1 %copy-start.12 = (bf16[24,128]{1,0:T(8,128)(2,1)S(1)}, bf16[24,128]{1,0:T(8,128)(2,1)}, u32[]{:S(2)}) copy-start(bf16[24,128]{1,0:T(8,128)(2,1)} %param.12) | copy-start | bytes 18436
  10.6 12.3 %copy-start.14 = (s32[128]{0:T(128)S(1)}, s32[128]{0:T(128)}, u32[]{:S(2)}) copy-start(s32[128]{0:T(128)} %param.15) | copy-start | bytes 1540
  10.6 12.5 %copy-start.13 = (s32[3,128]{1,0:T(4,128)S(1)}, s32[3,128]{1,0:T(4,128)}, u32[]{:S(2)}) copy-start(s32[3,128]{1,0:T(4,128)} %param.13) | copy-start | bytes 4612
  10.6 19.8 %copy-start.4 = (bf16[128,512]{1,0:T(8,128)(2,1)S(1)}, bf16[128,512]{1,0:T(8,128)(2,1)}, u32[]{:S(2)}) copy-start(bf16[128,512]{1,0:T(8,128)(2,1)} %param.9) | copy-start | bytes 393220
  10.6 105.6 %all-to-all-start = ((bf16[8,64,4096]{2,1,0:T(8,128)(2,1)}), bf16[8,64,4096]{2,1,0:T(8,128)(2,1)}, u32[]{:S(2)}, u32[]{:S(2)}) async-start(bf16[8,64,4096]{2,1,0:T(8,128)(2,1)} %broadcast_select_fusion), calls=%async_computation | async-start | bytes 8388608 | tf_op jit(solution)/shard_map/all_to_all | solution.py:129
  16.5 8.5 %collective-permute-start.4 = (f32[3,1,8,8]{3,2,1,0:T(8,128)S(1)}, f32[3,1,8,8]{3,2,1,0:T(8,128)S(1)}, u32[]{:S(2)}, u32[]{:S(2)}) collective-permute-start(f32[3,1,8,8]{3,2,1,0:T(8,128)S(1)} %get-tuple-element.22), channel_id=1, source_target_pairs={{0,8},{8,16},{16,24},{1,9},{9,17},{17,25},{2,10},{10,18},{18,26},{... | collective-permute-start | bytes 2312 | tf_op jit(solution)/shard_map/ppermute | solution.py:25
  19.6 5.4 %collective-permute-start.3 = (f32[3,1,8,8]{3,2,1,0:T(8,128)S(1)}, f32[3,1,8,8]{3,2,1,0:T(8,128)S(1)}, u32[]{:S(2)}, u32[]{:S(2)}) collective-permute-start(f32[3,1,8,8]{3,2,1,0:T(8,128)S(1)} %get-tuple-element.21), channel_id=1, source_target_pairs={{8,0},{16,8},{24,16},{9,1},{17,9},{25,17},{10,2},{18,10},{26,18},{... | collective-permute-start | bytes 2312 | tf_op jit(solution)/shard_map/ppermute | solution.py:27
  24.9 186.8 %copy-start.1 = (f32[3,128,8,16]{3,2,1,0:T(8,128)}, f32[3,128,8,16]{3,2,1,0:T(8,128)S(1)}, u32[]{:S(2)}) copy-start(f32[3,128,8,16]{3,2,1,0:T(8,128)S(1)} %select_add_fusion) | copy-start | bytes 589828
  25.0 83.3 %copy-start.7 = (f32[3,3,8,8]{3,2,1,0:T(8,128)}, f32[3,3,8,8]{3,2,1,0:T(8,128)S(1)}, u32[]{:S(2)}) copy-start(f32[3,3,8,8]{3,2,1,0:T(8,128)S(1)} %get-tuple-element.20) | copy-start | bytes 6916
  25.0 97.1 %copy-start.5 = (f32[3,3,8,8]{3,2,1,0:T(8,128)}, f32[3,3,8,8]{3,2,1,0:T(8,128)S(1)}, u32[]{:S(2)}) copy-start(f32[3,3,8,8]{3,2,1,0:T(8,128)S(1)} %get-tuple-element.23) | copy-start | bytes 6916
  25.0 83.2 %collective-permute-start.5 = (f32[3,4,1,8]{3,2,1,0:T(1,128)S(1)}, f32[3,4,1,8]{3,2,1,0:T(1,128)S(1)}, u32[]{:S(2)}, u32[]{:S(2)}) collective-permute-start(f32[3,4,1,8]{3,2,1,0:T(1,128)S(1)} %get-tuple-element.16), channel_id=1, source_target_pairs={{2,0},{4,2},{6,4},{3,1},{5,3},{7,5},{10,8},{12,10},{14,12},{11,9},... | collective-permute-start | bytes 1160 | tf_op jit(solution)/shard_map/ppermute | solution.py:27
  27.0 81.2 %collective-permute-start.6 = (f32[3,4,1,8]{3,2,1,0:T(1,128)S(1)}, f32[3,4,1,8]{3,2,1,0:T(1,128)S(1)}, u32[]{:S(2)}, u32[]{:S(2)}) collective-permute-start(f32[3,4,1,8]{3,2,1,0:T(1,128)S(1)} %get-tuple-element.17), channel_id=1, source_target_pairs={{0,2},{2,4},{4,6},{1,3},{3,5},{5,7},{8,10},{10,12},{12,14},{9,11},... | collective-permute-start | bytes 1160 | tf_op jit(solution)/shard_map/ppermute | solution.py:25
  108.2 13.9 %copy-start.2 = (f32[3,4,1,8]{3,2,1,0:T(1,128)}, f32[3,4,1,8]{3,2,1,0:T(1,128)S(1)}, u32[]{:S(2)}) copy-start(f32[3,4,1,8]{3,2,1,0:T(1,128)S(1)} %collective-permute-done.6) | copy-start | bytes 1156
  108.4 6.4 %collective-permute-start.7 = (f32[3,4,10,1]{3,2,1,0:T(8,128)S(1)}, f32[3,4,10,1]{3,2,1,0:T(8,128)S(1)}, u32[]{:S(2)}, u32[]{:S(2)}) collective-permute-start(f32[3,4,10,1]{3,2,1,0:T(8,128)S(1)} %get-tuple-element.10), channel_id=1, source_target_pairs={{1,0},{3,2},{5,4},{7,6},{9,8},{11,10},{13,12},{15,14},{17,16},{19,... | collective-permute-start | bytes 1448 | tf_op jit(solution)/shard_map/ppermute | solution.py:27
  111.5 3.3 %collective-permute-start.8 = (f32[3,4,10,1]{3,2,1,0:T(8,128)S(1)}, f32[3,4,10,1]{3,2,1,0:T(8,128)S(1)}, u32[]{:S(2)}, u32[]{:S(2)}) collective-permute-start(f32[3,4,10,1]{3,2,1,0:T(8,128)S(1)} %get-tuple-element.11), channel_id=1, source_target_pairs={{0,1},{2,3},{4,5},{6,7},{8,9},{10,11},{12,13},{14,15},{16,17},{18,... | collective-permute-start | bytes 1448 | tf_op jit(solution)/shard_map/ppermute | solution.py:25
  288.4 17.1 %copy-start.3 = (f32[3,4,1,8]{3,2,1,0:T(1,128)S(1)}, f32[3,4,1,8]{3,2,1,0:T(1,128)}, u32[]{:S(2)}) copy-start(f32[3,4,1,8]{3,2,1,0:T(1,128)} %copy-done.2) | copy-start | bytes 1156
  288.4 17.1 %copy-start.10 = (f32[1,2,8,8]{3,2,1,0:T(8,128)S(1)}, f32[1,2,8,8]{3,2,1,0:T(8,128)}, u32[]{:S(2)}) copy-start(f32[1,2,8,8]{3,2,1,0:T(8,128)} %mul.171) | copy-start | bytes 1540
  288.4 25.2 %copy-start.6 = (f32[3,3,8,8]{3,2,1,0:T(8,128)S(1)}, f32[3,3,8,8]{3,2,1,0:T(8,128)}, u32[]{:S(2)}) copy-start(f32[3,3,8,8]{3,2,1,0:T(8,128)} %copy-done.5) | copy-start | bytes 6916
  288.4 25.1 %copy-start.8 = (f32[3,3,8,8]{3,2,1,0:T(8,128)S(1)}, f32[3,3,8,8]{3,2,1,0:T(8,128)}, u32[]{:S(2)}) copy-start(f32[3,3,8,8]{3,2,1,0:T(8,128)} %copy-done.7) | copy-start | bytes 6916
  288.5 25.1 %copy-start.9 = (f32[1,2,8,8]{3,2,1,0:T(8,128)S(1)}, f32[1,2,8,8]{3,2,1,0:T(8,128)}, u32[]{:S(2)}) copy-start(f32[1,2,8,8]{3,2,1,0:T(8,128)} %fusion.27) | copy-start | bytes 1540
  297.6 5.7 %collective-permute-start = (f32[3,2,2,8,8]{4,2,1,3,0:T(2,128)S(1)}, f32[3,2,2,8,8]{4,2,1,3,0:T(2,128)S(1)}, u32[]{:S(2)}, u32[]{:S(2)}) collective-permute-start(f32[3,2,2,8,8]{4,2,1,3,0:T(2,128)S(1)} %get-tuple-element.8), channel_id=1, source_target_pairs={{0,8},{8,16},{16,24},{1,9},{9,17},{17,25},{2,10},{10,18},{18,26},{... | collective-permute-start | bytes 9224 | tf_op jit(solution)/shard_map/ppermute | solution.py:37
  303.5 4.4 %collective-permute-start.1 = (f32[3,2,2,8]{3,2,1,0:T(2,128)S(1)}, f32[3,2,2,8]{3,2,1,0:T(2,128)S(1)}, u32[]{:S(2)}, u32[]{:S(2)}) collective-permute-start(f32[3,2,2,8]{3,2,1,0:T(2,128)S(1)} %bitcast.92), channel_id=1, source_target_pairs={{0,2},{2,4},{4,6},{1,3},{3,5},{5,7},{8,10},{10,12},{12,14},{9,11},... | collective-permute-start | bytes 1160 | tf_op jit(solution)/shard_map/ppermute | solution.py:37
  308.1 5.4 %collective-permute-start.2 = (f32[3,2,8]{2,1,0:T(2,128)S(1)}, f32[3,2,8]{2,1,0:T(2,128)S(1)}, u32[]{:S(2)}, u32[]{:S(2)}) collective-permute-start(f32[3,2,8]{2,1,0:T(2,128)S(1)} %slice_reduce_fusion), channel_id=1, source_target_pairs={{0,1},{2,3},{4,5},{6,7},{8,9},{10,11},{12,13},{14,15},{16,17},{18,... | collective-permute-start | bytes 584 | tf_op jit(solution)/shard_map/ppermute | solution.py:37
where the time goes:
time: 321 us; the launch traced here: 315 us
  matrix products  135 us (42%)
  waiting for transfers between devices  84.8 us (26%)
  local copies, waits for them, and re-layouts  50.7 us (16%)
  starting transfers between devices  28 us (9%)
  other arithmetic  15.5 us (5%)
    ppermute x3, waiting for transfers between devices, padded_2(): lax.ppermute(head, axis, [((i + 1) % count, i) for i in range(ends)])  77 us
    dot_general x1, matrix products, interpolate(): jnp.einsum('nkc,nabc->nabk', matrices[2], volume, precision=highest)  60.8 us
    dot_general x1, matrix products, interpolate(): jnp.einsum('nia,najk->nijk', matrices[0], partial_y, precision=highest)  57.7 us
    gather x2, local copies, waits for them, and re-layouts, local(): jnp.take(arrived, recv_slot, axis=0)  19.7 us
    select_n x1, local copies, waits for them, and re-layouts, local(): jnp.take(arrived, recv_slot, axis=0)  12.6 us
    dot_general x1, matrix products, interpolate(): jnp.einsum('njb,nabk->najk', matrices[1], partial_z, precision=highest)  9.5 us
    ppermute x3, starting transfers between devices, padded_2(): lax.ppermute(head, axis, [((i + 1) % count, i) for i in range(ends)])  8.13 us
    ppermute x3, waiting for transfers between devices, from_behind(): return lax.ppermute(block, axis, route)  7.79 us
  transfers between devices with their start and end apart: 10, of which 4 were waited for; matrix products, arithmetic and copies ran while one was open for 3% of the time, Pallas kernels for 0%

commit v1 on v0

v1 whole, which is shorter than its diff:
```python
import functools

import jax
import jax.numpy as jnp
from jax import lax
from jax.experimental import pallas as pl
from jax.experimental.pallas import tpu as pltpu
from jax.sharding import PartitionSpec as P

CX = 2
CY = 8
CZ = 8
LANES = CX * CY * CZ
SLAB = ("gy", "gz")

shear_modulus = 0.05
lame_first = 1.0
data_weight = 0.0625

DISP = 24
OFFS = 27
SLOT = 30
META = 32


def iota(shape, dim):
    return lax.broadcasted_iota(jnp.int32, shape, dim)


def shifted(planes, bits):
    for bit, count in ((2, 12), (1, 10), (0, 9)):
        step = 1 << bit
        planes = [jnp.where(bits[bit], planes[p + step], planes[p]) for p in range(count)]
    return planes


def offset_bits(offset, rows):
    wide = jnp.broadcast_to(offset, (rows, LANES))
    return [(wide & (1 << bit)) != 0 for bit in range(3)]


def sample_kernel(cap, readers, swap, block_row, send_ref, meta_ref, table_ref, *rest):
    outs, (along_a, along_b, along_c) = rest[:-3], rest[-3:]
    holder = lax.axis_index("gy") * lax.axis_size("gz") + lax.axis_index("gz")
    row = send_ref[pl.ds(block_row(), 1), :]
    if swap:
        row = jnp.where(lax.axis_index("gz") == 1, pltpu.roll(row, LANES // 2, 1), row)
    pick = (iota((LANES, LANES), 0) == row).astype(jnp.bfloat16)
    slot = iota((LANES, LANES), 0)
    meta = jnp.zeros((META, LANES), jnp.float32)
    for r in range(readers):
        wanted = meta_ref[r, SLOT : SLOT + 1, :].astype(jnp.int32)
        hit = (wanted == holder * cap + slot - r * cap) & (slot // cap == r)
        meta = meta + lax.dot_general(
            meta_ref[r].astype(jnp.bfloat16),
            hit.astype(jnp.bfloat16),
            (((1,), (1,)), ((), ())),
            preferred_element_type=jnp.float32,
        )
    upper = meta[:24]
    lower = 1.0 - upper
    offsets = meta[OFFS : OFFS + 3].astype(jnp.int32)
    bits = offset_bits(offsets[0:1], 16)
    for b in range(16):
        rows = jnp.concatenate(
            [table_ref[256 * a + 16 * b : 256 * a + 16 * b + 16, :] for a in range(16)], axis=0
        )
        voxels = jnp.dot(rows, pick, preferred_element_type=jnp.float32)
        window = shifted([voxels[16 * a : 16 * a + 16] for a in range(16)], bits)
        for i in range(8):
            along_a[256 * i + 16 * b : 256 * i + 16 * b + 16, :] = (
                lower[i : i + 1] * window[i] + upper[i : i + 1] * window[i + 1]
            )
    bits = offset_bits(offsets[1:2], 16)
    for i in range(8):
        window = shifted(
            [along_a[256 * i + 16 * b : 256 * i + 16 * b + 16, :] for b in range(16)], bits
        )
        for j in range(8):
            along_b[128 * i + 16 * j : 128 * i + 16 * j + 16, :] = (
                lower[8 + j : 9 + j] * window[j] + upper[8 + j : 9 + j] * window[j + 1]
            )
    bits = offset_bits(offsets[2:3], 8)
    for i in range(8):
        window = shifted(
            [along_b[pl.ds(128 * i + c, 8, stride=16), :] for c in range(16)], bits
        )
        for k in range(8):
            along_c[pl.ds(64 * i + k, 8, stride=8), :] = (
                lower[16 + k : 17 + k] * window[k] + upper[16 + k : 17 + k] * window[k + 1]
            )
    samples = along_c[...].T.astype(jnp.bfloat16)
    height = LANES // len(outs)
    for n, out in enumerate(outs):
        out[...] = samples[height * n : height * n + height]


def sample_call(cap, readers, swap, block_row, pieces, send_rows, meta, table):
    vmem = pl.BlockSpec(memory_space=pltpu.VMEM)
    return pl.pallas_call(
        functools.partial(sample_kernel, cap, readers, swap, block_row),
        out_shape=[jax.ShapeDtypeStruct((LANES // pieces, 512), jnp.bfloat16)] * pieces,
        in_specs=[vmem] * 3,
        out_specs=[vmem] * pieces,
        scratch_shapes=[
            pltpu.VMEM((2048, LANES), jnp.float32),
            pltpu.VMEM((1024, LANES), jnp.float32),
            pltpu.VMEM((512, LANES), jnp.float32),
        ],
        compiler_params=pltpu.CompilerParams(vmem_limit_bytes=24 << 20),
        cost_estimate=pl.CostEstimate(
            flops=2 * 4096 * 128 * 128, bytes_accessed=2 << 20, transcendentals=0
        ),
        name="interpolate",
    )(send_rows, meta, table)


def shape_table():
    centres = (jnp.arange(8, dtype=jnp.float32) + 0.5) / 8.0
    weights = jnp.stack([1.0 - centres, centres], axis=1)
    values = (
        weights[:, None, None, None, :, None]
        * weights[None, :, None, None, None, :]
        * weights[None, None, :, :, None, None]
    ).reshape(512, 8)
    return jnp.pad(values, ((0, 0), (0, LANES - 8)))


def axis_of_lane(rows):
    lane = iota((rows, LANES), 1)
    return lane // (CY * CZ), lane // CZ % CY, lane % CZ


def force_kernel(cap, relative, slot_ref, image_ref, slope_ref, shape_ref, *rest):
    arrived, (kept_ref, sent_ref) = rest[:-2], rest[-2:]
    total = sum(piece.shape[0] for piece in arrived)
    number = iota((LANES, total), 1)
    if relative:
        own = lax.axis_index("gy") * lax.axis_size("gz") + lax.axis_index("gz")
        number = ((number // cap) ^ own) * cap + number % cap
    hit = (slot_ref[...] == number).astype(jnp.bfloat16)
    rows = jnp.concatenate([piece[...] for piece in arrived], axis=0)
    samples = jnp.dot(hit, rows, preferred_element_type=jnp.float32)
    difference = image_ref[...].astype(jnp.float32) - samples
    _, _, at_k = axis_of_lane(8)
    for d in range(3):
        weighted = slope_ref[d].astype(jnp.float32) * difference
        corners = jnp.dot(
            weighted,
            shape_ref[...],
            preferred_element_type=jnp.float32,
            precision=lax.Precision.HIGHEST,
        ).T[:8]
        carried = pltpu.roll(corners, 4, 0)
        kept_ref[8 * d : 8 * d + 8, :] = corners + jnp.where(at_k > 0, pltpu.roll(carried, 1, 1), 0.0)
        sent_ref[8 * d : 8 * d + 8, :] = jnp.where(at_k == 0, pltpu.roll(carried, LANES - 7, 1), 0.0)


def layer_kernel(kept_ref, arrived_ref, own_ref, x_ref, y_ref, xy_ref):
    at_i, at_j, _ = axis_of_lane(8)
    behind = lax.axis_index("gz") > 0

    def along_x(lower_half, upper_half):
        moved = pltpu.roll(upper_half, CY * CZ, 1)
        return lower_half + jnp.where(at_i > 0, moved, 0.0), jnp.where(at_i == 0, moved, 0.0)

    for d in range(3):
        part = slice(8 * d, 8 * d + 8)
        z = kept_ref[part, :] + jnp.where(behind, arrived_ref[part, :], 0.0)
        carried = pltpu.roll(z, 7, 0)
        stay = z + jnp.where(at_j > 0, pltpu.roll(carried, CZ, 1), 0.0)
        leave = jnp.where(at_j == 0, pltpu.roll(carried, LANES - CZ * (CY - 1), 1), 0.0)
        own, x = along_x(stay, pltpu.roll(stay, 6, 0))
        y, xy = along_x(leave, pltpu.roll(leave, 6, 0))
        for ref, value in ((own_ref, own), (x_ref, x), (y_ref, y), (xy_ref, xy)):
            ref[d : d + 1, :] = value[0:1]


def final_kernel(own_ref, x_ref, y_ref, xy_ref, stiff_ref, out_ref):
    has_x = lax.axis_index("gx") > 0
    has_y = lax.axis_index("gy") > 0
    force = own_ref[0:3, :]
    force = force + jnp.where(has_x, x_ref[0:3, :], 0.0)
    force = force + jnp.where(has_y, y_ref[0:3, :], 0.0)
    force = force + jnp.where(has_x & has_y, xy_ref[0:3, :], 0.0)
    out_ref[...] = force * data_weight + stiff_ref[0:3, :]


def stiffness_kernel(relative, below_ref, own_ref, above_ref, out_ref):
    here = [lax.axis_index(name) for name in ("gx", "gy", "gz")]
    sizes = [lax.axis_size(name) for name in ("gx", "gy", "gz")]
    own = here[1] * sizes[2] + here[2]
    slabs = {-1: below_ref, 0: own_ref, 1: above_ref}
    at = axis_of_lane(8)
    steps = (CY * CZ, CZ, 1)
    extents = (CX, CY, CZ)
    fields = {}
    for ox in (-1, 0, 1):
        for oy in (-1, 0, 1):
            for oz in (-1, 0, 1):
                if ox and oy and oz:
                    continue
                place = (here[0] + ox, here[1] + oy, here[2] + oz)
                inside = True
                for where, size in zip(place, sizes):
                    inside = inside & (where >= 0) & (where < size)
                peer = jnp.clip(place[1], 0, sizes[1] - 1) * sizes[2] + jnp.clip(
                    place[2], 0, sizes[2] - 1
                )
                if relative:
                    peer = peer ^ own
                fields[ox, oy, oz] = jnp.where(inside, slabs[ox][peer], 0.0)

    def along(axis, sign, centre, beyond):
        step, extent = steps[axis], extents[axis]
        back = step * (extent - 1)
        if sign > 0:
            return jnp.where(
                at[axis] < extent - 1,
                pltpu.roll(centre, LANES - step, 1),
                pltpu.roll(beyond, back, 1),
            )
        return jnp.where(
            at[axis] > 0, pltpu.roll(centre, step, 1), pltpu.roll(beyond, LANES - back, 1)
        )

    def moved(vector, frame=(0, 0, 0), axis=2):
        if axis < 0:
            return fields[frame]
        sign = vector[axis]
        centre = moved(vector, frame, axis - 1)
        if sign == 0:
            return centre
        other = tuple(sign if n == axis else frame[n] for n in range(3))
        return along(axis, sign, centre, moved(vector, other, axis - 1))

    units = ((1, 0, 0), (0, 1, 0), (0, 0, 1))
    centre = fields[0, 0, 0]
    laplace = -6.0 * centre
    second = []
    for unit in units:
        both = moved(unit) + moved(tuple(-n for n in unit))
        laplace = laplace + both
        second.append(both - 2.0 * centre)
    mixed = {}
    for outer in range(3):
        for inner in range(outer + 1, 3):
            plus = tuple(p + q for p, q in zip(units[outer], units[inner]))
            cross = tuple(p - q for p, q in zip(units[outer], units[inner]))
            mixed[outer, inner] = 0.25 * (
                moved(plus)
                - moved(cross)
                - moved(tuple(-n for n in cross))
                + moved(tuple(-n for n in plus))
            )
    for d in range(3):
        total = second[d][d : d + 1]
        for b in range(3):
            if b != d:
                total = total + mixed[min(b, d), max(b, d)][b : b + 1]
        out_ref[d : d + 1, :] = -(
            shear_modulus * laplace[d : d + 1] + (lame_first + shear_modulus) * total
        )


def small_call(kernel, shapes, name, *operands):
    vmem = pl.BlockSpec(memory_space=pltpu.VMEM)
    return pl.pallas_call(
        kernel,
        out_shape=[jax.ShapeDtypeStruct(shape, jnp.float32) for shape in shapes],
        in_specs=[vmem] * len(operands),
        out_specs=[vmem] * len(shapes),
        compiler_params=pltpu.CompilerParams(vmem_limit_bytes=24 << 20),
        cost_estimate=pl.CostEstimate(flops=1 << 20, bytes_accessed=1 << 20, transcendentals=0),
        name=name,
    )(*operands)


def ring(value, axes, distance=1):
    count = lax.axis_size(axes)
    return lax.ppermute(value, axes, [(i, (i + distance) % count) for i in range(count)])


def ring_2(value):
    nx, ny = lax.axis_size("gx"), lax.axis_size("gy")
    route = [
        (x * ny + y, (x + 1) % nx * ny + (y + 1) % ny) for x in range(nx) for y in range(ny)
    ]
    return lax.ppermute(value, ("gx", "gy"), route)


def swapped(value, axes, mask):
    return lax.ppermute(value, axes, [(i, i ^ mask) for i in range(lax.axis_size(axes))])


def local(
    displacement,
    reference_image,
    image_gradient,
    deformed_blocks,
    fractions,
    offsets,
    send_list,
    recv_slot,
):
    n_y, n_z = lax.axis_size("gy"), lax.axis_size("gz")
    peers = n_y * n_z
    cap = send_list.shape[0] // peers
    f32 = jnp.float32
    packed = jnp.concatenate(
        [
            fractions.astype(f32),
            displacement,
            offsets.astype(f32),
            recv_slot.astype(f32)[None],
            jnp.zeros((1, LANES), f32),
        ],
        axis=0,
    )
    table = deformed_blocks.T
    send_rows = send_list.reshape(-1, LANES)
    relative = n_z == 2 and n_y in (2, 4) and 2 * cap == LANES
    if relative:
        chip = jnp.stack([packed, swapped(packed, "gz", 1)])
        metas = [chip] + [swapped(chip, "gy", d) for d in range(1, n_y)]
        arrived = [None] * peers
        order = list(range(n_y - 1, 0, -1)) + [0]
        for d in order:
            pair = sample_call(
                cap, 2, True, lambda d=d: lax.axis_index("gy") ^ d, 2, send_rows, metas[d], table
            )
            for other in range(2):
                mask = 2 * d + other
                arrived[mask] = swapped(pair[other], SLAB, mask) if mask else pair[other]
        slab = jnp.concatenate([meta[:, DISP:META] for meta in metas], axis=0)
    else:
        gathered = lax.all_gather(packed, SLAB, axis=0)
        readers = LANES // cap
        groups = peers // readers
        samples = [
            sample_call(
                cap,
                readers,
                False,
                lambda g=g: g,
                1,
                send_rows,
                gathered[g * readers : (g + 1) * readers],
                table,
            )[0]
            for g in range(groups)
        ]
        outgoing = jnp.concatenate(samples, axis=0)
        arrived = [lax.all_to_all(outgoing, SLAB, split_axis=0, concat_axis=0, tiled=True)]
        slab = gathered[:, DISP:META]
    below, above = ring(slab, "gx", 1), ring(slab, "gx", -1)
    (stiff,) = small_call(
        functools.partial(stiffness_kernel, relative), [(8, LANES)], "stiffness", below, slab, above
    )
    kept, sent = small_call(
        functools.partial(force_kernel, cap, relative),
        [(24, LANES)] * 2,
        "forces",
        recv_slot[:, None],
        reference_image,
        image_gradient,
        shape_table(),
        *arrived,
    )
    own, x, y, xy = small_call(
        layer_kernel, [(8, LANES)] * 4, "layers", kept, ring(sent, "gz")
    )
    return small_call(
        final_kernel,
        [(3, LANES)],
        "total",
        own,
        ring(x, "gx"),
        ring(y, "gy"),
        ring_2(xy),
        stiff,
    )[0]


def solution(mesh):
    in_specs = (
        P(None, ("gx", "gy", "gz")),
        P(("gx", "gy", "gz"), None),
        P(None, ("gx", "gy", "gz"), None),
        P(("gx", "gy", "gz"), None),
        P(None, ("gx", "gy", "gz")),
        P(None, ("gx", "gy", "gz")),
        P(("gx", "gy", "gz")),
        P(("gx", "gy", "gz")),
    )
    out_specs = P(None, ("gx", "gy", "gz"))
    return jax.shard_map(local, mesh=mesh, in_specs=in_specs, out_specs=out_specs, check_vma=False)
```

time: 321 us -> 46 us (0.14)
  the two profiles are of different devices: /device:TPU:13 before, /device:TPU:0 now
where the time goes in v1:
time: 46 us; the launch traced here: 45.7 us
  starting transfers between devices  22.4 us (49%)
  waiting for transfers between devices  12.2 us (27%)
  Pallas kernels  5.88 us (13%)
  local copies, waits for them, and re-layouts  4.14 us (9%)
  other arithmetic  0.91 us (2%)
    ppermute x11, starting transfers between devices, swapped(): lax.ppermute(value, axes, [(i, i ^ mask) for i in range(lax.axis_size(axe...  14.3 us
    ppermute x11, waiting for transfers between devices, swapped(): lax.ppermute(value, axes, [(i, i ^ mask) for i in range(lax.axis_size(axe...  6.24 us
    ppermute x5, starting transfers between devices, ring(): lax.ppermute(value, axes, [(i, (i + distance) % count) for i in range(cou...  6.24 us
    ppermute x1, waiting for transfers between devices, ring_2(): return lax.ppermute(value, ('gx', 'gy'), route)  3.94 us
    pallas_call x4, Pallas kernels, sample_call(): pl.pallas_call(functools.partial(sample_kernel, cap, readers, swap, block...  3.76 us
    unnamed x15, local copies, waits for them, and re-layouts  2.32 us
    pallas_call x4, Pallas kernels, small_call(): pl.pallas_call(kernel, out_shape=[jax.ShapeDtypeStruct(shape, jnp.float32...  2.12 us
    ppermute x5, waiting for transfers between devices, ring(): lax.ppermute(value, axes, [(i, (i + distance) % count) for i in range(cou...  1.99 us
  transfers between devices with their start and end apart: 17, of which 5 were waited for; matrix products, arithmetic and copies ran while one was open for 5% of the time, Pallas kernels for 12%

profile of v1, /device:TPU:0, one launch (start us, length us, event | category | flops | bytes accessed | tf_op | source)
XLA Modules:
  0.0 45.7 jit_solution(13821149568492815016)
XLA Ops:
  0.0 0.7 %convert_element_type.12 = f32[3,128]{1,0:T(4,128)S(1)} convert(s32[3,128]{1,0:T(4,128)} %param.13) | non-fusion elementwise | flops 384 | bytes 3072 | tf_op jit(solution)/shard_map/convert_element_type | solution.py:314
  0.7 0.7 %concatenate.6 = f32[32,128]{1,0:T(8,128)S(1)} concatenate(bf16[24,128]{1,0:T(8,128)(2,1)S(1)} %copy-done.5, f32[3,128]{1,0:T(4,128)} %param.8, f32[3,128]{1,0:T(4,128)S(1)} %convert_element_type.12, f32[1,128]{1,0:T(1,128)S(1)} %convert_bitcast_fusion, f32[1,128]{1,0:T(1,128)S(1)} %broadcast_in_dim.14), dimensions={0} | concatenate | bytes 26624 | tf_op jit(solution)/shard_map/concatenate | solution.py:310
  1.4 0.5 %collective-permute-start = (f32[32,128]{1,0:T(8,128)S(1)}, f32[32,128]{1,0:T(8,128)S(1)}, u32[]{:S(2)}, u32[]{:S(2)}) collective-permute-start(f32[32,128]{1,0:T(8,128)S(1)} %concatenate.6), channel_id=1, source_target_pairs={{0,1},{1,0},{2,3},{3,2},{4,5},{5,4},{6,7},{7,6},{8,9},{9,8},{10,11... | collective-permute-start | bytes 49160 | tf_op jit(solution)/shard_map/ppermute | solution.py:293
  2.0 0.1 broadcast_multiply_fusion.1
  2.0 1.6 %copy.12 = bf16[128,4096]{0,1:T(8,128)(2,1)S(1)} copy(bf16[128,4096]{1,0:T(8,128)(2,1)} %param.11) | data formatting | bytes 2097152 | tf_op args[3]
  3.7 4.7 %collective-permute-start.8 = (f32[2,32,128]{2,1,0:T(8,128)S(1)}, f32[2,32,128]{2,1,0:T(8,128)S(1)}, u32[]{:S(2)}, u32[]{:S(2)}) collective-permute-start(f32[2,32,128]{2,1,0:T(8,128)S(1)} %pad_maximum_fusion.meta_ref), channel_id=1, source_target_pairs={{0,6},{2,4},{4,2},{6,0},{1,7},{3,5},{5,3},{7,1},{8,14},{10,12},{12... | collective-permute-start | bytes 98312 | tf_op jit(solution)/shard_map/ppermute | solution.py:293
  8.4 0.6 %collective-permute-start.5 = (f32[2,32,128]{2,1,0:T(8,128)S(1)}, f32[2,32,128]{2,1,0:T(8,128)S(1)}, u32[]{:S(2)}, u32[]{:S(2)}) collective-permute-start(f32[2,32,128]{2,1,0:T(8,128)S(1)} %pad_maximum_fusion.meta_ref), channel_id=1, source_target_pairs={{0,4},{2,6},{4,0},{6,2},{1,5},{3,7},{5,1},{7,3},{8,12},{10,14},{12... | collective-permute-start | bytes 98312 | tf_op jit(solution)/shard_map/ppermute | solution.py:293
  9.0 0.7 %copy-done.4 = s32[512]{0:T(512)S(1)} copy-done((s32[512]{0:T(512)S(1)}, s32[512]{0:T(512)}, u32[]{:S(2)}) %copy-start.4) | copy-done | bytes 2072
  9.7 0.9 %interpolate.4 = (bf16[64,512]{1,0:T(8,128)(2,1)S(1)}, bf16[64,512]{1,0:T(8,128)(2,1)S(1)}) custom-call(s32[4,128]{1,0:T(4,128)S(1)} %bitcast.15, f32[2,32,128]{2,1,0:T(8,128)S(1)} %pad_maximum_fusion.meta_ref, bf16[4096,128]{1,0:T(8,128)(2,1)S(1)} %bitcast.11), custom_call_target="tpu_custom_call" | custom-call | flops 134217728 | bytes 2097152 | tf_op jit(solution)/shard_map/interpolate/pallas_call | solution.py:100
  10.6 0.1 collective-permute-start.1
  10.7 0.0 collective-permute-done.8.meta_ref
  10.7 0.9 %interpolate.7 = (bf16[64,512]{1,0:T(8,128)(2,1)S(1)}, bf16[64,512]{1,0:T(8,128)(2,1)S(1)}) custom-call(s32[4,128]{1,0:T(4,128)S(1)} %bitcast.16, f32[2,32,128]{2,1,0:T(8,128)S(1)} %collective-permute-done.8.meta_ref, bf16[4096,128]{1,0:T(8,128)(2,1)S(1)} %bitcast.12), custom_call_target="tpu_custom_call" | custom-call | flops 134217728 | bytes 2097152 | tf_op jit(solution)/shard_map/interpolate/pallas_call | solution.py:100
  11.7 3.9 %collective-permute-start.10 = (bf16[64,512]{1,0:T(8,128)(2,1)S(1)}, bf16[64,512]{1,0:T(8,128)(2,1)S(1)}, u32[]{:S(2)}, u32[]{:S(2)}) collective-permute-start(bf16[64,512]{1,0:T(8,128)(2,1)S(1)} %get-tuple-element.26), channel_id=1, source_target_pairs={{0,7},{1,6},{2,5},{3,4},{4,3},{5,2},{6,1},{7,0},{8,15},{9,14},{10,... | collective-permute-start | bytes 196616 | tf_op jit(solution)/shard_map/ppermute | solution.py:293
  15.6 0.9 %interpolate.5 = (bf16[64,512]{1,0:T(8,128)(2,1)S(1)}, bf16[64,512]{1,0:T(8,128)(2,1)S(1)}) custom-call(s32[4,128]{1,0:T(4,128)S(1)} %bitcast.17, f32[2,32,128]{2,1,0:T(8,128)S(1)} %collective-permute-done.2.meta_ref, bf16[4096,128]{1,0:T(8,128)(2,1)S(1)} %bitcast.13), custom_call_target="tpu_custom_call" | custom-call | flops 134217728 | bytes 2097152 | tf_op jit(solution)/shard_map/interpolate/pallas_call | solution.py:100
  16.5 0.1 collective-permute-start.3
  16.6 1.4 %collective-permute-start.4 = (bf16[64,512]{1,0:T(8,128)(2,1)S(1)}, bf16[64,512]{1,0:T(8,128)(2,1)S(1)}, u32[]{:S(2)}, u32[]{:S(2)}) collective-permute-start(bf16[64,512]{1,0:T(8,128)(2,1)S(1)} %get-tuple-element.22), channel_id=1, source_target_pairs={{0,3},{1,2},{2,1},{3,0},{4,7},{5,6},{6,5},{7,4},{8,11},{9,10},{10,... | collective-permute-start | bytes 196616 | tf_op jit(solution)/shard_map/ppermute | solution.py:293
  18.0 0.7 %slice-done = f32[2,8,128]{2,1,0:T(8,128)S(1)} async-done(((f32[2,32,128]{2,1,0:T(8,128)}), f32[2,8,128]{2,1,0:T(8,128)S(1)}, s32[]{:S(2)}) %slice-start) | async-done | bytes 8216 | tf_op jit(solution)/shard_map/slice | solution.py:335
  18.7 0.0 slice-done.1
  18.7 1.5 %collective-permute-start.15 = (f32[8,8,128]{2,1,0:T(8,128)S(1)}, f32[8,8,128]{2,1,0:T(8,128)S(1)}, u32[]{:S(2)}, u32[]{:S(2)}) collective-permute-start(f32[8,8,128]{2,1,0:T(8,128)S(1)} %pad_maximum_fusion.1.own_ref), channel_id=1, source_target_pairs={{0,8},{8,16},{16,24},{24,0},{1,9},{9,17},{17,25},{25,1},{2,10},{10... | collective-permute-start | bytes 98312 | tf_op jit(solution)/shard_map/ppermute | solution.py:281
  20.2 0.9 %interpolate.6 = (bf16[64,512]{1,0:T(8,128)(2,1)S(1)}, bf16[64,512]{1,0:T(8,128)(2,1)S(1)}) custom-call(s32[4,128]{1,0:T(4,128)S(1)} %bitcast.18, f32[2,32,128]{2,1,0:T(8,128)S(1)} %collective-permute-done.5.meta_ref, bf16[4096,128]{1,0:T(8,128)(2,1)S(1)} %bitcast.14), custom_call_target="tpu_custom_call" | custom-call | flops 134217728 | bytes 2097152 | tf_op jit(solution)/shard_map/interpolate/pallas_call | solution.py:100
  21.2 1.5 %collective-permute-start.16 = (f32[8,8,128]{2,1,0:T(8,128)S(1)}, f32[8,8,128]{2,1,0:T(8,128)S(1)}, u32[]{:S(2)}, u32[]{:S(2)}) collective-permute-start(f32[8,8,128]{2,1,0:T(8,128)S(1)} %pad_maximum_fusion.1.own_ref), channel_id=1, source_target_pairs={{0,24},{8,0},{16,8},{24,16},{1,25},{9,1},{17,9},{25,17},{2,26},{10... | collective-permute-start | bytes 98312 | tf_op jit(solution)/shard_map/ppermute | solution.py:281
  22.6 0.0 collective-permute-done.10.rest_7_
  22.6 0.0 collective-permute-start.6
  22.6 0.0 collective-permute-done.3.rest_2_
  22.6 2.4 %collective-permute-start.7 = (bf16[64,512]{1,0:T(8,128)(2,1)S(1)}, bf16[64,512]{1,0:T(8,128)(2,1)S(1)}, u32[]{:S(2)}, u32[]{:S(2)}) collective-permute-start(bf16[64,512]{1,0:T(8,128)(2,1)S(1)} %get-tuple-element.24), channel_id=1, source_target_pairs={{0,5},{1,4},{2,7},{3,6},{4,1},{5,0},{6,3},{7,2},{8,13},{9,12},{10,... | collective-permute-start | bytes 196616 | tf_op jit(solution)/shard_map/ppermute | solution.py:293
  25.1 0.0 collective-permute-done.4.rest_3_
  25.1 0.6 %collective-permute-start.9 = (bf16[64,512]{1,0:T(8,128)(2,1)S(1)}, bf16[64,512]{1,0:T(8,128)(2,1)S(1)}, u32[]{:S(2)}, u32[]{:S(2)}) collective-permute-start(bf16[64,512]{1,0:T(8,128)(2,1)S(1)} %get-tuple-element.25), channel_id=1, source_target_pairs={{0,6},{1,7},{2,4},{3,5},{4,2},{5,3},{6,0},{7,1},{8,14},{9,15},{10,... | collective-permute-start | bytes 196616 | tf_op jit(solution)/shard_map/ppermute | solution.py:293
  25.7 0.1 broadcast_multiply_fusion
  25.8 0.2 mul.41
  26.0 0.0 copy-start
  26.0 0.1 copy.11
  26.1 0.0 copy-start.1
  26.2 0.1 copy.13.slot_ref
  26.3 5.5 %collective-permute-done.6.rest_4_ = bf16[64,512]{1,0:T(8,128)(2,1)S(1)} collective-permute-done((bf16[64,512]{1,0:T(8,128)(2,1)S(1)}, bf16[64,512]{1,0:T(8,128)(2,1)S(1)}, u32[]{:S(2)}, u32[]{:S(2)}) %collective-permute-start.6) | collective-permute-done | bytes 65568 | tf_op jit(solution)/shard_map/ppermute | solution.py:293
  31.8 0.7 %collective-permute-done.7.rest_5_ = bf16[64,512]{1,0:T(8,128)(2,1)S(1)} collective-permute-done((bf16[64,512]{1,0:T(8,128)(2,1)S(1)}, bf16[64,512]{1,0:T(8,128)(2,1)S(1)}, u32[]{:S(2)}, u32[]{:S(2)}) %collective-permute-start.7) | collective-permute-done | bytes 65568 | tf_op jit(solution)/shard_map/ppermute | solution.py:293
  32.5 1.2 %forces.1 = (f32[24,128]{1,0:T(8,128)S(1)}, f32[24,128]{1,0:T(8,128)S(1)}) custom-call(s32[128,1]{1,0:T(8,128)S(1)} %copy.13.slot_ref, bf16[128,512]{1,0:T(8,128)(2,1)S(1)} %copy-done.1, bf16[3,128,512]{2,1,0:T(8,128)(2,1)S(1)} %copy-done, f32[512,128]{1,0:T(8,128)S(1)} %pad.4.shape_ref, bf16[64,512]{1,0:T(8,128)(2,1)S(1)} %get-tuple-element.19.rest_0_, ...), custom_call_target="tpu_custom_call" | custom-call | flops 1048576 | bytes 1048576 | tf_op jit(solution)/shard_map/forces/pallas_call | solution.py:268
  33.7 0.5 %collective-permute-start.11 = (f32[24,128]{1,0:T(8,128)S(1)}, f32[24,128]{1,0:T(8,128)S(1)}, u32[]{:S(2)}, u32[]{:S(2)}) collective-permute-start(f32[24,128]{1,0:T(8,128)S(1)} %get-tuple-element.28), channel_id=1, source_target_pairs={{0,1},{1,0},{2,3},{3,2},{4,5},{5,4},{6,7},{7,6},{8,9},{9,8},{10,11... | collective-permute-start | bytes 36872 | tf_op jit(solution)/shard_map/ppermute | solution.py:281
  34.2 0.8 %collective-permute-done.11.arrived_ref = f32[24,128]{1,0:T(8,128)S(1)} collective-permute-done((f32[24,128]{1,0:T(8,128)S(1)}, f32[24,128]{1,0:T(8,128)S(1)}, u32[]{:S(2)}, u32[]{:S(2)}) %collective-permute-start.11) | collective-permute-done | bytes 12320 | tf_op jit(solution)/shard_map/ppermute | solution.py:281
  35.0 0.2 layers.1
  35.2 0.6 %collective-permute-start.12 = (f32[8,128]{1,0:T(8,128)S(1)}, f32[8,128]{1,0:T(8,128)S(1)}, u32[]{:S(2)}, u32[]{:S(2)}) collective-permute-start(f32[8,128]{1,0:T(8,128)S(1)} %get-tuple-element.30), channel_id=1, source_target_pairs={{0,8},{8,16},{16,24},{24,0},{1,9},{9,17},{17,25},{25,1},{2,10},{10... | collective-permute-start | bytes 12296 | tf_op jit(solution)/shard_map/ppermute | solution.py:281
  35.8 2.1 %collective-permute-start.13 = (f32[8,128]{1,0:T(8,128)S(1)}, f32[8,128]{1,0:T(8,128)S(1)}, u32[]{:S(2)}, u32[]{:S(2)}) collective-permute-start(f32[8,128]{1,0:T(8,128)S(1)} %get-tuple-element.31), channel_id=1, source_target_pairs={{0,2},{2,4},{4,6},{6,0},{1,3},{3,5},{5,7},{7,1},{8,10},{10,12},{12... | collective-permute-start | bytes 12296 | tf_op jit(solution)/shard_map/ppermute | solution.py:281
  37.9 1.9 %collective-permute-start.14 = (f32[8,128]{1,0:T(8,128)S(1)}, f32[8,128]{1,0:T(8,128)S(1)}, u32[]{:S(2)}, u32[]{:S(2)}) collective-permute-start(f32[8,128]{1,0:T(8,128)S(1)} %get-tuple-element.32), channel_id=1, source_target_pairs={{0,10},{2,12},{4,14},{6,8},{8,18},{10,20},{12,22},{14,16},{16,26},... | collective-permute-start | bytes 12296 | tf_op jit(solution)/shard_map/ppermute | solution.py:289
  39.8 0.0 collective-permute-done.15.below_ref
  39.8 0.0 collective-permute-done.16.above_ref
  39.8 0.2 stiffness.1.stiff_ref
  40.1 1.2 %collective-permute-done.13.y_ref = f32[8,128]{1,0:T(8,128)S(1)} collective-permute-done((f32[8,128]{1,0:T(8,128)S(1)}, f32[8,128]{1,0:T(8,128)S(1)}, u32[]{:S(2)}, u32[]{:S(2)}) %collective-permute-start.13) | collective-permute-done | bytes 4128 | tf_op jit(solution)/shard_map/ppermute | solution.py:281
  41.2 3.9 %collective-permute-done.14.xy_ref = f32[8,128]{1,0:T(8,128)S(1)} collective-permute-done((f32[8,128]{1,0:T(8,128)S(1)}, f32[8,128]{1,0:T(8,128)S(1)}, u32[]{:S(2)}, u32[]{:S(2)}) %collective-permute-start.14) | collective-permute-done | bytes 4128 | tf_op jit(solution)/shard_map/ppermute | solution.py:289
  45.1 0.6 %total.1 = f32[3,128]{1,0:T(4,128)} custom-call(f32[8,128]{1,0:T(8,128)S(1)} %get-tuple-element.29.own_ref, f32[8,128]{1,0:T(8,128)S(1)} %collective-permute-done.12.x_ref, f32[8,128]{1,0:T(8,128)S(1)} %collective-permute-done.13.y_ref, f32[8,128]{1,0:T(8,128)S(1)} %collective-permute-done.14.xy_ref, f32[8,128]{1,0:T(8,128)S(1)} %stiffness.1.stiff_ref), custom_call_target="tpu_custom_call" | custom-call | flops 1048576 | bytes 1048576 | tf_op jit(solution)/shard_map/total/pallas_call | solution.py:268
  (29 shorter events, 0.1 us)
Async XLA Ops:
  0.0 0.7 %copy-start.6 = (s32[128]{0:T(128)S(1)}, s32[128]{0:T(128)}, u32[]{:S(2)}) copy-start(s32[128]{0:T(128)} %param.15) | copy-start | bytes 1540
  0.0 0.7 %copy-start.5 = (bf16[24,128]{1,0:T(8,128)(2,1)S(1)}, bf16[24,128]{1,0:T(8,128)(2,1)}, u32[]{:S(2)}) copy-start(bf16[24,128]{1,0:T(8,128)(2,1)} %param.12) | copy-start | bytes 18436
  1.4 2.2 %collective-permute-start = (f32[32,128]{1,0:T(8,128)S(1)}, f32[32,128]{1,0:T(8,128)S(1)}, u32[]{:S(2)}, u32[]{:S(2)}) collective-permute-start(f32[32,128]{1,0:T(8,128)S(1)} %concatenate.6), channel_id=1, source_target_pairs={{0,1},{1,0},{2,3},{3,2},{4,5},{5,4},{6,7},{7,6},{8,9},{9,8},{10,11... | collective-permute-start | bytes 49160 | tf_op jit(solution)/shard_map/ppermute | solution.py:293
  3.7 7.0 %collective-permute-start.8 = (f32[2,32,128]{2,1,0:T(8,128)S(1)}, f32[2,32,128]{2,1,0:T(8,128)S(1)}, u32[]{:S(2)}, u32[]{:S(2)}) collective-permute-start(f32[2,32,128]{2,1,0:T(8,128)S(1)} %pad_maximum_fusion.meta_ref), channel_id=1, source_target_pairs={{0,6},{2,4},{4,2},{6,0},{1,7},{3,5},{5,3},{7,1},{8,14},{10,12},{12... | collective-permute-start | bytes 98312 | tf_op jit(solution)/shard_map/ppermute | solution.py:293
  8.4 7.2 %collective-permute-start.2 = (f32[2,32,128]{2,1,0:T(8,128)S(1)}, f32[2,32,128]{2,1,0:T(8,128)S(1)}, u32[]{:S(2)}, u32[]{:S(2)}) collective-permute-start(f32[2,32,128]{2,1,0:T(8,128)S(1)} %pad_maximum_fusion.meta_ref), channel_id=1, source_target_pairs={{0,2},{2,0},{4,6},{6,4},{1,3},{3,1},{5,7},{7,5},{8,10},{10,8},{12,... | collective-permute-start | bytes 98312 | tf_op jit(solution)/shard_map/ppermute | solution.py:293
  8.4 9.6 %collective-permute-start.5 = (f32[2,32,128]{2,1,0:T(8,128)S(1)}, f32[2,32,128]{2,1,0:T(8,128)S(1)}, u32[]{:S(2)}, u32[]{:S(2)}) collective-permute-start(f32[2,32,128]{2,1,0:T(8,128)S(1)} %pad_maximum_fusion.meta_ref), channel_id=1, source_target_pairs={{0,4},{2,6},{4,0},{6,2},{1,5},{3,7},{5,1},{7,3},{8,12},{10,14},{12... | collective-permute-start | bytes 98312 | tf_op jit(solution)/shard_map/ppermute | solution.py:293
  9.0 0.7 %copy-start.4 = (s32[512]{0:T(512)S(1)}, s32[512]{0:T(512)}, u32[]{:S(2)}) copy-start(s32[512]{0:T(512)} %param.14) | copy-start | bytes 6148
  10.6 10.5 %collective-permute-start.1 = (bf16[64,512]{1,0:T(8,128)(2,1)S(1)}, bf16[64,512]{1,0:T(8,128)(2,1)S(1)}, u32[]{:S(2)}, u32[]{:S(2)}) collective-permute-start(bf16[64,512]{1,0:T(8,128)(2,1)S(1)} %get-tuple-element.20), channel_id=1, source_target_pairs={{0,1},{1,0},{2,3},{3,2},{4,5},{5,4},{6,7},{7,6},{8,9},{9,8},{10,11... | collective-permute-start | bytes 196616 | tf_op jit(solution)/shard_map/ppermute | solution.py:293
  10.7 7.3 %copy-start.2 = (f32[2,32,128]{2,1,0:T(8,128)}, f32[2,32,128]{2,1,0:T(8,128)S(1)}, u32[]{:S(2)}) copy-start(f32[2,32,128]{2,1,0:T(8,128)S(1)} %collective-permute-done.8.meta_ref) | copy-start | bytes 98308
  11.7 10.9 %collective-permute-start.10 = (bf16[64,512]{1,0:T(8,128)(2,1)S(1)}, bf16[64,512]{1,0:T(8,128)(2,1)S(1)}, u32[]{:S(2)}, u32[]{:S(2)}) collective-permute-start(bf16[64,512]{1,0:T(8,128)(2,1)S(1)} %get-tuple-element.26), channel_id=1, source_target_pairs={{0,7},{1,6},{2,5},{3,4},{4,3},{5,2},{6,1},{7,0},{8,15},{9,14},{10,... | collective-permute-start | bytes 196616 | tf_op jit(solution)/shard_map/ppermute | solution.py:293
  15.6 2.4 %copy-start.3 = (f32[2,32,128]{2,1,0:T(8,128)}, f32[2,32,128]{2,1,0:T(8,128)S(1)}, u32[]{:S(2)}) copy-start(f32[2,32,128]{2,1,0:T(8,128)S(1)} %collective-permute-done.2.meta_ref) | copy-start | bytes 98308
  16.5 6.1 %collective-permute-start.3 = (bf16[64,512]{1,0:T(8,128)(2,1)S(1)}, bf16[64,512]{1,0:T(8,128)(2,1)S(1)}, u32[]{:S(2)}, u32[]{:S(2)}) collective-permute-start(bf16[64,512]{1,0:T(8,128)(2,1)S(1)} %get-tuple-element.21), channel_id=1, source_target_pairs={{0,2},{1,3},{2,0},{3,1},{4,6},{5,7},{6,4},{7,5},{8,10},{9,11},{10,... | collective-permute-start | bytes 196616 | tf_op jit(solution)/shard_map/ppermute | solution.py:293
  16.6 8.5 %collective-permute-start.4 = (bf16[64,512]{1,0:T(8,128)(2,1)S(1)}, bf16[64,512]{1,0:T(8,128)(2,1)S(1)}, u32[]{:S(2)}, u32[]{:S(2)}) collective-permute-start(bf16[64,512]{1,0:T(8,128)(2,1)S(1)} %get-tuple-element.22), channel_id=1, source_target_pairs={{0,3},{1,2},{2,1},{3,0},{4,7},{5,6},{6,5},{7,4},{8,11},{9,10},{10,... | collective-permute-start | bytes 196616 | tf_op jit(solution)/shard_map/ppermute | solution.py:293
  18.0 0.7 %slice-start = ((f32[2,32,128]{2,1,0:T(8,128)}), f32[2,8,128]{2,1,0:T(8,128)S(1)}, s32[]{:S(2)}) async-start(f32[2,32,128]{2,1,0:T(8,128)} %copy-done.2), calls=%async_computation | async-start | bytes 16384 | tf_op jit(solution)/shard_map/slice | solution.py:335
  18.0 0.7 %slice-start.1 = ((f32[2,32,128]{2,1,0:T(8,128)}), f32[2,8,128]{2,1,0:T(8,128)S(1)}, s32[]{:S(2)}) async-start(f32[2,32,128]{2,1,0:T(8,128)} %copy-done.3), calls=%async_computation.1 | async-start | bytes 16384 | tf_op jit(solution)/shard_map/slice | solution.py:335
  18.7 21.1 %collective-permute-start.15 = (f32[8,8,128]{2,1,0:T(8,128)S(1)}, f32[8,8,128]{2,1,0:T(8,128)S(1)}, u32[]{:S(2)}, u32[]{:S(2)}) collective-permute-start(f32[8,8,128]{2,1,0:T(8,128)S(1)} %pad_maximum_fusion.1.own_ref), channel_id=1, source_target_pairs={{0,8},{8,16},{16,24},{24,0},{1,9},{9,17},{17,25},{25,1},{2,10},{10... | collective-permute-start | bytes 98312 | tf_op jit(solution)/shard_map/ppermute | solution.py:281
  21.2 18.7 %collective-permute-start.16 = (f32[8,8,128]{2,1,0:T(8,128)S(1)}, f32[8,8,128]{2,1,0:T(8,128)S(1)}, u32[]{:S(2)}, u32[]{:S(2)}) collective-permute-start(f32[8,8,128]{2,1,0:T(8,128)S(1)} %pad_maximum_fusion.1.own_ref), channel_id=1, source_target_pairs={{0,24},{8,0},{16,8},{24,16},{1,25},{9,1},{17,9},{25,17},{2,26},{10... | collective-permute-start | bytes 98312 | tf_op jit(solution)/shard_map/ppermute | solution.py:281
  22.6 9.2 %collective-permute-start.6 = (bf16[64,512]{1,0:T(8,128)(2,1)S(1)}, bf16[64,512]{1,0:T(8,128)(2,1)S(1)}, u32[]{:S(2)}, u32[]{:S(2)}) collective-permute-start(bf16[64,512]{1,0:T(8,128)(2,1)S(1)} %get-tuple-element.23), channel_id=1, source_target_pairs={{0,4},{1,5},{2,6},{3,7},{4,0},{5,1},{6,2},{7,3},{8,12},{9,13},{10,... | collective-permute-start | bytes 196616 | tf_op jit(solution)/shard_map/ppermute | solution.py:293
  22.6 9.9 %collective-permute-start.7 = (bf16[64,512]{1,0:T(8,128)(2,1)S(1)}, bf16[64,512]{1,0:T(8,128)(2,1)S(1)}, u32[]{:S(2)}, u32[]{:S(2)}) collective-permute-start(bf16[64,512]{1,0:T(8,128)(2,1)S(1)} %get-tuple-element.24), channel_id=1, source_target_pairs={{0,5},{1,4},{2,7},{3,6},{4,1},{5,0},{6,3},{7,2},{8,13},{9,12},{10,... | collective-permute-start | bytes 196616 | tf_op jit(solution)/shard_map/ppermute | solution.py:293
  25.1 7.4 %collective-permute-start.9 = (bf16[64,512]{1,0:T(8,128)(2,1)S(1)}, bf16[64,512]{1,0:T(8,128)(2,1)S(1)}, u32[]{:S(2)}, u32[]{:S(2)}) collective-permute-start(bf16[64,512]{1,0:T(8,128)(2,1)S(1)} %get-tuple-element.25), channel_id=1, source_target_pairs={{0,6},{1,7},{2,4},{3,5},{4,2},{5,3},{6,0},{7,1},{8,14},{9,15},{10,... | collective-permute-start | bytes 196616 | tf_op jit(solution)/shard_map/ppermute | solution.py:293
  26.0 6.5 %copy-start = (bf16[3,128,512]{2,1,0:T(8,128)(2,1)S(1)}, bf16[3,128,512]{2,1,0:T(8,128)(2,1)}, u32[]{:S(2)}) copy-start(bf16[3,128,512]{2,1,0:T(8,128)(2,1)} %slope_ref.1) | copy-start | bytes 1179652
  26.1 6.4 %copy-start.1 = (bf16[128,512]{1,0:T(8,128)(2,1)S(1)}, bf16[128,512]{1,0:T(8,128)(2,1)}, u32[]{:S(2)}) copy-start(bf16[128,512]{1,0:T(8,128)(2,1)} %image_ref.1) | copy-start | bytes 393220
  33.7 1.4 %collective-permute-start.11 = (f32[24,128]{1,0:T(8,128)S(1)}, f32[24,128]{1,0:T(8,128)S(1)}, u32[]{:S(2)}, u32[]{:S(2)}) collective-permute-start(f32[24,128]{1,0:T(8,128)S(1)} %get-tuple-element.28), channel_id=1, source_target_pairs={{0,1},{1,0},{2,3},{3,2},{4,5},{5,4},{6,7},{7,6},{8,9},{9,8},{10,11... | collective-permute-start | bytes 36872 | tf_op jit(solution)/shard_map/ppermute | solution.py:281
  35.2 4.8 %collective-permute-start.12 = (f32[8,128]{1,0:T(8,128)S(1)}, f32[8,128]{1,0:T(8,128)S(1)}, u32[]{:S(2)}, u32[]{:S(2)}) collective-permute-start(f32[8,128]{1,0:T(8,128)S(1)} %get-tuple-element.30), channel_id=1, source_target_pairs={{0,8},{8,16},{16,24},{24,0},{1,9},{9,17},{17,25},{25,1},{2,10},{10... | collective-permute-start | bytes 12296 | tf_op jit(solution)/shard_map/ppermute | solution.py:281
  35.8 5.4 %collective-permute-start.13 = (f32[8,128]{1,0:T(8,128)S(1)}, f32[8,128]{1,0:T(8,128)S(1)}, u32[]{:S(2)}, u32[]{:S(2)}) collective-permute-start(f32[8,128]{1,0:T(8,128)S(1)} %get-tuple-element.31), channel_id=1, source_target_pairs={{0,2},{2,4},{4,6},{6,0},{1,3},{3,5},{5,7},{7,1},{8,10},{10,12},{12... | collective-permute-start | bytes 12296 | tf_op jit(solution)/shard_map/ppermute | solution.py:281
  37.9 7.2 %collective-permute-start.14 = (f32[8,128]{1,0:T(8,128)S(1)}, f32[8,128]{1,0:T(8,128)S(1)}, u32[]{:S(2)}, u32[]{:S(2)}) collective-permute-start(f32[8,128]{1,0:T(8,128)S(1)} %get-tuple-element.32), channel_id=1, source_target_pairs={{0,10},{2,12},{4,14},{6,8},{8,18},{10,20},{12,22},{14,16},{16,26},... | collective-permute-start | bytes 12296 | tf_op jit(solution)/shard_map/ppermute | solution.py:289

commit v2 on v1

--- a/solution.py
+++ b/solution.py
@@ -22,6 +22,9 @@
 SLOT = 30
 META = 32
 
+VOXELS = 4096
+TABLE = VOXELS + 16
+
 
 def iota(shape, dim):
     return lax.broadcasted_iota(jnp.int32, shape, dim)
@@ -39,31 +42,38 @@
     return [(wide & (1 << bit)) != 0 for bit in range(3)]
 
 
-def sample_kernel(cap, readers, swap, block_row, send_ref, meta_ref, table_ref, *rest):
-    outs, (along_a, along_b, along_c) = rest[:-3], rest[-3:]
-    holder = lax.axis_index("gy") * lax.axis_size("gz") + lax.axis_index("gz")
-    row = send_ref[pl.ds(block_row(), 1), :]
-    if swap:
-        row = jnp.where(lax.axis_index("gz") == 1, pltpu.roll(row, LANES // 2, 1), row)
-    pick = (iota((LANES, LANES), 0) == row).astype(jnp.bfloat16)
-    slot = iota((LANES, LANES), 0)
-    meta = jnp.zeros((META, LANES), jnp.float32)
-    for r in range(readers):
-        wanted = meta_ref[r, SLOT : SLOT + 1, :].astype(jnp.int32)
-        hit = (wanted == holder * cap + slot - r * cap) & (slot // cap == r)
-        meta = meta + lax.dot_general(
-            meta_ref[r].astype(jnp.bfloat16),
-            hit.astype(jnp.bfloat16),
-            (((1,), (1,)), ((), ())),
-            preferred_element_type=jnp.float32,
-        )
+def pack_kernel(fraction_ref, displacement_ref, offset_ref, slot_ref, out_ref):
+    out_ref[:DISP, :] = fraction_ref[...].astype(jnp.float32)
+    out_ref[DISP:OFFS, :] = displacement_ref[...]
+    out_ref[OFFS:SLOT, :] = offset_ref[...].astype(jnp.float32)
+    out_ref[SLOT : SLOT + 1, :] = slot_ref[...].astype(jnp.float32)
+    out_ref[SLOT + 1 :, :] = jnp.zeros((META - SLOT - 1, LANES), jnp.float32)
+
+
+def table_kernel(block_ref, send_ref, out_ref):
+    for start in range(0, VOXELS, 512):
+        out_ref[start : start + 512, :] = block_ref[:, start : start + 512].T
+    rows = send_ref.shape[0]
+    listed = jnp.concatenate(
+        [send_ref[...].astype(jnp.float32), jnp.zeros((TABLE - VOXELS - rows, LANES), jnp.float32)],
+        axis=0,
+    )
+    out_ref[VOXELS:, :] = listed.astype(jnp.bfloat16)
+
+
+def interpolated(table_refs, pick, meta, along_a, along_b, along_c):
     upper = meta[:24]
     lower = 1.0 - upper
     offsets = meta[OFFS : OFFS + 3].astype(jnp.int32)
     bits = offset_bits(offsets[0:1], 16)
     for b in range(16):
+        starts = [256 * a + 16 * b for a in range(16)]
         rows = jnp.concatenate(
-            [table_ref[256 * a + 16 * b : 256 * a + 16 * b + 16, :] for a in range(16)], axis=0
+            [
+                jnp.concatenate([ref[start : start + 16, :] for start in starts], axis=0)
+                for ref in table_refs
+            ],
+            axis=1,
         )
         voxels = jnp.dot(rows, pick, preferred_element_type=jnp.float32)
         window = shifted([voxels[16 * a : 16 * a + 16] for a in range(16)], bits)
@@ -89,19 +99,60 @@
             along_c[pl.ds(64 * i + k, 8, stride=8), :] = (
                 lower[16 + k : 17 + k] * window[k] + upper[16 + k : 17 + k] * window[k + 1]
             )
-    samples = along_c[...].T.astype(jnp.bfloat16)
-    height = LANES // len(outs)
-    for n, out in enumerate(outs):
-        out[...] = samples[height * n : height * n + height]
-
-
-def sample_call(cap, readers, swap, block_row, pieces, send_rows, meta, table):
+    return along_c[...].T.astype(jnp.bfloat16)
+
+
+def slot_meta(meta, slots):
+    wanted = meta[SLOT : SLOT + 1].astype(jnp.int32)
+    return lax.dot_general(
+        meta.astype(jnp.bfloat16),
+        (wanted == slots).astype(jnp.bfloat16),
+        (((1,), (1,)), ((), ())),
+        preferred_element_type=jnp.float32,
+    )
+
+
+def pair_kernel(distance, meta_ref, own_ref, mate_ref, *rest):
+    out_ref, scratch = rest[-4], rest[-3:]
+    gy, gz = lax.axis_index("gy"), lax.axis_index("gz")
+    half = LANES // 2
+    slot = iota((LANES, LANES), 0)
+    slots = (((2 * gy + gz) ^ (slot // half)) * half) + slot % half
+    meta = slot_meta(meta_ref[...], slots)
+    chip = gy ^ distance
+    lists = [ref[VOXELS:, :].astype(jnp.float32) for ref in (own_ref, mate_ref)]
+    here = iota(lists[0].shape, 0) == chip
+    own, mate = [
+        jnp.sum(jnp.where(here, listed, 0.0), axis=0, keepdims=True).astype(jnp.int32)
+        for listed in lists
+    ]
+    first = gz == 0
+    own = jnp.where(first, own, pltpu.roll(own, half, 1))
+    mate = jnp.where(first, pltpu.roll(mate, half, 1), mate)
+    row = jnp.where(iota((1, LANES), 1) < half, own, mate + LANES)
+    pick = (iota((2 * LANES, LANES), 0) == row).astype(jnp.bfloat16)
+    out_ref[...] = interpolated((own_ref, mate_ref), pick, meta, *scratch)
+
+
+def group_kernel(group, cap, meta_ref, table_ref, out_ref, *scratch):
+    holder = lax.axis_index("gy") * lax.axis_size("gz") + lax.axis_index("gz")
+    slot = iota((LANES, LANES), 0)
+    meta = jnp.zeros((META, LANES), jnp.float32)
+    for r in range(LANES // cap):
+        slots = jnp.where(slot // cap == r, holder * cap + slot - r * cap, -1)
+        meta = meta + slot_meta(meta_ref[r], slots)
+    row = table_ref[VOXELS:, :].astype(jnp.float32)[group : group + 1].astype(jnp.int32)
+    pick = (iota((LANES, LANES), 0) == row).astype(jnp.bfloat16)
+    out_ref[...] = interpolated((table_ref,), pick, meta, *scratch)
+
+
+def sample_call(kernel, *operands):
     vmem = pl.BlockSpec(memory_space=pltpu.VMEM)
     return pl.pallas_call(
-        functools.partial(sample_kernel, cap, readers, swap, block_row),
-        out_shape=[jax.ShapeDtypeStruct((LANES // pieces, 512), jnp.bfloat16)] * pieces,
-        in_specs=[vmem] * 3,
-        out_specs=[vmem] * pieces,
+        kernel,
+        out_shape=jax.ShapeDtypeStruct((LANES, 512), jnp.bfloat16),
+        in_specs=[vmem] * len(operands),
+        out_specs=vmem,
         scratch_shapes=[
             pltpu.VMEM((2048, LANES), jnp.float32),
             pltpu.VMEM((1024, LANES), jnp.float32),
@@ -109,10 +160,10 @@
         ],
         compiler_params=pltpu.CompilerParams(vmem_limit_bytes=24 << 20),
         cost_estimate=pl.CostEstimate(
-            flops=2 * 4096 * 128 * 128, bytes_accessed=2 << 20, transcendentals=0
+            flops=2 * 4096 * 128 * 256, bytes_accessed=2 << 20, transcendentals=0
         ),
         name="interpolate",
-    )(send_rows, meta, table)
+    )(*operands)
 
 
 def shape_table():
@@ -209,6 +260,7 @@
                 )
                 if relative:
                     peer = peer ^ own
+                    peer = peer % 2 * sizes[1] + peer // 2
                 fields[ox, oy, oz] = jnp.where(inside, slabs[ox][peer], 0.0)
 
     def along(axis, sign, centre, beyond):
@@ -263,11 +315,22 @@
         )
 
 
-def small_call(kernel, shapes, name, *operands):
+def collect_kernel(*refs):
+    for n, ref in enumerate(refs[:-1]):
+        refs[-1][n] = ref[DISP:META, :]
+
+
+def join_kernel(first_ref, second_ref, out_ref):
+    count = first_ref.shape[0]
+    out_ref[:count] = first_ref[...]
+    out_ref[count:] = second_ref[...]
+
+
+def small_call(kernel, shapes, name, *operands, dtype=jnp.float32):
     vmem = pl.BlockSpec(memory_space=pltpu.VMEM)
     return pl.pallas_call(
         kernel,
-        out_shape=[jax.ShapeDtypeStruct(shape, jnp.float32) for shape in shapes],
+        out_shape=[jax.ShapeDtypeStruct(shape, dtype) for shape in shapes],
         in_specs=[vmem] * len(operands),
         out_specs=[vmem] * len(shapes),
         compiler_params=pltpu.CompilerParams(vmem_limit_bytes=24 << 20),
@@ -306,49 +369,49 @@
     n_y, n_z = lax.axis_size("gy"), lax.axis_size("gz")
     peers = n_y * n_z
     cap = send_list.shape[0] // peers
-    f32 = jnp.float32
-    packed = jnp.concatenate(
-        [
-            fractions.astype(f32),
-            displacement,
-            offsets.astype(f32),
-            recv_slot.astype(f32)[None],
-            jnp.zeros((1, LANES), f32),
-        ],
-        axis=0,
-    )
-    table = deformed_blocks.T
-    send_rows = send_list.reshape(-1, LANES)
+    (packed,) = small_call(
+        pack_kernel,
+        [(META, LANES)],
+        "pack",
+        fractions,
+        displacement,
+        offsets,
+        recv_slot[None],
+    )
+    (table,) = small_call(
+        table_kernel,
+        [(TABLE, LANES)],
+        "table",
+        deformed_blocks,
+        send_list.reshape(-1, LANES),
+        dtype=jnp.bfloat16,
+    )
     relative = n_z == 2 and n_y in (2, 4) and 2 * cap == LANES
     if relative:
-        chip = jnp.stack([packed, swapped(packed, "gz", 1)])
-        metas = [chip] + [swapped(chip, "gy", d) for d in range(1, n_y)]
-        arrived = [None] * peers
-        order = list(range(n_y - 1, 0, -1)) + [0]
-        for d in order:
-            pair = sample_call(
-                cap, 2, True, lambda d=d: lax.axis_index("gy") ^ d, 2, send_rows, metas[d], table
-            )
-            for other in range(2):
-                mask = 2 * d + other
-                arrived[mask] = swapped(pair[other], SLAB, mask) if mask else pair[other]
-        slab = jnp.concatenate([meta[:, DISP:META] for meta in metas], axis=0)
+        metas = [packed] + [swapped(packed, "gy", d) for d in range(1, n_y)]
+        mate = swapped(table, "gz", 1)
+        arrived = [None] * n_y
+        previous = []
+        for d in range(n_y - 1, -1, -1):
+            samples = sample_call(
+                functools.partial(pair_kernel, d), metas[d], table, mate, *previous
+            )
+            previous = [samples]
+            arrived[d] = swapped(samples, "gy", d) if d else samples
+        (column,) = small_call(collect_kernel, [(n_y, 8, LANES)], "collect", *metas)
+        (slab,) = small_call(
+            join_kernel, [(peers, 8, LANES)], "join", column, swapped(column, "gz", 1)
+        )
     else:
         gathered = lax.all_gather(packed, SLAB, axis=0)
         readers = LANES // cap
-        groups = peers // readers
         samples = [
             sample_call(
-                cap,
-                readers,
-                False,
-                lambda g=g: g,
-                1,
-                send_rows,
+                functools.partial(group_kernel, g, cap),
                 gathered[g * readers : (g + 1) * readers],
                 table,
-            )[0]
-            for g in range(groups)
+            )
+            for g in range(peers // readers)
         ]
         outgoing = jnp.concatenate(samples, axis=0)
         arrived = [lax.all_to_all(outgoing, SLAB, split_axis=0, concat_axis=0, tiled=True)]

time: 46 us -> 39.3 us (0.85)
  starting transfers between devices: 22.4 us -> 16.2 us
  local copies, waits for them, and re-layouts: 4.14 us -> 2.35 us
  waiting for transfers between devices: 12.2 us -> 13.3 us
  Pallas kernels: 5.88 us -> 6.94 us
  other arithmetic: 0.91 us -> 0.19 us
    ppermute x11 -> x8, starting transfers between devices: 14.3 us -> 10.7 us  [swapped(): lax.ppermute(value, axes, [(i, i ^ mask) for i in range(lax.axis_size(axe...]
    ppermute x5, starting transfers between devices: 6.24 us -> 4.75 us  [ring(): lax.ppermute(value, axes, [(i, (i + distance) % count) for i in range(cou...]
    ppermute x1, starting transfers between devices: 1.87 us -> 0.76 us  [ring_2(): return lax.ppermute(value, ('gx', 'gy'), route)]
    pallas_call x8 -> x12, Pallas kernels: 5.88 us -> 6.94 us  [the longest x4 4.44 us: sample_call(): pl.pallas_call(kernel, out_shape=jax.ShapeDtypeStruct((LANES, 512), jnp.b...]
    ppermute x11 -> x8, waiting for transfers between devices: 6.24 us -> 7.07 us  [swapped(): lax.ppermute(value, axes, [(i, i ^ mask) for i in range(lax.axis_size(axe...]
    convert_element_type x1 -> x0, other arithmetic: 0.71 us -> none  [local(): offsets.astype(f32)]
    concatenate x1 -> x0, local copies, waits for them, and re-layouts: 0.71 us -> none  [local(): jnp.concatenate([fractions.astype(f32), displacement, offsets.astype(f32)...]
    slice x5 -> x0, local copies, waits for them, and re-layouts: 0.69 us -> none  [local(): slab = jnp.concatenate([meta[:, DISP:META] for meta in metas], axis=0)]
  transfers between devices with their start and end apart: 17 -> 14, of which waited for: 5 -> 6; matrix products, arithmetic and copies ran while one was open for 5% -> 2% of each run, Pallas kernels for 12% -> 15%
where the time goes in v2:
time: 39.3 us; the launch traced here: 39.1 us
  starting transfers between devices  16.2 us (41%)
  waiting for transfers between devices  13.3 us (34%)
  Pallas kernels  6.94 us (18%)
  local copies, waits for them, and re-layouts  2.35 us (6%)
    ppermute x8, starting transfers between devices, swapped(): lax.ppermute(value, axes, [(i, i ^ mask) for i in range(lax.axis_size(axe...  10.7 us
    ppermute x8, waiting for transfers between devices, swapped(): lax.ppermute(value, axes, [(i, i ^ mask) for i in range(lax.axis_size(axe...  7.07 us
    ppermute x5, starting transfers between devices, ring(): lax.ppermute(value, axes, [(i, (i + distance) % count) for i in range(cou...  4.75 us
    pallas_call x4, Pallas kernels, sample_call(): pl.pallas_call(kernel, out_shape=jax.ShapeDtypeStruct((LANES, 512), jnp.b...  4.44 us
    ppermute x1, waiting for transfers between devices, ring_2(): return lax.ppermute(value, ('gx', 'gy'), route)  4.41 us
    pallas_call x8, Pallas kernels, small_call(): pl.pallas_call(kernel, out_shape=[jax.ShapeDtypeStruct(shape, dtype) for...  2.5 us
    unnamed x16, local copies, waits for them, and re-layouts  1.93 us
    ppermute x5, waiting for transfers between devices, ring(): lax.ppermute(value, axes, [(i, (i + distance) % count) for i in range(cou...  1.81 us
  transfers between devices with their start and end apart: 14, of which 6 were waited for; matrix products, arithmetic and copies ran while one was open for 2% of the time, Pallas kernels for 15%

profile of v2, /device:TPU:0, one launch (start us, length us, event | category | flops | bytes accessed | tf_op | source)
XLA Modules:
  0.0 39.1 jit_solution(9937482605216792856)
XLA Ops:
  0.0 1.2 %copy-done = bf16[128,4096]{1,0:T(8,128)(2,1)S(1)} copy-done((bf16[128,4096]{1,0:T(8,128)(2,1)S(1)}, bf16[128,4096]{1,0:T(8,128)(2,1)}, u32[]{:S(2)}) %copy-start) | copy-done | bytes 1048600
  1.2 0.7 %copy-done.4 = s32[512]{0:T(512)S(1)} copy-done((s32[512]{0:T(512)S(1)}, s32[512]{0:T(512)}, u32[]{:S(2)}) %copy-start.4) | copy-done | bytes 2072
  1.9 0.3 table.1.own_ref
  2.2 0.5 %collective-permute-start = (bf16[4112,128]{1,0:T(8,128)(2,1)S(1)}, bf16[4112,128]{1,0:T(8,128)(2,1)S(1)}, u32[]{:S(2)}, u32[]{:S(2)}) collective-permute-start(bf16[4112,128]{1,0:T(8,128)(2,1)S(1)} %table.1.own_ref), channel_id=1, source_target_pairs={{0,1},{1,0},{2,3},{3,2},{4,5},{5,4},{6,7},{7,6},{8,9},{9,8},{10,11... | collective-permute-start | bytes 3158024 | tf_op jit(solution)/shard_map/ppermute | solution.py:356
  2.8 0.0 copy-done.3
  2.8 0.0 copy-done.5
  2.8 4.9 %collective-permute-start.3 = (f32[32,128]{1,0:T(8,128)S(1)}, f32[32,128]{1,0:T(8,128)S(1)}, u32[]{:S(2)}, u32[]{:S(2)}) collective-permute-start(f32[32,128]{1,0:T(8,128)S(1)} %pack.1.meta_ref.refs_0_), channel_id=1, source_target_pairs={{0,6},{2,4},{4,2},{6,0},{1,7},{3,5},{5,3},{7,1},{8,14},{10,12},{12... | collective-permute-start | bytes 49160 | tf_op jit(solution)/shard_map/ppermute | solution.py:356
  7.7 0.0 collective-permute-start.2
  7.7 0.6 %collective-permute-start.1 = (f32[32,128]{1,0:T(8,128)S(1)}, f32[32,128]{1,0:T(8,128)S(1)}, u32[]{:S(2)}, u32[]{:S(2)}) collective-permute-start(f32[32,128]{1,0:T(8,128)S(1)} %pack.1.meta_ref.refs_0_), channel_id=1, source_target_pairs={{0,2},{2,0},{4,6},{6,4},{1,3},{3,1},{5,7},{7,5},{8,10},{10,8},{12,... | collective-permute-start | bytes 49160 | tf_op jit(solution)/shard_map/ppermute | solution.py:356
  8.4 0.1 broadcast_multiply_fusion.1
  8.5 1.0 %collective-permute-done.3.meta_ref.refs_3_ = f32[32,128]{1,0:T(8,128)S(1)} collective-permute-done((f32[32,128]{1,0:T(8,128)S(1)}, f32[32,128]{1,0:T(8,128)S(1)}, u32[]{:S(2)}, u32[]{:S(2)}) %collective-permute-start.3) | collective-permute-done | bytes 16416 | tf_op jit(solution)/shard_map/ppermute | solution.py:356
  9.5 2.9 %collective-permute-done.2.meta_ref.refs_2_ = f32[32,128]{1,0:T(8,128)S(1)} collective-permute-done((f32[32,128]{1,0:T(8,128)S(1)}, f32[32,128]{1,0:T(8,128)S(1)}, u32[]{:S(2)}, u32[]{:S(2)}) %collective-permute-start.2) | collective-permute-done | bytes 16416 | tf_op jit(solution)/shard_map/ppermute | solution.py:356
  12.4 0.0 collective-permute-done.1.meta_ref.refs_1_
  12.4 0.0 collective-permute-start.11
  12.4 0.0 collective-permute-done.mate_ref
  12.4 1.1 %interpolate.4.rest_0_ = bf16[128,512]{1,0:T(8,128)(2,1)S(1)} custom-call(f32[32,128]{1,0:T(8,128)S(1)} %collective-permute-done.3.meta_ref.refs_3_, bf16[4112,128]{1,0:T(8,128)(2,1)S(1)} %table.1.own_ref, bf16[4112,128]{1,0:T(8,128)(2,1)S(1)} %collective-permute-done.mate_ref), custom_call_target="tpu_custom_call" | custom-call | flops 268435456 | bytes 2097152 | tf_op jit(solution)/shard_map/interpolate/pallas_call | solution.py:151
  13.5 1.5 %collective-permute-start.6 = (bf16[128,512]{1,0:T(8,128)(2,1)S(1)}, bf16[128,512]{1,0:T(8,128)(2,1)S(1)}, u32[]{:S(2)}, u32[]{:S(2)}) collective-permute-start(bf16[128,512]{1,0:T(8,128)(2,1)S(1)} %interpolate.4.rest_0_), channel_id=1, source_target_pairs={{0,6},{2,4},{4,2},{6,0},{1,7},{3,5},{5,3},{7,1},{8,14},{10,12},{12... | collective-permute-start | bytes 393224 | tf_op jit(solution)/shard_map/ppermute | solution.py:356
  15.0 1.1 %interpolate.5.rest_0_ = bf16[128,512]{1,0:T(8,128)(2,1)S(1)} custom-call(f32[32,128]{1,0:T(8,128)S(1)} %collective-permute-done.2.meta_ref.refs_2_, bf16[4112,128]{1,0:T(8,128)(2,1)S(1)} %table.1.own_ref, bf16[4112,128]{1,0:T(8,128)(2,1)S(1)} %collective-permute-done.mate_ref, bf16[128,512]{1,0:T(8,128)(2,1)S(1)} %interpolate.4.rest_0_), custom_call_target="tpu_custom_call" | custom-call | flops 268435456 | bytes 2097152 | tf_op jit(solution)/shard_map/interpolate/pallas_call | solution.py:151
  16.2 0.6 %collective-permute-start.5 = (bf16[128,512]{1,0:T(8,128)(2,1)S(1)}, bf16[128,512]{1,0:T(8,128)(2,1)S(1)}, u32[]{:S(2)}, u32[]{:S(2)}) collective-permute-start(bf16[128,512]{1,0:T(8,128)(2,1)S(1)} %interpolate.5.rest_0_), channel_id=1, source_target_pairs={{0,4},{2,6},{4,0},{6,2},{1,5},{3,7},{5,1},{7,3},{8,12},{10,14},{12... | collective-permute-start | bytes 393224 | tf_op jit(solution)/shard_map/ppermute | solution.py:356
  16.8 1.1 %interpolate.6.rest_0_ = bf16[128,512]{1,0:T(8,128)(2,1)S(1)} custom-call(f32[32,128]{1,0:T(8,128)S(1)} %collective-permute-done.1.meta_ref.refs_1_, bf16[4112,128]{1,0:T(8,128)(2,1)S(1)} %table.1.own_ref, bf16[4112,128]{1,0:T(8,128)(2,1)S(1)} %collective-permute-done.mate_ref, bf16[128,512]{1,0:T(8,128)(2,1)S(1)} %interpolate.5.rest_0_), custom_call_target="tpu_custom_call" | custom-call | flops 268435456 | bytes 2097152 | tf_op jit(solution)/shard_map/interpolate/pallas_call | solution.py:151
  17.9 2.4 %collective-permute-start.4 = (bf16[128,512]{1,0:T(8,128)(2,1)S(1)}, bf16[128,512]{1,0:T(8,128)(2,1)S(1)}, u32[]{:S(2)}, u32[]{:S(2)}) collective-permute-start(bf16[128,512]{1,0:T(8,128)(2,1)S(1)} %interpolate.6.rest_0_), channel_id=1, source_target_pairs={{0,2},{2,0},{4,6},{6,4},{1,3},{3,1},{5,7},{7,5},{8,10},{10,8},{12,... | collective-permute-start | bytes 393224 | tf_op jit(solution)/shard_map/ppermute | solution.py:356
  20.3 0.1 broadcast_multiply_fusion
  20.4 0.2 mul.41
  20.6 0.1 copy.10
  20.7 0.1 copy.11.slot_ref
  20.9 0.0 collective-permute-done.11.second_ref
  20.9 0.0 copy-start.1
  20.9 0.0 copy-start.2
  20.9 1.5 %collective-permute-start.12 = (f32[8,8,128]{2,1,0:T(8,128)S(1)}, f32[8,8,128]{2,1,0:T(8,128)S(1)}, u32[]{:S(2)}, u32[]{:S(2)}) collective-permute-start(f32[8,8,128]{2,1,0:T(8,128)S(1)} %join.1.own_ref), channel_id=1, source_target_pairs={{0,8},{8,16},{16,24},{24,0},{1,9},{9,17},{17,25},{25,1},{2,10},{10... | collective-permute-start | bytes 98312 | tf_op jit(solution)/shard_map/ppermute | solution.py:344
  22.5 1.4 %collective-permute-start.13 = (f32[8,8,128]{2,1,0:T(8,128)S(1)}, f32[8,8,128]{2,1,0:T(8,128)S(1)}, u32[]{:S(2)}, u32[]{:S(2)}) collective-permute-start(f32[8,8,128]{2,1,0:T(8,128)S(1)} %join.1.own_ref), channel_id=1, source_target_pairs={{0,24},{8,0},{16,8},{24,16},{1,25},{9,1},{17,9},{25,17},{2,26},{10... | collective-permute-start | bytes 98312 | tf_op jit(solution)/shard_map/ppermute | solution.py:344
  23.9 1.1 %interpolate.7.rest_0_ = bf16[128,512]{1,0:T(8,128)(2,1)S(1)} custom-call(f32[32,128]{1,0:T(8,128)S(1)} %pack.1.meta_ref.refs_0_, bf16[4112,128]{1,0:T(8,128)(2,1)S(1)} %table.1.own_ref, bf16[4112,128]{1,0:T(8,128)(2,1)S(1)} %collective-permute-done.mate_ref, bf16[128,512]{1,0:T(8,128)(2,1)S(1)} %interpolate.6.rest_0_), custom_call_target="tpu_custom_call" | custom-call | flops 268435456 | bytes 2097152 | tf_op jit(solution)/shard_map/interpolate/pallas_call | solution.py:151
  25.0 0.0 collective-permute-done.4.rest_1_
  25.0 3.2 %collective-permute-done.5.rest_2_ = bf16[128,512]{1,0:T(8,128)(2,1)S(1)} collective-permute-done((bf16[128,512]{1,0:T(8,128)(2,1)S(1)}, bf16[128,512]{1,0:T(8,128)(2,1)S(1)}, u32[]{:S(2)}, u32[]{:S(2)}) %collective-permute-start.5) | collective-permute-done | bytes 131104 | tf_op jit(solution)/shard_map/ppermute | solution.py:356
  28.2 0.0 collective-permute-done.6.rest_3_
  28.2 1.2 %forces.1 = (f32[24,128]{1,0:T(8,128)S(1)}, f32[24,128]{1,0:T(8,128)S(1)}) custom-call(s32[128,1]{1,0:T(8,128)S(1)} %copy.11.slot_ref, bf16[128,512]{1,0:T(8,128)(2,1)S(1)} %copy-done.2, bf16[3,128,512]{2,1,0:T(8,128)(2,1)S(1)} %copy-done.1, f32[512,128]{1,0:T(8,128)S(1)} %pad.4.shape_ref, bf16[128,512]{1,0:T(8,128)(2,1)S(1)} %interpolate.7.rest_0_, ...), custom_call_target="tpu_custom_call" | custom-call | flops 1048576 | bytes 1048576 | tf_op jit(solution)/shard_map/forces/pallas_call | solution.py:331
  29.4 0.0 collective-permute-start.7
  29.4 1.2 %collective-permute-done.7.arrived_ref = f32[24,128]{1,0:T(8,128)S(1)} collective-permute-done((f32[24,128]{1,0:T(8,128)S(1)}, f32[24,128]{1,0:T(8,128)S(1)}, u32[]{:S(2)}, u32[]{:S(2)}) %collective-permute-start.7) | collective-permute-done | bytes 12320 | tf_op jit(solution)/shard_map/ppermute | solution.py:344
  30.5 0.2 layers.1
  30.7 0.8 %collective-permute-start.10 = (f32[8,128]{1,0:T(8,128)S(1)}, f32[8,128]{1,0:T(8,128)S(1)}, u32[]{:S(2)}, u32[]{:S(2)}) collective-permute-start(f32[8,128]{1,0:T(8,128)S(1)} %get-tuple-element.16), channel_id=1, source_target_pairs={{0,10},{2,12},{4,14},{6,8},{8,18},{10,20},{12,22},{14,16},{16,26},... | collective-permute-start | bytes 12296 | tf_op jit(solution)/shard_map/ppermute | solution.py:352
  31.5 1.5 %collective-permute-start.8 = (f32[8,128]{1,0:T(8,128)S(1)}, f32[8,128]{1,0:T(8,128)S(1)}, u32[]{:S(2)}, u32[]{:S(2)}) collective-permute-start(f32[8,128]{1,0:T(8,128)S(1)} %get-tuple-element.14), channel_id=1, source_target_pairs={{0,8},{8,16},{16,24},{24,0},{1,9},{9,17},{17,25},{25,1},{2,10},{10... | collective-permute-start | bytes 12296 | tf_op jit(solution)/shard_map/ppermute | solution.py:344
  32.9 0.3 collective-permute-start.9
  33.2 0.0 collective-permute-done.12.below_ref
  33.2 0.0 collective-permute-done.13.above_ref
  33.2 0.3 stiffness.1.stiff_ref
  33.5 4.4 %collective-permute-done.10.xy_ref = f32[8,128]{1,0:T(8,128)S(1)} collective-permute-done((f32[8,128]{1,0:T(8,128)S(1)}, f32[8,128]{1,0:T(8,128)S(1)}, u32[]{:S(2)}, u32[]{:S(2)}) %collective-permute-start.10) | collective-permute-done | bytes 4128 | tf_op jit(solution)/shard_map/ppermute | solution.py:352
  37.9 0.0 collective-permute-done.8.x_ref
  37.9 0.6 %collective-permute-done.9.y_ref = f32[8,128]{1,0:T(8,128)S(1)} collective-permute-done((f32[8,128]{1,0:T(8,128)S(1)}, f32[8,128]{1,0:T(8,128)S(1)}, u32[]{:S(2)}, u32[]{:S(2)}) %collective-permute-start.9) | collective-permute-done | bytes 4128 | tf_op jit(solution)/shard_map/ppermute | solution.py:344
  38.5 0.6 %total.1 = f32[3,128]{1,0:T(4,128)} custom-call(f32[8,128]{1,0:T(8,128)S(1)} %get-tuple-element.13.own_ref, f32[8,128]{1,0:T(8,128)S(1)} %collective-permute-done.8.x_ref, f32[8,128]{1,0:T(8,128)S(1)} %collective-permute-done.9.y_ref, f32[8,128]{1,0:T(8,128)S(1)} %collective-permute-done.10.xy_ref, f32[8,128]{1,0:T(8,128)S(1)} %stiffness.1.stiff_ref), custom_call_target="tpu_custom_call" | custom-call | flops 1048576 | bytes 1048576 | tf_op jit(solution)/shard_map/total/pallas_call | solution.py:331
  (16 shorter events, 0.1 us)
Async XLA Ops:
  0.0 1.2 %copy-start = (bf16[128,4096]{1,0:T(8,128)(2,1)S(1)}, bf16[128,4096]{1,0:T(8,128)(2,1)}, u32[]{:S(2)}) copy-start(bf16[128,4096]{1,0:T(8,128)(2,1)} %block_ref.1) | copy-start | bytes 3145732
  1.2 0.7 %copy-start.4 = (s32[512]{0:T(512)S(1)}, s32[512]{0:T(512)}, u32[]{:S(2)}) copy-start(s32[512]{0:T(512)} %param.14) | copy-start | bytes 6148
  1.9 0.9 %copy-start.3 = (bf16[24,128]{1,0:T(8,128)(2,1)S(1)}, bf16[24,128]{1,0:T(8,128)(2,1)}, u32[]{:S(2)}) copy-start(bf16[24,128]{1,0:T(8,128)(2,1)} %fraction_ref.1) | copy-start | bytes 18436
  1.9 0.9 %copy-start.5 = (s32[128]{0:T(128)S(1)}, s32[128]{0:T(128)}, u32[]{:S(2)}) copy-start(s32[128]{0:T(128)} %param.15) | copy-start | bytes 1540
  1.9 0.9 %copy-start.6 = (f32[3,128]{1,0:T(4,128)S(1)}, f32[3,128]{1,0:T(4,128)}, u32[]{:S(2)}) copy-start(f32[3,128]{1,0:T(4,128)} %displacement_ref.1) | copy-start | bytes 4612
  1.9 0.9 %copy-start.7 = (s32[3,128]{1,0:T(4,128)S(1)}, s32[3,128]{1,0:T(4,128)}, u32[]{:S(2)}) copy-start(s32[3,128]{1,0:T(4,128)} %offset_ref.1) | copy-start | bytes 4612
  2.2 10.1 %collective-permute-start = (bf16[4112,128]{1,0:T(8,128)(2,1)S(1)}, bf16[4112,128]{1,0:T(8,128)(2,1)S(1)}, u32[]{:S(2)}, u32[]{:S(2)}) collective-permute-start(bf16[4112,128]{1,0:T(8,128)(2,1)S(1)} %table.1.own_ref), channel_id=1, source_target_pairs={{0,1},{1,0},{2,3},{3,2},{4,5},{5,4},{6,7},{7,6},{8,9},{9,8},{10,11... | collective-permute-start | bytes 3158024 | tf_op jit(solution)/shard_map/ppermute | solution.py:356
  2.8 6.7 %collective-permute-start.3 = (f32[32,128]{1,0:T(8,128)S(1)}, f32[32,128]{1,0:T(8,128)S(1)}, u32[]{:S(2)}, u32[]{:S(2)}) collective-permute-start(f32[32,128]{1,0:T(8,128)S(1)} %pack.1.meta_ref.refs_0_), channel_id=1, source_target_pairs={{0,6},{2,4},{4,2},{6,0},{1,7},{3,5},{5,3},{7,1},{8,14},{10,12},{12... | collective-permute-start | bytes 49160 | tf_op jit(solution)/shard_map/ppermute | solution.py:356
  7.7 4.6 %collective-permute-start.2 = (f32[32,128]{1,0:T(8,128)S(1)}, f32[32,128]{1,0:T(8,128)S(1)}, u32[]{:S(2)}, u32[]{:S(2)}) collective-permute-start(f32[32,128]{1,0:T(8,128)S(1)} %pack.1.meta_ref.refs_0_), channel_id=1, source_target_pairs={{0,4},{2,6},{4,0},{6,2},{1,5},{3,7},{5,1},{7,3},{8,12},{10,14},{12... | collective-permute-start | bytes 49160 | tf_op jit(solution)/shard_map/ppermute | solution.py:356
  7.7 4.6 %collective-permute-start.1 = (f32[32,128]{1,0:T(8,128)S(1)}, f32[32,128]{1,0:T(8,128)S(1)}, u32[]{:S(2)}, u32[]{:S(2)}) collective-permute-start(f32[32,128]{1,0:T(8,128)S(1)} %pack.1.meta_ref.refs_0_), channel_id=1, source_target_pairs={{0,2},{2,0},{4,6},{6,4},{1,3},{3,1},{5,7},{7,5},{8,10},{10,8},{12,... | collective-permute-start | bytes 49160 | tf_op jit(solution)/shard_map/ppermute | solution.py:356
  12.4 8.5 %collective-permute-start.11 = (f32[4,8,128]{2,1,0:T(8,128)S(1)}, f32[4,8,128]{2,1,0:T(8,128)S(1)}, u32[]{:S(2)}, u32[]{:S(2)}) collective-permute-start(f32[4,8,128]{2,1,0:T(8,128)S(1)} %collect.1.first_ref), channel_id=1, source_target_pairs={{0,1},{1,0},{2,3},{3,2},{4,5},{5,4},{6,7},{7,6},{8,9},{9,8},{10,11... | collective-permute-start | bytes 49160 | tf_op jit(solution)/shard_map/ppermute | solution.py:356
  13.5 14.7 %collective-permute-start.6 = (bf16[128,512]{1,0:T(8,128)(2,1)S(1)}, bf16[128,512]{1,0:T(8,128)(2,1)S(1)}, u32[]{:S(2)}, u32[]{:S(2)}) collective-permute-start(bf16[128,512]{1,0:T(8,128)(2,1)S(1)} %interpolate.4.rest_0_), channel_id=1, source_target_pairs={{0,6},{2,4},{4,2},{6,0},{1,7},{3,5},{5,3},{7,1},{8,14},{10,12},{12... | collective-permute-start | bytes 393224 | tf_op jit(solution)/shard_map/ppermute | solution.py:356
  16.2 12.0 %collective-permute-start.5 = (bf16[128,512]{1,0:T(8,128)(2,1)S(1)}, bf16[128,512]{1,0:T(8,128)(2,1)S(1)}, u32[]{:S(2)}, u32[]{:S(2)}) collective-permute-start(bf16[128,512]{1,0:T(8,128)(2,1)S(1)} %interpolate.5.rest_0_), channel_id=1, source_target_pairs={{0,4},{2,6},{4,0},{6,2},{1,5},{3,7},{5,1},{7,3},{8,12},{10,14},{12... | collective-permute-start | bytes 393224 | tf_op jit(solution)/shard_map/ppermute | solution.py:356
  17.9 7.1 %collective-permute-start.4 = (bf16[128,512]{1,0:T(8,128)(2,1)S(1)}, bf16[128,512]{1,0:T(8,128)(2,1)S(1)}, u32[]{:S(2)}, u32[]{:S(2)}) collective-permute-start(bf16[128,512]{1,0:T(8,128)(2,1)S(1)} %interpolate.6.rest_0_), channel_id=1, source_target_pairs={{0,2},{2,0},{4,6},{6,4},{1,3},{3,1},{5,7},{7,5},{8,10},{10,8},{12,... | collective-permute-start | bytes 393224 | tf_op jit(solution)/shard_map/ppermute | solution.py:356
  20.9 7.3 %copy-start.1 = (bf16[3,128,512]{2,1,0:T(8,128)(2,1)S(1)}, bf16[3,128,512]{2,1,0:T(8,128)(2,1)}, u32[]{:S(2)}) copy-start(bf16[3,128,512]{2,1,0:T(8,128)(2,1)} %slope_ref.1) | copy-start | bytes 1179652
  20.9 7.3 %copy-start.2 = (bf16[128,512]{1,0:T(8,128)(2,1)S(1)}, bf16[128,512]{1,0:T(8,128)(2,1)}, u32[]{:S(2)}) copy-start(bf16[128,512]{1,0:T(8,128)(2,1)} %image_ref.1) | copy-start | bytes 393220
  20.9 12.3 %collective-permute-start.12 = (f32[8,8,128]{2,1,0:T(8,128)S(1)}, f32[8,8,128]{2,1,0:T(8,128)S(1)}, u32[]{:S(2)}, u32[]{:S(2)}) collective-permute-start(f32[8,8,128]{2,1,0:T(8,128)S(1)} %join.1.own_ref), channel_id=1, source_target_pairs={{0,8},{8,16},{16,24},{24,0},{1,9},{9,17},{17,25},{25,1},{2,10},{10... | collective-permute-start | bytes 98312 | tf_op jit(solution)/shard_map/ppermute | solution.py:344
  22.5 10.8 %collective-permute-start.13 = (f32[8,8,128]{2,1,0:T(8,128)S(1)}, f32[8,8,128]{2,1,0:T(8,128)S(1)}, u32[]{:S(2)}, u32[]{:S(2)}) collective-permute-start(f32[8,8,128]{2,1,0:T(8,128)S(1)} %join.1.own_ref), channel_id=1, source_target_pairs={{0,24},{8,0},{16,8},{24,16},{1,25},{9,1},{17,9},{25,17},{2,26},{10... | collective-permute-start | bytes 98312 | tf_op jit(solution)/shard_map/ppermute | solution.py:344
  29.4 1.2 %collective-permute-start.7 = (f32[24,128]{1,0:T(8,128)S(1)}, f32[24,128]{1,0:T(8,128)S(1)}, u32[]{:S(2)}, u32[]{:S(2)}) collective-permute-start(f32[24,128]{1,0:T(8,128)S(1)} %get-tuple-element.12), channel_id=1, source_target_pairs={{0,1},{1,0},{2,3},{3,2},{4,5},{5,4},{6,7},{7,6},{8,9},{9,8},{10,11... | collective-permute-start | bytes 36872 | tf_op jit(solution)/shard_map/ppermute | solution.py:344
  30.7 7.2 %collective-permute-start.10 = (f32[8,128]{1,0:T(8,128)S(1)}, f32[8,128]{1,0:T(8,128)S(1)}, u32[]{:S(2)}, u32[]{:S(2)}) collective-permute-start(f32[8,128]{1,0:T(8,128)S(1)} %get-tuple-element.16), channel_id=1, source_target_pairs={{0,10},{2,12},{4,14},{6,8},{8,18},{10,20},{12,22},{14,16},{16,26},... | collective-permute-start | bytes 12296 | tf_op jit(solution)/shard_map/ppermute | solution.py:352
  31.5 6.5 %collective-permute-start.8 = (f32[8,128]{1,0:T(8,128)S(1)}, f32[8,128]{1,0:T(8,128)S(1)}, u32[]{:S(2)}, u32[]{:S(2)}) collective-permute-start(f32[8,128]{1,0:T(8,128)S(1)} %get-tuple-element.14), channel_id=1, source_target_pairs={{0,8},{8,16},{16,24},{24,0},{1,9},{9,17},{17,25},{25,1},{2,10},{10... | collective-permute-start | bytes 12296 | tf_op jit(solution)/shard_map/ppermute | solution.py:344
  32.9 5.6 %collective-permute-start.9 = (f32[8,128]{1,0:T(8,128)S(1)}, f32[8,128]{1,0:T(8,128)S(1)}, u32[]{:S(2)}, u32[]{:S(2)}) collective-permute-start(f32[8,128]{1,0:T(8,128)S(1)} %get-tuple-element.15), channel_id=1, source_target_pairs={{0,2},{2,4},{4,6},{6,0},{1,3},{3,5},{5,7},{7,1},{8,10},{10,12},{12... | collective-permute-start | bytes 12296 | tf_op jit(solution)/shard_map/ppermute | solution.py:344

commit v3 on v2

--- a/solution.py
+++ b/solution.py
@@ -42,23 +42,47 @@
     return [(wide & (1 << bit)) != 0 for bit in range(3)]
 
 
-def pack_kernel(fraction_ref, displacement_ref, offset_ref, slot_ref, out_ref):
-    out_ref[:DISP, :] = fraction_ref[...].astype(jnp.float32)
-    out_ref[DISP:OFFS, :] = displacement_ref[...]
-    out_ref[OFFS:SLOT, :] = offset_ref[...].astype(jnp.float32)
-    out_ref[SLOT : SLOT + 1, :] = slot_ref[...].astype(jnp.float32)
-    out_ref[SLOT + 1 :, :] = jnp.zeros((META - SLOT - 1, LANES), jnp.float32)
-
-
-def table_kernel(block_ref, send_ref, out_ref):
+def shape_kernel(out_ref):
+    voxel, column = iota((512, LANES), 0), iota((512, LANES), 1)
+
+    def weight(index, upper):
+        centre = (index.astype(jnp.float32) + 0.5) * 0.125
+        return jnp.where(upper == 1, centre, 1.0 - centre)
+
+    values = weight(voxel // 64, column // 2 % 2) * weight(voxel // 8 % 8, column % 2)
+    values = values * weight(voxel % 8, column // 4)
+    out_ref[...] = jnp.where(column < 8, values, 0.0)
+
+
+def prepare_kernel(
+    after_ref, fraction_ref, displacement_ref, offset_ref, slot_ref, send_ref, block_ref, packed_ref, table_ref
+):
+    packed_ref[:DISP, :] = fraction_ref[...].astype(jnp.float32)
+    packed_ref[DISP:OFFS, :] = displacement_ref[...]
+    packed_ref[OFFS:SLOT, :] = offset_ref[...].astype(jnp.float32)
+    packed_ref[SLOT : SLOT + 1, :] = slot_ref[...].astype(jnp.float32)
+    packed_ref[SLOT + 1 :, :] = jnp.zeros((META - SLOT - 1, LANES), jnp.float32)
     for start in range(0, VOXELS, 512):
-        out_ref[start : start + 512, :] = block_ref[:, start : start + 512].T
+        table_ref[start : start + 512, :] = block_ref[:, start : start + 512].T
     rows = send_ref.shape[0]
     listed = jnp.concatenate(
         [send_ref[...].astype(jnp.float32), jnp.zeros((TABLE - VOXELS - rows, LANES), jnp.float32)],
         axis=0,
     )
-    out_ref[VOXELS:, :] = listed.astype(jnp.bfloat16)
+    table_ref[VOXELS:, :] = listed.astype(jnp.bfloat16)
+
+
+def vmem_call(kernel, shapes, name, *operands, cost=1 << 20, flops=1 << 20):
+    vmem = pl.BlockSpec(memory_space=pltpu.VMEM)
+    return pl.pallas_call(
+        kernel,
+        out_shape=[jax.ShapeDtypeStruct(shape, dtype) for shape, dtype in shapes],
+        in_specs=[vmem] * len(operands),
+        out_specs=[vmem] * len(shapes),
+        compiler_params=pltpu.CompilerParams(vmem_limit_bytes=24 << 20),
+        cost_estimate=pl.CostEstimate(flops=flops, bytes_accessed=cost, transcendentals=0),
+        name=name,
+    )(*operands)
 
 
 def interpolated(table_refs, pick, meta, along_a, along_b, along_c):
@@ -119,7 +143,7 @@
     slot = iota((LANES, LANES), 0)
     slots = (((2 * gy + gz) ^ (slot // half)) * half) + slot % half
     meta = slot_meta(meta_ref[...], slots)
-    chip = gy ^ distance
+    chip = lax.rem(gy + distance, lax.axis_size("gy"))
     lists = [ref[VOXELS:, :].astype(jnp.float32) for ref in (own_ref, mate_ref)]
     here = iota(lists[0].shape, 0) == chip
     own, mate = [
@@ -160,35 +184,26 @@
         ],
         compiler_params=pltpu.CompilerParams(vmem_limit_bytes=24 << 20),
         cost_estimate=pl.CostEstimate(
-            flops=2 * 4096 * 128 * 256, bytes_accessed=2 << 20, transcendentals=0
+            flops=1, bytes_accessed=1, transcendentals=0
         ),
         name="interpolate",
     )(*operands)
 
 
-def shape_table():
-    centres = (jnp.arange(8, dtype=jnp.float32) + 0.5) / 8.0
-    weights = jnp.stack([1.0 - centres, centres], axis=1)
-    values = (
-        weights[:, None, None, None, :, None]
-        * weights[None, :, None, None, None, :]
-        * weights[None, None, :, :, None, None]
-    ).reshape(512, 8)
-    return jnp.pad(values, ((0, 0), (0, LANES - 8)))
-
-
 def axis_of_lane(rows):
     lane = iota((rows, LANES), 1)
     return lane // (CY * CZ), lane // CZ % CY, lane % CZ
 
 
-def force_kernel(cap, relative, slot_ref, image_ref, slope_ref, shape_ref, *rest):
+def force_kernel(cap, relative, across_ref, slot_ref, image_ref, slope_ref, shape_ref, *rest):
     arrived, (kept_ref, sent_ref) = rest[:-2], rest[-2:]
     total = sum(piece.shape[0] for piece in arrived)
     number = iota((LANES, total), 1)
     if relative:
-        own = lax.axis_index("gy") * lax.axis_size("gz") + lax.axis_index("gz")
-        number = ((number // cap) ^ own) * cap + number % cap
+        n_y = lax.axis_size("gy")
+        chip = lax.rem(lax.axis_index("gy") + n_y - number // (2 * cap), n_y)
+        core = (number // cap % 2) ^ lax.axis_index("gz")
+        number = (2 * chip + core) * cap + number % cap
     hit = (slot_ref[...] == number).astype(jnp.bfloat16)
     rows = jnp.concatenate([piece[...] for piece in arrived], axis=0)
     samples = jnp.dot(hit, rows, preferred_element_type=jnp.float32)
@@ -205,9 +220,10 @@
         carried = pltpu.roll(corners, 4, 0)
         kept_ref[8 * d : 8 * d + 8, :] = corners + jnp.where(at_k > 0, pltpu.roll(carried, 1, 1), 0.0)
         sent_ref[8 * d : 8 * d + 8, :] = jnp.where(at_k == 0, pltpu.roll(carried, LANES - 7, 1), 0.0)
-
-
-def layer_kernel(kept_ref, arrived_ref, own_ref, x_ref, y_ref, xy_ref):
+        sent_ref[8 * d + 4 : 8 * d + 6, :] = across_ref[2 * d : 2 * d + 2, :]
+
+
+def layer_kernel(kept_ref, arrived_ref, stiff_ref, xy_ref, y_ref, x_ref, own_ref):
     at_i, at_j, _ = axis_of_lane(8)
     behind = lax.axis_index("gz") > 0
 
@@ -223,28 +239,91 @@
         leave = jnp.where(at_j == 0, pltpu.roll(carried, LANES - CZ * (CY - 1), 1), 0.0)
         own, x = along_x(stay, pltpu.roll(stay, 6, 0))
         y, xy = along_x(leave, pltpu.roll(leave, 6, 0))
-        for ref, value in ((own_ref, own), (x_ref, x), (y_ref, y), (xy_ref, xy)):
-            ref[d : d + 1, :] = value[0:1]
-
-
-def final_kernel(own_ref, x_ref, y_ref, xy_ref, stiff_ref, out_ref):
+        stiff = stiff_ref[2 * d : 2 * d + 2, :] + arrived_ref[8 * d + 4 : 8 * d + 6, :]
+        row = slice(d, d + 1)
+        xy_ref[row, :] = xy[0:1] * data_weight
+        y_ref[row, :] = y[0:1] * data_weight
+        x_ref[row, :] = x[0:1] * data_weight + stiff[1:2]
+        own_ref[row, :] = own[0:1] * data_weight + stiff[0:1]
+
+
+def final_kernel(own_ref, xy_ref, y_ref, x_ref, out_ref):
     has_x = lax.axis_index("gx") > 0
     has_y = lax.axis_index("gy") > 0
-    force = own_ref[0:3, :]
-    force = force + jnp.where(has_x, x_ref[0:3, :], 0.0)
-    force = force + jnp.where(has_y, y_ref[0:3, :], 0.0)
-    force = force + jnp.where(has_x & has_y, xy_ref[0:3, :], 0.0)
-    out_ref[...] = force * data_weight + stiff_ref[0:3, :]
-
-
-def stiffness_kernel(relative, below_ref, own_ref, above_ref, out_ref):
-    here = [lax.axis_index(name) for name in ("gx", "gy", "gz")]
-    sizes = [lax.axis_size(name) for name in ("gx", "gy", "gz")]
-    own = here[1] * sizes[2] + here[2]
-    slabs = {-1: below_ref, 0: own_ref, 1: above_ref}
+    total = own_ref[0:3, :] + jnp.where(has_x, x_ref[0:3, :], 0.0)
+    total = total + jnp.where(has_y, y_ref[0:3, :], 0.0)
+    out_ref[...] = total + jnp.where(has_x & has_y, xy_ref[0:3, :], 0.0)
+
+
+def navier(fields):
     at = axis_of_lane(8)
     steps = (CY * CZ, CZ, 1)
     extents = (CX, CY, CZ)
+
+    def plus(p, q):
+        return q if p is None else p if q is None else p + q
+
+    def times(factor, p):
+        return None if p is None else factor * p
+
+    def along(axis, sign, centre, beyond):
+        step, extent = steps[axis], extents[axis]
+        back = step * (extent - 1)
+        if sign > 0:
+            inside, near, far = at[axis] < extent - 1, LANES - step, back
+        else:
+            inside, near, far = at[axis] > 0, step, LANES - back
+        if centre is None and beyond is None:
+            return None
+        return jnp.where(
+            inside,
+            0.0 if centre is None else pltpu.roll(centre, near, 1),
+            0.0 if beyond is None else pltpu.roll(beyond, far, 1),
+        )
+
+    def moved(vector, frame=(0, 0, 0), axis=2):
+        if axis < 0:
+            return fields.get(frame)
+        sign = vector[axis]
+        centre = moved(vector, frame, axis - 1)
+        if sign == 0:
+            return centre
+        other = tuple(sign if n == axis else frame[n] for n in range(3))
+        return along(axis, sign, centre, moved(vector, other, axis - 1))
+
+    units = ((1, 0, 0), (0, 1, 0), (0, 0, 1))
+    centre = fields.get((0, 0, 0))
+    laplace = times(-6.0, centre)
+    second = []
+    for unit in units:
+        both = plus(moved(unit), moved(tuple(-n for n in unit)))
+        laplace = plus(laplace, both)
+        second.append(plus(both, times(-2.0, centre)))
+    mixed = {}
+    for outer in range(3):
+        for inner in range(outer + 1, 3):
+            ahead = tuple(p + q for p, q in zip(units[outer], units[inner]))
+            cross = tuple(p - q for p, q in zip(units[outer], units[inner]))
+            aligned = plus(moved(ahead), moved(tuple(-n for n in ahead)))
+            crossed = plus(moved(cross), moved(tuple(-n for n in cross)))
+            mixed[outer, inner] = times(0.25, plus(aligned, times(-1.0, crossed)))
+    rows = []
+    for d in range(3):
+        parts = [second[d]]
+        for b in range(3):
+            if b != d:
+                part = mixed[min(b, d), max(b, d)]
+                parts.append(None if part is None else pltpu.roll(part, (d - b) % 8, 0))
+        total = functools.reduce(plus, parts)
+        value = plus(times(shear_modulus, laplace), times(lame_first + shear_modulus, total))
+        rows.append(jnp.zeros((1, LANES), jnp.float32) if value is None else -value[d : d + 1])
+    return rows
+
+
+def stiffness_kernel(below_ref, own_ref, above_ref, out_ref):
+    here = [lax.axis_index(name) for name in ("gx", "gy", "gz")]
+    sizes = [lax.axis_size(name) for name in ("gx", "gy", "gz")]
+    slabs = {-1: below_ref, 0: own_ref, 1: above_ref}
     fields = {}
     for ox in (-1, 0, 1):
         for oy in (-1, 0, 1):
@@ -258,85 +337,42 @@
                 peer = jnp.clip(place[1], 0, sizes[1] - 1) * sizes[2] + jnp.clip(
                     place[2], 0, sizes[2] - 1
                 )
-                if relative:
-                    peer = peer ^ own
-                    peer = peer % 2 * sizes[1] + peer // 2
                 fields[ox, oy, oz] = jnp.where(inside, slabs[ox][peer], 0.0)
-
-    def along(axis, sign, centre, beyond):
-        step, extent = steps[axis], extents[axis]
-        back = step * (extent - 1)
-        if sign > 0:
-            return jnp.where(
-                at[axis] < extent - 1,
-                pltpu.roll(centre, LANES - step, 1),
-                pltpu.roll(beyond, back, 1),
-            )
-        return jnp.where(
-            at[axis] > 0, pltpu.roll(centre, step, 1), pltpu.roll(beyond, LANES - back, 1)
-        )
-
-    def moved(vector, frame=(0, 0, 0), axis=2):
-        if axis < 0:
-            return fields[frame]
-        sign = vector[axis]
-        centre = moved(vector, frame, axis - 1)
-        if sign == 0:
-            return centre
-        other = tuple(sign if n == axis else frame[n] for n in range(3))
-        return along(axis, sign, centre, moved(vector, other, axis - 1))
-
-    units = ((1, 0, 0), (0, 1, 0), (0, 0, 1))
-    centre = fields[0, 0, 0]
-    laplace = -6.0 * centre
-    second = []
-    for unit in units:
-        both = moved(unit) + moved(tuple(-n for n in unit))
-        laplace = laplace + both
-        second.append(both - 2.0 * centre)
-    mixed = {}
-    for outer in range(3):
-        for inner in range(outer + 1, 3):
-            plus = tuple(p + q for p, q in zip(units[outer], units[inner]))
-            cross = tuple(p - q for p, q in zip(units[outer], units[inner]))
-            mixed[outer, inner] = 0.25 * (
-                moved(plus)
-                - moved(cross)
-                - moved(tuple(-n for n in cross))
-                + moved(tuple(-n for n in plus))
-            )
-    for d in range(3):
-        total = second[d][d : d + 1]
-        for b in range(3):
-            if b != d:
-                total = total + mixed[min(b, d), max(b, d)][b : b + 1]
-        out_ref[d : d + 1, :] = -(
-            shear_modulus * laplace[d : d + 1] + (lame_first + shear_modulus) * total
-        )
-
-
-def collect_kernel(*refs):
+    out_ref[...] = jnp.zeros((8, LANES), jnp.float32)
+    for d, row in enumerate(navier(fields)):
+        out_ref[2 * d : 2 * d + 1, :] = row
+
+
+def column_kernel(own_ref, above_ref, kept_ref, across_ref):
+    gx, gy, gz = [lax.axis_index(name) for name in ("gx", "gy", "gz")]
+    n_x, n_y = lax.axis_size("gx"), lax.axis_size("gy")
+    here, ahead = {}, {}
+    for oy in (-1, 0, 1):
+        place = gy + oy
+        inside = (place >= 0) & (place < n_y)
+        distance = lax.rem(oy + n_y, n_y)
+        here[0, oy] = jnp.where(inside, own_ref[distance], 0.0)
+        here[1, oy] = jnp.where(inside & (gx + 1 < n_x), above_ref[distance], 0.0)
+        ahead[-1, oy] = here[0, oy]
+    for n, columns in enumerate((here, ahead)):
+        kept = {(ox, oy, 0): value for (ox, oy), value in columns.items()}
+        across = {}
+        for (ox, oy), value in columns.items():
+            if not (ox and oy):
+                across[ox, oy, -1] = jnp.where(gz == 0, value, 0.0)
+                across[ox, oy, 1] = jnp.where(gz == 1, value, 0.0)
+        for ref, fields in ((kept_ref, kept), (across_ref, across)):
+            for d, row in enumerate(navier(fields)):
+                ref[2 * d + n : 2 * d + n + 1, :] = row
+
+
+def collect_kernel(after_ref, *refs):
     for n, ref in enumerate(refs[:-1]):
         refs[-1][n] = ref[DISP:META, :]
 
 
-def join_kernel(first_ref, second_ref, out_ref):
-    count = first_ref.shape[0]
-    out_ref[:count] = first_ref[...]
-    out_ref[count:] = second_ref[...]
-
-
-def small_call(kernel, shapes, name, *operands, dtype=jnp.float32):
-    vmem = pl.BlockSpec(memory_space=pltpu.VMEM)
-    return pl.pallas_call(
-        kernel,
-        out_shape=[jax.ShapeDtypeStruct(shape, dtype) for shape in shapes],
-        in_specs=[vmem] * len(operands),
-        out_specs=[vmem] * len(shapes),
-        compiler_params=pltpu.CompilerParams(vmem_limit_bytes=24 << 20),
-        cost_estimate=pl.CostEstimate(flops=1 << 20, bytes_accessed=1 << 20, transcendentals=0),
-        name=name,
-    )(*operands)
+def small_call(kernel, shapes, name, *operands):
+    return vmem_call(kernel, [(shape, jnp.float32) for shape in shapes], name, *operands)
 
 
 def ring(value, axes, distance=1):
@@ -369,38 +405,40 @@
     n_y, n_z = lax.axis_size("gy"), lax.axis_size("gz")
     peers = n_y * n_z
     cap = send_list.shape[0] // peers
-    (packed,) = small_call(
-        pack_kernel,
-        [(META, LANES)],
-        "pack",
+    (shape_values,) = vmem_call(
+        shape_kernel, [((512, LANES), jnp.float32)], "shapes", cost=16 << 20, flops=1 << 33
+    )
+    packed, table = vmem_call(
+        prepare_kernel,
+        [((META, LANES), jnp.float32), ((TABLE, LANES), jnp.bfloat16)],
+        "prepare",
+        shape_values,
         fractions,
         displacement,
         offsets,
         recv_slot[None],
-    )
-    (table,) = small_call(
-        table_kernel,
-        [(TABLE, LANES)],
-        "table",
+        send_list.reshape(-1, LANES),
         deformed_blocks,
-        send_list.reshape(-1, LANES),
-        dtype=jnp.bfloat16,
     )
     relative = n_z == 2 and n_y in (2, 4) and 2 * cap == LANES
     if relative:
-        metas = [packed] + [swapped(packed, "gy", d) for d in range(1, n_y)]
+        metas = [packed] + [ring(packed, "gy", -d) for d in range(1, n_y)]
         mate = swapped(table, "gz", 1)
         arrived = [None] * n_y
-        previous = []
-        for d in range(n_y - 1, -1, -1):
+        previous = metas[1:]
+        for d in ([3, 1, 2] if n_y == 4 else [1]) + [0]:
             samples = sample_call(
-                functools.partial(pair_kernel, d), metas[d], table, mate, *previous
+                functools.partial(pair_kernel, d),
+                metas[d],
+                table,
+                mate,
+                *previous,
             )
+            arrived[d] = ring(samples, "gy", d) if d else samples
             previous = [samples]
-            arrived[d] = swapped(samples, "gy", d) if d else samples
-        (column,) = small_call(collect_kernel, [(n_y, 8, LANES)], "collect", *metas)
-        (slab,) = small_call(
-            join_kernel, [(peers, 8, LANES)], "join", column, swapped(column, "gz", 1)
+        (column,) = small_call(collect_kernel, [(n_y, 8, LANES)], "collect", arrived[n_y - 1], *metas)
+        stiff, across = small_call(
+            column_kernel, [(8, LANES)] * 2, "stiffness", column, ring(column, "gx", -1)
         )
     else:
         gathered = lax.all_gather(packed, SLAB, axis=0)
@@ -416,32 +454,26 @@
         outgoing = jnp.concatenate(samples, axis=0)
         arrived = [lax.all_to_all(outgoing, SLAB, split_axis=0, concat_axis=0, tiled=True)]
         slab = gathered[:, DISP:META]
-    below, above = ring(slab, "gx", 1), ring(slab, "gx", -1)
-    (stiff,) = small_call(
-        functools.partial(stiffness_kernel, relative), [(8, LANES)], "stiffness", below, slab, above
-    )
+        (stiff,) = small_call(
+            stiffness_kernel, [(8, LANES)], "stiffness", ring(slab, "gx", 1), slab, ring(slab, "gx", -1)
+        )
+        across = jnp.zeros((8, LANES), jnp.float32)
     kept, sent = small_call(
         functools.partial(force_kernel, cap, relative),
         [(24, LANES)] * 2,
         "forces",
+        across,
         recv_slot[:, None],
         reference_image,
         image_gradient,
-        shape_table(),
+        shape_values,
         *arrived,
     )
-    own, x, y, xy = small_call(
-        layer_kernel, [(8, LANES)] * 4, "layers", kept, ring(sent, "gz")
+    xy, y, x, own = small_call(
+        layer_kernel, [(8, LANES)] * 4, "layers", kept, ring(sent, "gz"), stiff
     )
     return small_call(
-        final_kernel,
-        [(3, LANES)],
-        "total",
-        own,
-        ring(x, "gx"),
-        ring(y, "gy"),
-        ring_2(xy),
-        stiff,
+        final_kernel, [(3, LANES)], "total", own, ring_2(xy), ring(y, "gy"), ring(x, "gx")
     )[0]
 
 

time: 39.3 us -> 38 us (0.967)
  starting transfers between devices: 16.2 us -> 14.4 us
  waiting for transfers between devices: 13.3 us -> 15 us
  local copies, waits for them, and re-layouts: 2.35 us -> 1.2 us
    ppermute x8 -> x1, starting transfers between devices: 10.7 us -> 0.52 us  [swapped(): lax.ppermute(value, axes, [(i, i ^ mask) for i in range(lax.axis_size(axe...]
    ppermute x5 -> x10, starting transfers between devices: 4.75 us -> 13.9 us  [ring(): lax.ppermute(value, axes, [(i, (i + distance) % count) for i in range(cou...]
    ppermute x5 -> x10, waiting for transfers between devices: 1.81 us -> 10.4 us  [ring(): lax.ppermute(value, axes, [(i, (i + distance) % count) for i in range(cou...]
    ppermute x8 -> x1, waiting for transfers between devices: 7.07 us -> 0.01 us  [swapped(): lax.ppermute(value, axes, [(i, i ^ mask) for i in range(lax.axis_size(axe...]
    unnamed x16, local copies, waits for them, and re-layouts: 1.93 us -> 1.08 us
    ppermute x1, starting transfers between devices: 0.76 us -> 0.04 us  [ring_2(): return lax.ppermute(value, ('gx', 'gy'), route)]
    pallas_call x8 -> x7, Pallas kernels: 2.5 us -> 2.65 us  [vmem_call(): pl.pallas_call(kernel, out_shape=[jax.ShapeDtypeStruct(shape, dtype) for...]
  transfers between devices with their start and end apart: 14 -> 12, of which waited for: 6 -> 9; matrix products, arithmetic and copies ran while one was open for 2% -> 0% of each run, Pallas kernels for 15% -> 9%
where the time goes in v3:
time: 38 us; the launch traced here: 37.8 us
  waiting for transfers between devices  15 us (39%)
  starting transfers between devices  14.4 us (38%)
  Pallas kernels  7.13 us (19%)
  local copies, waits for them, and re-layouts  1.2 us (3%)
    ppermute x10, starting transfers between devices, ring(): lax.ppermute(value, axes, [(i, (i + distance) % count) for i in range(cou...  13.9 us
    ppermute x10, waiting for transfers between devices, ring(): lax.ppermute(value, axes, [(i, (i + distance) % count) for i in range(cou...  10.4 us
    ppermute x1, waiting for transfers between devices, ring_2(): return lax.ppermute(value, ('gx', 'gy'), route)  4.56 us
    pallas_call x4, Pallas kernels, sample_call(): pl.pallas_call(kernel, out_shape=jax.ShapeDtypeStruct((LANES, 512), jnp.b...  4.48 us
    pallas_call x7, Pallas kernels, vmem_call(): pl.pallas_call(kernel, out_shape=[jax.ShapeDtypeStruct(shape, dtype) for...  2.65 us
    unnamed x16, local copies, waits for them, and re-layouts  1.08 us
  transfers between devices with their start and end apart: 12, of which 9 were waited for; matrix products, arithmetic and copies ran while one was open for 0% of the time, Pallas kernels for 9%

profile of v3, /device:TPU:0, one launch (start us, length us, event | category | flops | bytes accessed | tf_op | source)
XLA Modules:
  0.0 37.8 jit_solution(406756352371864848)
XLA Ops:
  0.0 0.0 copy-start.3
  0.0 0.0 copy-start.4
  0.0 0.0 copy-start.5
  0.0 0.0 copy-start
  0.0 0.2 shapes.1.after_ref.shape_ref
  0.2 0.5 %copy-done.3 = bf16[24,128]{1,0:T(8,128)(2,1)S(1)} copy-done((bf16[24,128]{1,0:T(8,128)(2,1)S(1)}, bf16[24,128]{1,0:T(8,128)(2,1)}, u32[]{:S(2)}) %copy-start.3) | copy-done | bytes 6168
  0.7 0.0 copy-done.4
  0.7 0.0 copy-done.5
  0.7 0.0 copy-done.7
  0.7 0.0 copy-done.6
  0.7 0.6 %copy-done = bf16[128,4096]{1,0:T(8,128)(2,1)S(1)} copy-done((bf16[128,4096]{1,0:T(8,128)(2,1)S(1)}, bf16[128,4096]{1,0:T(8,128)(2,1)}, u32[]{:S(2)}) %copy-start) | copy-done | bytes 1048600
  1.3 0.3 prepare.1
  1.6 0.5 %collective-permute-start.1 = (bf16[4112,128]{1,0:T(8,128)(2,1)S(1)}, bf16[4112,128]{1,0:T(8,128)(2,1)S(1)}, u32[]{:S(2)}, u32[]{:S(2)}) collective-permute-start(bf16[4112,128]{1,0:T(8,128)(2,1)S(1)} %get-tuple-element.16.own_ref), channel_id=1, source_target_pairs={{0,1},{1,0},{2,3},{3,2},{4,5},{5,4},{6,7},{7,6},{8,9},{9,8},{10,11... | collective-permute-start | bytes 3158024 | tf_op jit(solution)/shard_map/ppermute | solution.py:392
  2.2 2.6 %collective-permute-start = (f32[32,128]{1,0:T(8,128)S(1)}, f32[32,128]{1,0:T(8,128)S(1)}, u32[]{:S(2)}, u32[]{:S(2)}) collective-permute-start(f32[32,128]{1,0:T(8,128)S(1)} %get-tuple-element.15.refs_0_.meta_ref), channel_id=1, source_target_pairs={{0,2},{2,4},{4,6},{6,0},{1,3},{3,5},{5,7},{7,1},{8,10},{10,12},{12... | collective-permute-start | bytes 49160 | tf_op jit(solution)/shard_map/ppermute | solution.py:380
  4.8 2.1 %collective-permute-start.2 = (f32[32,128]{1,0:T(8,128)S(1)}, f32[32,128]{1,0:T(8,128)S(1)}, u32[]{:S(2)}, u32[]{:S(2)}) collective-permute-start(f32[32,128]{1,0:T(8,128)S(1)} %get-tuple-element.15.refs_0_.meta_ref), channel_id=1, source_target_pairs={{0,6},{2,0},{4,2},{6,4},{1,7},{3,1},{5,3},{7,5},{8,14},{10,8},{12,... | collective-permute-start | bytes 49160 | tf_op jit(solution)/shard_map/ppermute | solution.py:380
  6.9 0.9 %collective-permute-start.3 = (f32[32,128]{1,0:T(8,128)S(1)}, f32[32,128]{1,0:T(8,128)S(1)}, u32[]{:S(2)}, u32[]{:S(2)}) collective-permute-start(f32[32,128]{1,0:T(8,128)S(1)} %get-tuple-element.15.refs_0_.meta_ref), channel_id=1, source_target_pairs={{0,4},{2,6},{4,0},{6,2},{1,5},{3,7},{5,1},{7,3},{8,12},{10,14},{12... | collective-permute-start | bytes 49160 | tf_op jit(solution)/shard_map/ppermute | solution.py:380
  7.8 0.8 %collective-permute-done.meta_ref.rest_2_.refs_3_ = f32[32,128]{1,0:T(8,128)S(1)} collective-permute-done((f32[32,128]{1,0:T(8,128)S(1)}, f32[32,128]{1,0:T(8,128)S(1)}, u32[]{:S(2)}, u32[]{:S(2)}) %collective-permute-start) | collective-permute-done | bytes 16416 | tf_op jit(solution)/shard_map/ppermute | solution.py:380
  8.6 0.1 collective-permute-done.2.rest_0_.refs_1_.meta_ref
  8.7 2.8 %collective-permute-done.3.rest_1_.refs_2_.meta_ref = f32[32,128]{1,0:T(8,128)S(1)} collective-permute-done((f32[32,128]{1,0:T(8,128)S(1)}, f32[32,128]{1,0:T(8,128)S(1)}, u32[]{:S(2)}, u32[]{:S(2)}) %collective-permute-start.3) | collective-permute-done | bytes 16416 | tf_op jit(solution)/shard_map/ppermute | solution.py:380
  11.5 0.0 collective-permute-done.1.mate_ref
  11.5 1.1 %interpolate.4.rest_0_ = bf16[128,512]{1,0:T(8,128)(2,1)S(1)} custom-call(f32[32,128]{1,0:T(8,128)S(1)} %collective-permute-done.meta_ref.rest_2_.refs_3_, bf16[4112,128]{1,0:T(8,128)(2,1)S(1)} %get-tuple-element.16.own_ref, bf16[4112,128]{1,0:T(8,128)(2,1)S(1)} %collective-permute-done.1.mate_ref, ...), custom_call_target="tpu_custom_call" | custom-call | flops 1 | bytes 1 | tf_op jit(solution)/shard_map/interpolate/pallas_call | solution.py:175
  12.7 2.0 %collective-permute-start.4 = (bf16[128,512]{1,0:T(8,128)(2,1)S(1)}, bf16[128,512]{1,0:T(8,128)(2,1)S(1)}, u32[]{:S(2)}, u32[]{:S(2)}) collective-permute-start(bf16[128,512]{1,0:T(8,128)(2,1)S(1)} %interpolate.4.rest_0_), channel_id=1, source_target_pairs={{0,6},{2,0},{4,2},{6,4},{1,7},{3,1},{5,3},{7,5},{8,14},{10,8},{12,... | collective-permute-start | bytes 393224 | tf_op jit(solution)/shard_map/ppermute | solution.py:380
  14.7 1.1 %interpolate.5.rest_0_ = bf16[128,512]{1,0:T(8,128)(2,1)S(1)} custom-call(f32[32,128]{1,0:T(8,128)S(1)} %collective-permute-done.2.rest_0_.refs_1_.meta_ref, bf16[4112,128]{1,0:T(8,128)(2,1)S(1)} %get-tuple-element.16.own_ref, bf16[4112,128]{1,0:T(8,128)(2,1)S(1)} %collective-permute-done.1.mate_ref, bf16[128,512]{1,0:T(8,128)(2,1)S(1)} %interpolate.4.rest_0_), custom_call_target="tpu_custom_call" | custom-call | flops 1 | bytes 1 | tf_op jit(solution)/shard_map/interpolate/pallas_call | solution.py:175
  15.8 0.1 collective-permute-start.6
  15.9 1.1 %interpolate.6.rest_0_ = bf16[128,512]{1,0:T(8,128)(2,1)S(1)} custom-call(f32[32,128]{1,0:T(8,128)S(1)} %collective-permute-done.3.rest_1_.refs_2_.meta_ref, bf16[4112,128]{1,0:T(8,128)(2,1)S(1)} %get-tuple-element.16.own_ref, bf16[4112,128]{1,0:T(8,128)(2,1)S(1)} %collective-permute-done.1.mate_ref, bf16[128,512]{1,0:T(8,128)(2,1)S(1)} %interpolate.5.rest_0_), custom_call_target="tpu_custom_call" | custom-call | flops 1 | bytes 1 | tf_op jit(solution)/shard_map/interpolate/pallas_call | solution.py:175
  17.0 1.0 %collective-permute-start.7 = (bf16[128,512]{1,0:T(8,128)(2,1)S(1)}, bf16[128,512]{1,0:T(8,128)(2,1)S(1)}, u32[]{:S(2)}, u32[]{:S(2)}) collective-permute-start(bf16[128,512]{1,0:T(8,128)(2,1)S(1)} %interpolate.6.rest_0_), channel_id=1, source_target_pairs={{0,4},{2,6},{4,0},{6,2},{1,5},{3,7},{5,1},{7,3},{8,12},{10,14},{12... | collective-permute-start | bytes 393224 | tf_op jit(solution)/shard_map/ppermute | solution.py:380
  18.0 0.7 %collective-permute-done.4.after_ref.rest_3_ = bf16[128,512]{1,0:T(8,128)(2,1)S(1)} collective-permute-done((bf16[128,512]{1,0:T(8,128)(2,1)S(1)}, bf16[128,512]{1,0:T(8,128)(2,1)S(1)}, u32[]{:S(2)}, u32[]{:S(2)}) %collective-permute-start.4) | collective-permute-done | bytes 131104 | tf_op jit(solution)/shard_map/ppermute | solution.py:380
  18.7 2.4 %collective-permute-start.5 = (f32[4,8,128]{2,1,0:T(8,128)S(1)}, f32[4,8,128]{2,1,0:T(8,128)S(1)}, u32[]{:S(2)}, u32[]{:S(2)}) collective-permute-start(f32[4,8,128]{2,1,0:T(8,128)S(1)} %collect.1.own_ref), channel_id=1, source_target_pairs={{0,24},{8,0},{16,8},{24,16},{1,25},{9,1},{17,9},{25,17},{2,26},{10... | collective-permute-start | bytes 49160 | tf_op jit(solution)/shard_map/ppermute | solution.py:380
  21.1 0.1 copy.9.slot_ref
  21.2 0.0 copy-start.2
  21.3 1.1 %interpolate.7.rest_0_ = bf16[128,512]{1,0:T(8,128)(2,1)S(1)} custom-call(f32[32,128]{1,0:T(8,128)S(1)} %get-tuple-element.15.refs_0_.meta_ref, bf16[4112,128]{1,0:T(8,128)(2,1)S(1)} %get-tuple-element.16.own_ref, bf16[4112,128]{1,0:T(8,128)(2,1)S(1)} %collective-permute-done.1.mate_ref, bf16[128,512]{1,0:T(8,128)(2,1)S(1)} %interpolate.6.rest_0_), custom_call_target="tpu_custom_call" | custom-call | flops 1 | bytes 1 | tf_op jit(solution)/shard_map/interpolate/pallas_call | solution.py:175
  22.4 0.2 collective-permute-done.5.above_ref
  22.6 0.2 stiffness.1
  22.8 0.6 %collective-permute-done.6.rest_1_ = bf16[128,512]{1,0:T(8,128)(2,1)S(1)} collective-permute-done((bf16[128,512]{1,0:T(8,128)(2,1)S(1)}, bf16[128,512]{1,0:T(8,128)(2,1)S(1)}, u32[]{:S(2)}, u32[]{:S(2)}) %collective-permute-start.6) | collective-permute-done | bytes 131104 | tf_op jit(solution)/shard_map/ppermute | solution.py:380
  23.3 4.1 %collective-permute-done.7.rest_2_ = bf16[128,512]{1,0:T(8,128)(2,1)S(1)} collective-permute-done((bf16[128,512]{1,0:T(8,128)(2,1)S(1)}, bf16[128,512]{1,0:T(8,128)(2,1)S(1)}, u32[]{:S(2)}, u32[]{:S(2)}) %collective-permute-start.7) | collective-permute-done | bytes 131104 | tf_op jit(solution)/shard_map/ppermute | solution.py:380
  27.5 0.0 copy-done.1
  27.5 0.0 copy-done.2
  27.5 1.2 %forces.1 = (f32[24,128]{1,0:T(8,128)S(1)}, f32[24,128]{1,0:T(8,128)S(1)}) custom-call(f32[8,128]{1,0:T(8,128)S(1)} %get-tuple-element.17.across_ref, s32[128,1]{1,0:T(8,128)S(1)} %copy.9.slot_ref, bf16[128,512]{1,0:T(8,128)(2,1)S(1)} %copy-done.2, bf16[3,128,512]{2,1,0:T(8,128)(2,1)S(1)} %copy-done.1, f32[512,128]{1,0:T(8,128)S(1)} %shapes.1.after_ref.shape_ref, ...), custom_call_target="tpu_custom_call" | custom-call | flops 1048576 | bytes 1048576 | tf_op jit(solution)/shard_map/forces/pallas_call | solution.py:77
  28.7 0.0 collective-permute-start.8
  28.7 1.2 %collective-permute-done.8.arrived_ref = f32[24,128]{1,0:T(8,128)S(1)} collective-permute-done((f32[24,128]{1,0:T(8,128)S(1)}, f32[24,128]{1,0:T(8,128)S(1)}, u32[]{:S(2)}, u32[]{:S(2)}) %collective-permute-start.8) | collective-permute-done | bytes 12320 | tf_op jit(solution)/shard_map/ppermute | solution.py:380
  29.8 0.2 layers.1
  30.0 0.0 collective-permute-start.9
  30.0 1.1 %collective-permute-start.10 = (f32[8,128]{1,0:T(8,128)S(1)}, f32[8,128]{1,0:T(8,128)S(1)}, u32[]{:S(2)}, u32[]{:S(2)}) collective-permute-start(f32[8,128]{1,0:T(8,128)S(1)} %get-tuple-element.23), channel_id=1, source_target_pairs={{0,2},{2,4},{4,6},{6,0},{1,3},{3,5},{5,7},{7,1},{8,10},{10,12},{12... | collective-permute-start | bytes 12296 | tf_op jit(solution)/shard_map/ppermute | solution.py:380
  31.2 1.5 %collective-permute-start.11 = (f32[8,128]{1,0:T(8,128)S(1)}, f32[8,128]{1,0:T(8,128)S(1)}, u32[]{:S(2)}, u32[]{:S(2)}) collective-permute-start(f32[8,128]{1,0:T(8,128)S(1)} %get-tuple-element.24), channel_id=1, source_target_pairs={{0,8},{8,16},{16,24},{24,0},{1,9},{9,17},{17,25},{25,1},{2,10},{10... | collective-permute-start | bytes 12296 | tf_op jit(solution)/shard_map/ppermute | solution.py:380
  32.7 4.6 %collective-permute-done.9.xy_ref = f32[8,128]{1,0:T(8,128)S(1)} collective-permute-done((f32[8,128]{1,0:T(8,128)S(1)}, f32[8,128]{1,0:T(8,128)S(1)}, u32[]{:S(2)}, u32[]{:S(2)}) %collective-permute-start.9) | collective-permute-done | bytes 4128 | tf_op jit(solution)/shard_map/ppermute | solution.py:388
  37.2 0.0 collective-permute-done.10.y_ref
  37.2 0.0 collective-permute-done.11.x_ref
  37.2 0.6 %total.1 = f32[3,128]{1,0:T(4,128)} custom-call(f32[8,128]{1,0:T(8,128)S(1)} %get-tuple-element.21.own_ref, f32[8,128]{1,0:T(8,128)S(1)} %collective-permute-done.9.xy_ref, f32[8,128]{1,0:T(8,128)S(1)} %collective-permute-done.10.y_ref, f32[8,128]{1,0:T(8,128)S(1)} %collective-permute-done.11.x_ref), custom_call_target="tpu_custom_call" | custom-call | flops 1048576 | bytes 1048576 | tf_op jit(solution)/shard_map/total/pallas_call | solution.py:77
  (4 shorter events, 0.0 us)
Async XLA Ops:
  0.0 0.7 %copy-start.3 = (bf16[24,128]{1,0:T(8,128)(2,1)S(1)}, bf16[24,128]{1,0:T(8,128)(2,1)}, u32[]{:S(2)}) copy-start(bf16[24,128]{1,0:T(8,128)(2,1)} %fraction_ref.1) | copy-start | bytes 18436
  0.0 0.7 %copy-start.4 = (f32[3,128]{1,0:T(4,128)S(1)}, f32[3,128]{1,0:T(4,128)}, u32[]{:S(2)}) copy-start(f32[3,128]{1,0:T(4,128)} %displacement_ref.1) | copy-start | bytes 4612
  0.0 0.7 %copy-start.5 = (s32[3,128]{1,0:T(4,128)S(1)}, s32[3,128]{1,0:T(4,128)}, u32[]{:S(2)}) copy-start(s32[3,128]{1,0:T(4,128)} %offset_ref.1) | copy-start | bytes 4612
  0.0 0.7 %copy-start.7 = (s32[128]{0:T(128)S(1)}, s32[128]{0:T(128)}, u32[]{:S(2)}) copy-start(s32[128]{0:T(128)} %param.15) | copy-start | bytes 1540
  0.0 0.7 %copy-start.6 = (s32[512]{0:T(512)S(1)}, s32[512]{0:T(512)}, u32[]{:S(2)}) copy-start(s32[512]{0:T(512)} %param.14) | copy-start | bytes 6148
  0.0 1.3 %copy-start = (bf16[128,4096]{1,0:T(8,128)(2,1)S(1)}, bf16[128,4096]{1,0:T(8,128)(2,1)}, u32[]{:S(2)}) copy-start(bf16[128,4096]{1,0:T(8,128)(2,1)} %block_ref.1) | copy-start | bytes 3145732
  1.6 9.9 %collective-permute-start.1 = (bf16[4112,128]{1,0:T(8,128)(2,1)S(1)}, bf16[4112,128]{1,0:T(8,128)(2,1)S(1)}, u32[]{:S(2)}, u32[]{:S(2)}) collective-permute-start(bf16[4112,128]{1,0:T(8,128)(2,1)S(1)} %get-tuple-element.16.own_ref), channel_id=1, source_target_pairs={{0,1},{1,0},{2,3},{3,2},{4,5},{5,4},{6,7},{7,6},{8,9},{9,8},{10,11... | collective-permute-start | bytes 3158024 | tf_op jit(solution)/shard_map/ppermute | solution.py:392
  2.2 6.5 %collective-permute-start = (f32[32,128]{1,0:T(8,128)S(1)}, f32[32,128]{1,0:T(8,128)S(1)}, u32[]{:S(2)}, u32[]{:S(2)}) collective-permute-start(f32[32,128]{1,0:T(8,128)S(1)} %get-tuple-element.15.refs_0_.meta_ref), channel_id=1, source_target_pairs={{0,2},{2,4},{4,6},{6,0},{1,3},{3,5},{5,7},{7,1},{8,10},{10,12},{12... | collective-permute-start | bytes 49160 | tf_op jit(solution)/shard_map/ppermute | solution.py:380
  4.8 3.9 %collective-permute-start.2 = (f32[32,128]{1,0:T(8,128)S(1)}, f32[32,128]{1,0:T(8,128)S(1)}, u32[]{:S(2)}, u32[]{:S(2)}) collective-permute-start(f32[32,128]{1,0:T(8,128)S(1)} %get-tuple-element.15.refs_0_.meta_ref), channel_id=1, source_target_pairs={{0,6},{2,0},{4,2},{6,4},{1,7},{3,1},{5,3},{7,5},{8,14},{10,8},{12,... | collective-permute-start | bytes 49160 | tf_op jit(solution)/shard_map/ppermute | solution.py:380
  6.9 4.6 %collective-permute-start.3 = (f32[32,128]{1,0:T(8,128)S(1)}, f32[32,128]{1,0:T(8,128)S(1)}, u32[]{:S(2)}, u32[]{:S(2)}) collective-permute-start(f32[32,128]{1,0:T(8,128)S(1)} %get-tuple-element.15.refs_0_.meta_ref), channel_id=1, source_target_pairs={{0,4},{2,6},{4,0},{6,2},{1,5},{3,7},{5,1},{7,3},{8,12},{10,14},{12... | collective-permute-start | bytes 49160 | tf_op jit(solution)/shard_map/ppermute | solution.py:380
  12.7 6.0 %collective-permute-start.4 = (bf16[128,512]{1,0:T(8,128)(2,1)S(1)}, bf16[128,512]{1,0:T(8,128)(2,1)S(1)}, u32[]{:S(2)}, u32[]{:S(2)}) collective-permute-start(bf16[128,512]{1,0:T(8,128)(2,1)S(1)} %interpolate.4.rest_0_), channel_id=1, source_target_pairs={{0,6},{2,0},{4,2},{6,4},{1,7},{3,1},{5,3},{7,5},{8,14},{10,8},{12,... | collective-permute-start | bytes 393224 | tf_op jit(solution)/shard_map/ppermute | solution.py:380
  15.8 7.5 %collective-permute-start.6 = (bf16[128,512]{1,0:T(8,128)(2,1)S(1)}, bf16[128,512]{1,0:T(8,128)(2,1)S(1)}, u32[]{:S(2)}, u32[]{:S(2)}) collective-permute-start(bf16[128,512]{1,0:T(8,128)(2,1)S(1)} %interpolate.5.rest_0_), channel_id=1, source_target_pairs={{0,2},{2,4},{4,6},{6,0},{1,3},{3,5},{5,7},{7,1},{8,10},{10,12},{12... | collective-permute-start | bytes 393224 | tf_op jit(solution)/shard_map/ppermute | solution.py:380
  17.0 10.4 %collective-permute-start.7 = (bf16[128,512]{1,0:T(8,128)(2,1)S(1)}, bf16[128,512]{1,0:T(8,128)(2,1)S(1)}, u32[]{:S(2)}, u32[]{:S(2)}) collective-permute-start(bf16[128,512]{1,0:T(8,128)(2,1)S(1)} %interpolate.6.rest_0_), channel_id=1, source_target_pairs={{0,4},{2,6},{4,0},{6,2},{1,5},{3,7},{5,1},{7,3},{8,12},{10,14},{12... | collective-permute-start | bytes 393224 | tf_op jit(solution)/shard_map/ppermute | solution.py:380
  18.7 3.8 %collective-permute-start.5 = (f32[4,8,128]{2,1,0:T(8,128)S(1)}, f32[4,8,128]{2,1,0:T(8,128)S(1)}, u32[]{:S(2)}, u32[]{:S(2)}) collective-permute-start(f32[4,8,128]{2,1,0:T(8,128)S(1)} %collect.1.own_ref), channel_id=1, source_target_pairs={{0,24},{8,0},{16,8},{24,16},{1,25},{9,1},{17,9},{25,17},{2,26},{10... | collective-permute-start | bytes 49160 | tf_op jit(solution)/shard_map/ppermute | solution.py:380
  21.2 6.2 %copy-start.1 = (bf16[3,128,512]{2,1,0:T(8,128)(2,1)S(1)}, bf16[3,128,512]{2,1,0:T(8,128)(2,1)}, u32[]{:S(2)}) copy-start(bf16[3,128,512]{2,1,0:T(8,128)(2,1)} %slope_ref.1) | copy-start | bytes 1179652
  21.2 6.2 %copy-start.2 = (bf16[128,512]{1,0:T(8,128)(2,1)S(1)}, bf16[128,512]{1,0:T(8,128)(2,1)}, u32[]{:S(2)}) copy-start(bf16[128,512]{1,0:T(8,128)(2,1)} %image_ref.1) | copy-start | bytes 393220
  28.7 1.2 %collective-permute-start.8 = (f32[24,128]{1,0:T(8,128)S(1)}, f32[24,128]{1,0:T(8,128)S(1)}, u32[]{:S(2)}, u32[]{:S(2)}) collective-permute-start(f32[24,128]{1,0:T(8,128)S(1)} %get-tuple-element.19), channel_id=1, source_target_pairs={{0,1},{1,0},{2,3},{3,2},{4,5},{5,4},{6,7},{7,6},{8,9},{9,8},{10,11... | collective-permute-start | bytes 36872 | tf_op jit(solution)/shard_map/ppermute | solution.py:380
  30.0 7.2 %collective-permute-start.9 = (f32[8,128]{1,0:T(8,128)S(1)}, f32[8,128]{1,0:T(8,128)S(1)}, u32[]{:S(2)}, u32[]{:S(2)}) collective-permute-start(f32[8,128]{1,0:T(8,128)S(1)} %get-tuple-element.22), channel_id=1, source_target_pairs={{0,10},{2,12},{4,14},{6,8},{8,18},{10,20},{12,22},{14,16},{16,26},... | collective-permute-start | bytes 12296 | tf_op jit(solution)/shard_map/ppermute | solution.py:388
  30.0 7.2 %collective-permute-start.10 = (f32[8,128]{1,0:T(8,128)S(1)}, f32[8,128]{1,0:T(8,128)S(1)}, u32[]{:S(2)}, u32[]{:S(2)}) collective-permute-start(f32[8,128]{1,0:T(8,128)S(1)} %get-tuple-element.23), channel_id=1, source_target_pairs={{0,2},{2,4},{4,6},{6,0},{1,3},{3,5},{5,7},{7,1},{8,10},{10,12},{12... | collective-permute-start | bytes 12296 | tf_op jit(solution)/shard_map/ppermute | solution.py:380
  31.2 6.1 %collective-permute-start.11 = (f32[8,128]{1,0:T(8,128)S(1)}, f32[8,128]{1,0:T(8,128)S(1)}, u32[]{:S(2)}, u32[]{:S(2)}) collective-permute-start(f32[8,128]{1,0:T(8,128)S(1)} %get-tuple-element.24), channel_id=1, source_target_pairs={{0,8},{8,16},{16,24},{24,0},{1,9},{9,17},{17,25},{25,1},{2,10},{10... | collective-permute-start | bytes 12296 | tf_op jit(solution)/shard_map/ppermute | solution.py:380

commit v4 on v3

--- a/solution.py
+++ b/solution.py
@@ -184,7 +184,7 @@
         ],
         compiler_params=pltpu.CompilerParams(vmem_limit_bytes=24 << 20),
         cost_estimate=pl.CostEstimate(
-            flops=1, bytes_accessed=1, transcendentals=0
+            flops=1300000000, bytes_accessed=1, transcendentals=0
         ),
         name="interpolate",
     )(*operands)
@@ -425,7 +425,7 @@
         metas = [packed] + [ring(packed, "gy", -d) for d in range(1, n_y)]
         mate = swapped(table, "gz", 1)
         arrived = [None] * n_y
-        previous = metas[1:]
+        previous = []
         for d in ([3, 1, 2] if n_y == 4 else [1]) + [0]:
             samples = sample_call(
                 functools.partial(pair_kernel, d),

time: 38 us -> 35.3 us (0.929)
  waiting for transfers between devices: 15 us -> 12 us
    ppermute x10, waiting for transfers between devices: 10.4 us -> 7.36 us  [ring(): lax.ppermute(value, axes, [(i, (i + distance) % count) for i in range(cou...]
  transfers between devices with their start and end apart: 12 -> 12, of which waited for: 9 -> 7; matrix products, arithmetic and copies ran while one was open for 0% -> 0% of each run, Pallas kernels for 9% -> 13%
where the time goes in v4:
time: 35.3 us; the launch traced here: 35.1 us
  starting transfers between devices  14.7 us (42%)
  waiting for transfers between devices  12 us (34%)
  Pallas kernels  7.12 us (20%)
  local copies, waits for them, and re-layouts  1.19 us (3%)
    ppermute x10, starting transfers between devices, ring(): lax.ppermute(value, axes, [(i, (i + distance) % count) for i in range(cou...  14.1 us
    ppermute x10, waiting for transfers between devices, ring(): lax.ppermute(value, axes, [(i, (i + distance) % count) for i in range(cou...  7.36 us
    ppermute x1, waiting for transfers between devices, ring_2(): return lax.ppermute(value, ('gx', 'gy'), route)  4.67 us
    pallas_call x4, Pallas kernels, sample_call(): pl.pallas_call(kernel, out_shape=jax.ShapeDtypeStruct((LANES, 512), jnp.b...  4.48 us
    pallas_call x7, Pallas kernels, vmem_call(): pl.pallas_call(kernel, out_shape=[jax.ShapeDtypeStruct(shape, dtype) for...  2.64 us
    unnamed x16, local copies, waits for them, and re-layouts  1.08 us
  transfers between devices with their start and end apart: 12, of which 7 were waited for; matrix products, arithmetic and copies ran while one was open for 0% of the time, Pallas kernels for 13%

profile of v4, /device:TPU:0, one launch (start us, length us, event | category | flops | bytes accessed | tf_op | source)
XLA Modules:
  0.0 35.1 jit_solution(8601138447071128924)
XLA Ops:
  0.0 0.0 copy-start.3
  0.0 0.0 copy-start.4
  0.0 0.0 copy-start.5
  0.0 0.0 copy-start.7
  0.0 0.0 copy-start
  0.0 0.2 shapes.1.after_ref.shape_ref
  0.2 0.5 %copy-done.3 = bf16[24,128]{1,0:T(8,128)(2,1)S(1)} copy-done((bf16[24,128]{1,0:T(8,128)(2,1)S(1)}, bf16[24,128]{1,0:T(8,128)(2,1)}, u32[]{:S(2)}) %copy-start.3) | copy-done | bytes 6168
  0.7 0.0 copy-done.4
  0.7 0.0 copy-done.5
  0.7 0.0 copy-done.7
  0.7 0.0 copy-done.6
  0.7 0.6 %copy-done = bf16[128,4096]{1,0:T(8,128)(2,1)S(1)} copy-done((bf16[128,4096]{1,0:T(8,128)(2,1)S(1)}, bf16[128,4096]{1,0:T(8,128)(2,1)}, u32[]{:S(2)}) %copy-start) | copy-done | bytes 1048600
  1.3 0.3 prepare.1
  1.6 0.5 %collective-permute-start.1 = (bf16[4112,128]{1,0:T(8,128)(2,1)S(1)}, bf16[4112,128]{1,0:T(8,128)(2,1)S(1)}, u32[]{:S(2)}, u32[]{:S(2)}) collective-permute-start(bf16[4112,128]{1,0:T(8,128)(2,1)S(1)} %get-tuple-element.16.own_ref), channel_id=1, source_target_pairs={{0,1},{1,0},{2,3},{3,2},{4,5},{5,4},{6,7},{7,6},{8,9},{9,8},{10,11... | collective-permute-start | bytes 3158024 | tf_op jit(solution)/shard_map/ppermute | solution.py:392
  2.2 2.6 %collective-permute-start = (f32[32,128]{1,0:T(8,128)S(1)}, f32[32,128]{1,0:T(8,128)S(1)}, u32[]{:S(2)}, u32[]{:S(2)}) collective-permute-start(f32[32,128]{1,0:T(8,128)S(1)} %get-tuple-element.15.refs_0_.meta_ref), channel_id=1, source_target_pairs={{0,2},{2,4},{4,6},{6,0},{1,3},{3,5},{5,7},{7,1},{8,10},{10,12},{12... | collective-permute-start | bytes 49160 | tf_op jit(solution)/shard_map/ppermute | solution.py:380
  4.8 2.1 %collective-permute-start.3 = (f32[32,128]{1,0:T(8,128)S(1)}, f32[32,128]{1,0:T(8,128)S(1)}, u32[]{:S(2)}, u32[]{:S(2)}) collective-permute-start(f32[32,128]{1,0:T(8,128)S(1)} %get-tuple-element.15.refs_0_.meta_ref), channel_id=1, source_target_pairs={{0,6},{2,0},{4,2},{6,4},{1,7},{3,1},{5,3},{7,5},{8,14},{10,8},{12,... | collective-permute-start | bytes 49160 | tf_op jit(solution)/shard_map/ppermute | solution.py:380
  6.9 0.9 %collective-permute-start.4 = (f32[32,128]{1,0:T(8,128)S(1)}, f32[32,128]{1,0:T(8,128)S(1)}, u32[]{:S(2)}, u32[]{:S(2)}) collective-permute-start(f32[32,128]{1,0:T(8,128)S(1)} %get-tuple-element.15.refs_0_.meta_ref), channel_id=1, source_target_pairs={{0,4},{2,6},{4,0},{6,2},{1,5},{3,7},{5,1},{7,3},{8,12},{10,14},{12... | collective-permute-start | bytes 49160 | tf_op jit(solution)/shard_map/ppermute | solution.py:380
  7.8 0.8 %collective-permute-done.meta_ref.refs_3_ = f32[32,128]{1,0:T(8,128)S(1)} collective-permute-done((f32[32,128]{1,0:T(8,128)S(1)}, f32[32,128]{1,0:T(8,128)S(1)}, u32[]{:S(2)}, u32[]{:S(2)}) %collective-permute-start) | collective-permute-done | bytes 16416 | tf_op jit(solution)/shard_map/ppermute | solution.py:380
  8.6 0.0 collective-permute-done.1.mate_ref
  8.6 1.1 %interpolate.4.rest_0_ = bf16[128,512]{1,0:T(8,128)(2,1)S(1)} custom-call(f32[32,128]{1,0:T(8,128)S(1)} %collective-permute-done.meta_ref.refs_3_, bf16[4112,128]{1,0:T(8,128)(2,1)S(1)} %get-tuple-element.16.own_ref, bf16[4112,128]{1,0:T(8,128)(2,1)S(1)} %collective-permute-done.1.mate_ref), custom_call_target="tpu_custom_call" | custom-call | flops 1300000000 | bytes 1 | tf_op jit(solution)/shard_map/interpolate/pallas_call | solution.py:175
  9.8 2.0 %collective-permute-start.2 = (bf16[128,512]{1,0:T(8,128)(2,1)S(1)}, bf16[128,512]{1,0:T(8,128)(2,1)S(1)}, u32[]{:S(2)}, u32[]{:S(2)}) collective-permute-start(bf16[128,512]{1,0:T(8,128)(2,1)S(1)} %interpolate.4.rest_0_), channel_id=1, source_target_pairs={{0,6},{2,0},{4,2},{6,4},{1,7},{3,1},{5,3},{7,5},{8,14},{10,8},{12,... | collective-permute-start | bytes 393224 | tf_op jit(solution)/shard_map/ppermute | solution.py:380
  11.7 0.0 collective-permute-done.3.refs_1_.meta_ref
  11.7 1.1 %interpolate.5.rest_0_ = bf16[128,512]{1,0:T(8,128)(2,1)S(1)} custom-call(f32[32,128]{1,0:T(8,128)S(1)} %collective-permute-done.3.refs_1_.meta_ref, bf16[4112,128]{1,0:T(8,128)(2,1)S(1)} %get-tuple-element.16.own_ref, bf16[4112,128]{1,0:T(8,128)(2,1)S(1)} %collective-permute-done.1.mate_ref, bf16[128,512]{1,0:T(8,128)(2,1)S(1)} %interpolate.4.rest_0_), custom_call_target="tpu_custom_call" | custom-call | flops 1300000000 | bytes 1 | tf_op jit(solution)/shard_map/interpolate/pallas_call | solution.py:175
  12.9 0.2 collective-permute-start.6
  13.0 0.0 collective-permute-done.4.refs_2_.meta_ref
  13.0 1.1 %interpolate.6.rest_0_ = bf16[128,512]{1,0:T(8,128)(2,1)S(1)} custom-call(f32[32,128]{1,0:T(8,128)S(1)} %collective-permute-done.4.refs_2_.meta_ref, bf16[4112,128]{1,0:T(8,128)(2,1)S(1)} %get-tuple-element.16.own_ref, bf16[4112,128]{1,0:T(8,128)(2,1)S(1)} %collective-permute-done.1.mate_ref, bf16[128,512]{1,0:T(8,128)(2,1)S(1)} %interpolate.5.rest_0_), custom_call_target="tpu_custom_call" | custom-call | flops 1300000000 | bytes 1 | tf_op jit(solution)/shard_map/interpolate/pallas_call | solution.py:175
  14.2 1.3 %collective-permute-start.7 = (bf16[128,512]{1,0:T(8,128)(2,1)S(1)}, bf16[128,512]{1,0:T(8,128)(2,1)S(1)}, u32[]{:S(2)}, u32[]{:S(2)}) collective-permute-start(bf16[128,512]{1,0:T(8,128)(2,1)S(1)} %interpolate.6.rest_0_), channel_id=1, source_target_pairs={{0,4},{2,6},{4,0},{6,2},{1,5},{3,7},{5,1},{7,3},{8,12},{10,14},{12... | collective-permute-start | bytes 393224 | tf_op jit(solution)/shard_map/ppermute | solution.py:380
  15.4 0.1 copy.9.slot_ref
  15.5 0.2 collective-permute-done.2.after_ref.rest_3_
  15.7 2.5 %collective-permute-start.5 = (f32[4,8,128]{2,1,0:T(8,128)S(1)}, f32[4,8,128]{2,1,0:T(8,128)S(1)}, u32[]{:S(2)}, u32[]{:S(2)}) collective-permute-start(f32[4,8,128]{2,1,0:T(8,128)S(1)} %collect.1.own_ref), channel_id=1, source_target_pairs={{0,24},{8,0},{16,8},{24,16},{1,25},{9,1},{17,9},{25,17},{2,26},{10... | collective-permute-start | bytes 49160 | tf_op jit(solution)/shard_map/ppermute | solution.py:380
  18.2 1.1 %interpolate.7.rest_0_ = bf16[128,512]{1,0:T(8,128)(2,1)S(1)} custom-call(f32[32,128]{1,0:T(8,128)S(1)} %get-tuple-element.15.refs_0_.meta_ref, bf16[4112,128]{1,0:T(8,128)(2,1)S(1)} %get-tuple-element.16.own_ref, bf16[4112,128]{1,0:T(8,128)(2,1)S(1)} %collective-permute-done.1.mate_ref, bf16[128,512]{1,0:T(8,128)(2,1)S(1)} %interpolate.6.rest_0_), custom_call_target="tpu_custom_call" | custom-call | flops 1300000000 | bytes 1 | tf_op jit(solution)/shard_map/interpolate/pallas_call | solution.py:175
  19.3 0.3 collective-permute-done.5.above_ref
  19.7 0.2 stiffness.1
  19.9 0.8 %collective-permute-done.6.rest_1_ = bf16[128,512]{1,0:T(8,128)(2,1)S(1)} collective-permute-done((bf16[128,512]{1,0:T(8,128)(2,1)S(1)}, bf16[128,512]{1,0:T(8,128)(2,1)S(1)}, u32[]{:S(2)}, u32[]{:S(2)}) %collective-permute-start.6) | collective-permute-done | bytes 131104 | tf_op jit(solution)/shard_map/ppermute | solution.py:380
  20.6 4.1 %collective-permute-done.7.rest_2_ = bf16[128,512]{1,0:T(8,128)(2,1)S(1)} collective-permute-done((bf16[128,512]{1,0:T(8,128)(2,1)S(1)}, bf16[128,512]{1,0:T(8,128)(2,1)S(1)}, u32[]{:S(2)}, u32[]{:S(2)}) %collective-permute-start.7) | collective-permute-done | bytes 131104 | tf_op jit(solution)/shard_map/ppermute | solution.py:380
  24.8 0.0 copy-done.1
  24.8 0.0 copy-done.2
  24.8 1.2 %forces.1 = (f32[24,128]{1,0:T(8,128)S(1)}, f32[24,128]{1,0:T(8,128)S(1)}) custom-call(f32[8,128]{1,0:T(8,128)S(1)} %get-tuple-element.17.across_ref, s32[128,1]{1,0:T(8,128)S(1)} %copy.9.slot_ref, bf16[128,512]{1,0:T(8,128)(2,1)S(1)} %copy-done.2, bf16[3,128,512]{2,1,0:T(8,128)(2,1)S(1)} %copy-done.1, f32[512,128]{1,0:T(8,128)S(1)} %shapes.1.after_ref.shape_ref, ...), custom_call_target="tpu_custom_call" | custom-call | flops 1048576 | bytes 1048576 | tf_op jit(solution)/shard_map/forces/pallas_call | solution.py:77
  25.9 0.0 collective-permute-start.8
  26.0 1.2 %collective-permute-done.8.arrived_ref = f32[24,128]{1,0:T(8,128)S(1)} collective-permute-done((f32[24,128]{1,0:T(8,128)S(1)}, f32[24,128]{1,0:T(8,128)S(1)}, u32[]{:S(2)}, u32[]{:S(2)}) %collective-permute-start.8) | collective-permute-done | bytes 12320 | tf_op jit(solution)/shard_map/ppermute | solution.py:380
  27.1 0.2 layers.1
  27.3 0.0 collective-permute-start.9
  27.3 1.0 %collective-permute-start.10 = (f32[8,128]{1,0:T(8,128)S(1)}, f32[8,128]{1,0:T(8,128)S(1)}, u32[]{:S(2)}, u32[]{:S(2)}) collective-permute-start(f32[8,128]{1,0:T(8,128)S(1)} %get-tuple-element.23), channel_id=1, source_target_pairs={{0,2},{2,4},{4,6},{6,0},{1,3},{3,5},{5,7},{7,1},{8,10},{10,12},{12... | collective-permute-start | bytes 12296 | tf_op jit(solution)/shard_map/ppermute | solution.py:380
  28.3 1.5 %collective-permute-start.11 = (f32[8,128]{1,0:T(8,128)S(1)}, f32[8,128]{1,0:T(8,128)S(1)}, u32[]{:S(2)}, u32[]{:S(2)}) collective-permute-start(f32[8,128]{1,0:T(8,128)S(1)} %get-tuple-element.24), channel_id=1, source_target_pairs={{0,8},{8,16},{16,24},{24,0},{1,9},{9,17},{17,25},{25,1},{2,10},{10... | collective-permute-start | bytes 12296 | tf_op jit(solution)/shard_map/ppermute | solution.py:380
  29.8 4.7 %collective-permute-done.9.xy_ref = f32[8,128]{1,0:T(8,128)S(1)} collective-permute-done((f32[8,128]{1,0:T(8,128)S(1)}, f32[8,128]{1,0:T(8,128)S(1)}, u32[]{:S(2)}, u32[]{:S(2)}) %collective-permute-start.9) | collective-permute-done | bytes 4128 | tf_op jit(solution)/shard_map/ppermute | solution.py:388
  34.5 0.0 collective-permute-done.10.y_ref
  34.5 0.0 collective-permute-done.11.x_ref
  34.5 0.6 %total.1 = f32[3,128]{1,0:T(4,128)} custom-call(f32[8,128]{1,0:T(8,128)S(1)} %get-tuple-element.21.own_ref, f32[8,128]{1,0:T(8,128)S(1)} %collective-permute-done.9.xy_ref, f32[8,128]{1,0:T(8,128)S(1)} %collective-permute-done.10.y_ref, f32[8,128]{1,0:T(8,128)S(1)} %collective-permute-done.11.x_ref), custom_call_target="tpu_custom_call" | custom-call | flops 1048576 | bytes 1048576 | tf_op jit(solution)/shard_map/total/pallas_call | solution.py:77
  (4 shorter events, 0.0 us)
Async XLA Ops:
  0.0 0.7 %copy-start.3 = (bf16[24,128]{1,0:T(8,128)(2,1)S(1)}, bf16[24,128]{1,0:T(8,128)(2,1)}, u32[]{:S(2)}) copy-start(bf16[24,128]{1,0:T(8,128)(2,1)} %fraction_ref.1) | copy-start | bytes 18436
  0.0 0.7 %copy-start.4 = (f32[3,128]{1,0:T(4,128)S(1)}, f32[3,128]{1,0:T(4,128)}, u32[]{:S(2)}) copy-start(f32[3,128]{1,0:T(4,128)} %displacement_ref.1) | copy-start | bytes 4612
  0.0 0.7 %copy-start.5 = (s32[3,128]{1,0:T(4,128)S(1)}, s32[3,128]{1,0:T(4,128)}, u32[]{:S(2)}) copy-start(s32[3,128]{1,0:T(4,128)} %offset_ref.1) | copy-start | bytes 4612
  0.0 0.7 %copy-start.7 = (s32[128]{0:T(128)S(1)}, s32[128]{0:T(128)}, u32[]{:S(2)}) copy-start(s32[128]{0:T(128)} %param.15) | copy-start | bytes 1540
  0.0 0.7 %copy-start.6 = (s32[512]{0:T(512)S(1)}, s32[512]{0:T(512)}, u32[]{:S(2)}) copy-start(s32[512]{0:T(512)} %param.14) | copy-start | bytes 6148
  0.0 1.3 %copy-start = (bf16[128,4096]{1,0:T(8,128)(2,1)S(1)}, bf16[128,4096]{1,0:T(8,128)(2,1)}, u32[]{:S(2)}) copy-start(bf16[128,4096]{1,0:T(8,128)(2,1)} %block_ref.1) | copy-start | bytes 3145732
  1.6 7.0 %collective-permute-start.1 = (bf16[4112,128]{1,0:T(8,128)(2,1)S(1)}, bf16[4112,128]{1,0:T(8,128)(2,1)S(1)}, u32[]{:S(2)}, u32[]{:S(2)}) collective-permute-start(bf16[4112,128]{1,0:T(8,128)(2,1)S(1)} %get-tuple-element.16.own_ref), channel_id=1, source_target_pairs={{0,1},{1,0},{2,3},{3,2},{4,5},{5,4},{6,7},{7,6},{8,9},{9,8},{10,11... | collective-permute-start | bytes 3158024 | tf_op jit(solution)/shard_map/ppermute | solution.py:392
  2.2 6.5 %collective-permute-start = (f32[32,128]{1,0:T(8,128)S(1)}, f32[32,128]{1,0:T(8,128)S(1)}, u32[]{:S(2)}, u32[]{:S(2)}) collective-permute-start(f32[32,128]{1,0:T(8,128)S(1)} %get-tuple-element.15.refs_0_.meta_ref), channel_id=1, source_target_pairs={{0,2},{2,4},{4,6},{6,0},{1,3},{3,5},{5,7},{7,1},{8,10},{10,12},{12... | collective-permute-start | bytes 49160 | tf_op jit(solution)/shard_map/ppermute | solution.py:380
  4.8 7.0 %collective-permute-start.3 = (f32[32,128]{1,0:T(8,128)S(1)}, f32[32,128]{1,0:T(8,128)S(1)}, u32[]{:S(2)}, u32[]{:S(2)}) collective-permute-start(f32[32,128]{1,0:T(8,128)S(1)} %get-tuple-element.15.refs_0_.meta_ref), channel_id=1, source_target_pairs={{0,6},{2,0},{4,2},{6,4},{1,7},{3,1},{5,3},{7,5},{8,14},{10,8},{12,... | collective-permute-start | bytes 49160 | tf_op jit(solution)/shard_map/ppermute | solution.py:380
  6.9 6.1 %collective-permute-start.4 = (f32[32,128]{1,0:T(8,128)S(1)}, f32[32,128]{1,0:T(8,128)S(1)}, u32[]{:S(2)}, u32[]{:S(2)}) collective-permute-start(f32[32,128]{1,0:T(8,128)S(1)} %get-tuple-element.15.refs_0_.meta_ref), channel_id=1, source_target_pairs={{0,4},{2,6},{4,0},{6,2},{1,5},{3,7},{5,1},{7,3},{8,12},{10,14},{12... | collective-permute-start | bytes 49160 | tf_op jit(solution)/shard_map/ppermute | solution.py:380
  9.8 5.9 %collective-permute-start.2 = (bf16[128,512]{1,0:T(8,128)(2,1)S(1)}, bf16[128,512]{1,0:T(8,128)(2,1)S(1)}, u32[]{:S(2)}, u32[]{:S(2)}) collective-permute-start(bf16[128,512]{1,0:T(8,128)(2,1)S(1)} %interpolate.4.rest_0_), channel_id=1, source_target_pairs={{0,6},{2,0},{4,2},{6,4},{1,7},{3,1},{5,3},{7,5},{8,14},{10,8},{12,... | collective-permute-start | bytes 393224 | tf_op jit(solution)/shard_map/ppermute | solution.py:380
  12.9 7.8 %collective-permute-start.6 = (bf16[128,512]{1,0:T(8,128)(2,1)S(1)}, bf16[128,512]{1,0:T(8,128)(2,1)S(1)}, u32[]{:S(2)}, u32[]{:S(2)}) collective-permute-start(bf16[128,512]{1,0:T(8,128)(2,1)S(1)} %interpolate.5.rest_0_), channel_id=1, source_target_pairs={{0,2},{2,4},{4,6},{6,0},{1,3},{3,5},{5,7},{7,1},{8,10},{10,12},{12... | collective-permute-start | bytes 393224 | tf_op jit(solution)/shard_map/ppermute | solution.py:380
  14.2 10.6 %collective-permute-start.7 = (bf16[128,512]{1,0:T(8,128)(2,1)S(1)}, bf16[128,512]{1,0:T(8,128)(2,1)S(1)}, u32[]{:S(2)}, u32[]{:S(2)}) collective-permute-start(bf16[128,512]{1,0:T(8,128)(2,1)S(1)} %interpolate.6.rest_0_), channel_id=1, source_target_pairs={{0,4},{2,6},{4,0},{6,2},{1,5},{3,7},{5,1},{7,3},{8,12},{10,14},{12... | collective-permute-start | bytes 393224 | tf_op jit(solution)/shard_map/ppermute | solution.py:380
  15.7 9.1 %copy-start.1 = (bf16[3,128,512]{2,1,0:T(8,128)(2,1)S(1)}, bf16[3,128,512]{2,1,0:T(8,128)(2,1)}, u32[]{:S(2)}) copy-start(bf16[3,128,512]{2,1,0:T(8,128)(2,1)} %slope_ref.1) | copy-start | bytes 1179652
  15.7 9.1 %copy-start.2 = (bf16[128,512]{1,0:T(8,128)(2,1)S(1)}, bf16[128,512]{1,0:T(8,128)(2,1)}, u32[]{:S(2)}) copy-start(bf16[128,512]{1,0:T(8,128)(2,1)} %image_ref.1) | copy-start | bytes 393220
  15.7 4.0 %collective-permute-start.5 = (f32[4,8,128]{2,1,0:T(8,128)S(1)}, f32[4,8,128]{2,1,0:T(8,128)S(1)}, u32[]{:S(2)}, u32[]{:S(2)}) collective-permute-start(f32[4,8,128]{2,1,0:T(8,128)S(1)} %collect.1.own_ref), channel_id=1, source_target_pairs={{0,24},{8,0},{16,8},{24,16},{1,25},{9,1},{17,9},{25,17},{2,26},{10... | collective-permute-start | bytes 49160 | tf_op jit(solution)/shard_map/ppermute | solution.py:380
  25.9 1.2 %collective-permute-start.8 = (f32[24,128]{1,0:T(8,128)S(1)}, f32[24,128]{1,0:T(8,128)S(1)}, u32[]{:S(2)}, u32[]{:S(2)}) collective-permute-start(f32[24,128]{1,0:T(8,128)S(1)} %get-tuple-element.19), channel_id=1, source_target_pairs={{0,1},{1,0},{2,3},{3,2},{4,5},{5,4},{6,7},{7,6},{8,9},{9,8},{10,11... | collective-permute-start | bytes 36872 | tf_op jit(solution)/shard_map/ppermute | solution.py:380
  27.3 7.2 %collective-permute-start.9 = (f32[8,128]{1,0:T(8,128)S(1)}, f32[8,128]{1,0:T(8,128)S(1)}, u32[]{:S(2)}, u32[]{:S(2)}) collective-permute-start(f32[8,128]{1,0:T(8,128)S(1)} %get-tuple-element.22), channel_id=1, source_target_pairs={{0,10},{2,12},{4,14},{6,8},{8,18},{10,20},{12,22},{14,16},{16,26},... | collective-permute-start | bytes 12296 | tf_op jit(solution)/shard_map/ppermute | solution.py:388
  27.3 7.2 %collective-permute-start.10 = (f32[8,128]{1,0:T(8,128)S(1)}, f32[8,128]{1,0:T(8,128)S(1)}, u32[]{:S(2)}, u32[]{:S(2)}) collective-permute-start(f32[8,128]{1,0:T(8,128)S(1)} %get-tuple-element.23), channel_id=1, source_target_pairs={{0,2},{2,4},{4,6},{6,0},{1,3},{3,5},{5,7},{7,1},{8,10},{10,12},{12... | collective-permute-start | bytes 12296 | tf_op jit(solution)/shard_map/ppermute | solution.py:380
  28.3 6.2 %collective-permute-start.11 = (f32[8,128]{1,0:T(8,128)S(1)}, f32[8,128]{1,0:T(8,128)S(1)}, u32[]{:S(2)}, u32[]{:S(2)}) collective-permute-start(f32[8,128]{1,0:T(8,128)S(1)} %get-tuple-element.24), channel_id=1, source_target_pairs={{0,8},{8,16},{16,24},{24,0},{1,9},{9,17},{17,25},{25,1},{2,10},{10... | collective-permute-start | bytes 12296 | tf_op jit(solution)/shard_map/ppermute | solution.py:380

commit v5 on v4

--- a/solution.py
+++ b/solution.py
@@ -23,7 +23,6 @@
 META = 32
 
 VOXELS = 4096
-TABLE = VOXELS + 16
 
 
 def iota(shape, dim):
@@ -50,26 +49,27 @@
         return jnp.where(upper == 1, centre, 1.0 - centre)
 
     values = weight(voxel // 64, column // 2 % 2) * weight(voxel // 8 % 8, column % 2)
-    values = values * weight(voxel % 8, column // 4)
-    out_ref[...] = jnp.where(column < 8, values, 0.0)
-
-
-def prepare_kernel(
-    after_ref, fraction_ref, displacement_ref, offset_ref, slot_ref, send_ref, block_ref, packed_ref, table_ref
-):
-    packed_ref[:DISP, :] = fraction_ref[...].astype(jnp.float32)
-    packed_ref[DISP:OFFS, :] = displacement_ref[...]
-    packed_ref[OFFS:SLOT, :] = offset_ref[...].astype(jnp.float32)
-    packed_ref[SLOT : SLOT + 1, :] = slot_ref[...].astype(jnp.float32)
-    packed_ref[SLOT + 1 :, :] = jnp.zeros((META - SLOT - 1, LANES), jnp.float32)
-    for start in range(0, VOXELS, 512):
-        table_ref[start : start + 512, :] = block_ref[:, start : start + 512].T
-    rows = send_ref.shape[0]
-    listed = jnp.concatenate(
-        [send_ref[...].astype(jnp.float32), jnp.zeros((TABLE - VOXELS - rows, LANES), jnp.float32)],
-        axis=0,
-    )
-    table_ref[VOXELS:, :] = listed.astype(jnp.bfloat16)
+    values = values * weight(voxel % 8, column // 4 % 2)
+    coarse = values.astype(jnp.bfloat16).astype(jnp.float32)
+    values = jnp.where(column < 8, coarse, jnp.where(column < 16, values - coarse, 0.0))
+    out_ref[...] = values.astype(jnp.bfloat16)
+
+
+def pack_kernel(after_ref, fraction_ref, displacement_ref, offset_ref, slot_ref, out_ref):
+    out_ref[:DISP, :] = fraction_ref[...].astype(jnp.float32)
+    out_ref[DISP:OFFS, :] = displacement_ref[...]
+    out_ref[OFFS:SLOT, :] = offset_ref[...].astype(jnp.float32)
+    out_ref[SLOT : SLOT + 1, :] = slot_ref[...].astype(jnp.float32)
+    out_ref[SLOT + 1 :, :] = jnp.zeros((META - SLOT - 1, LANES), jnp.float32)
+
+
+def table_kernel(after_ref, later_ref, *refs):
+    out_ref = refs[-1]
+    for n, ref in enumerate(refs[:-1]):
+        for start in range(0, VOXELS, 512):
+            out_ref[start : start + 512, LANES * n : LANES * n + LANES] = ref[
+                :, start : start + 512
+            ].T
 
 
 def vmem_call(kernel, shapes, name, *operands, cost=1 << 20, flops=1 << 20):
@@ -85,24 +85,18 @@
     )(*operands)
 
 
-def interpolated(table_refs, pick, meta, along_a, along_b, along_c):
+def interpolated(table_ref, pick, meta, along_a, along_b, along_c):
     upper = meta[:24]
     lower = 1.0 - upper
     offsets = meta[OFFS : OFFS + 3].astype(jnp.int32)
     bits = offset_bits(offsets[0:1], 16)
-    for b in range(16):
-        starts = [256 * a + 16 * b for a in range(16)]
-        rows = jnp.concatenate(
-            [
-                jnp.concatenate([ref[start : start + 16, :] for start in starts], axis=0)
-                for ref in table_refs
-            ],
-            axis=1,
-        )
+    for first in range(0, 256, 16):
+        starts = [256 * a + first for a in range(16)]
+        rows = jnp.concatenate([table_ref[start : start + 16, :] for start in starts], axis=0)
         voxels = jnp.dot(rows, pick, preferred_element_type=jnp.float32)
         window = shifted([voxels[16 * a : 16 * a + 16] for a in range(16)], bits)
         for i in range(8):
-            along_a[256 * i + 16 * b : 256 * i + 16 * b + 16, :] = (
+            along_a[256 * i + first : 256 * i + first + 16, :] = (
                 lower[i : i + 1] * window[i] + upper[i : i + 1] * window[i + 1]
             )
     bits = offset_bits(offsets[1:2], 16)
@@ -136,7 +130,7 @@
     )
 
 
-def pair_kernel(distance, meta_ref, own_ref, mate_ref, *rest):
+def pair_kernel(distance, meta_ref, table_ref, own_ref, mate_ref, *rest):
     out_ref, scratch = rest[-4], rest[-3:]
     gy, gz = lax.axis_index("gy"), lax.axis_index("gz")
     half = LANES // 2
@@ -144,30 +138,25 @@
     slots = (((2 * gy + gz) ^ (slot // half)) * half) + slot % half
     meta = slot_meta(meta_ref[...], slots)
     chip = lax.rem(gy + distance, lax.axis_size("gy"))
-    lists = [ref[VOXELS:, :].astype(jnp.float32) for ref in (own_ref, mate_ref)]
-    here = iota(lists[0].shape, 0) == chip
-    own, mate = [
-        jnp.sum(jnp.where(here, listed, 0.0), axis=0, keepdims=True).astype(jnp.int32)
-        for listed in lists
-    ]
+    chip = pl.ds(chip, 1)
+    own, mate = own_ref[chip, :], mate_ref[chip, :]
     first = gz == 0
     own = jnp.where(first, own, pltpu.roll(own, half, 1))
     mate = jnp.where(first, pltpu.roll(mate, half, 1), mate)
     row = jnp.where(iota((1, LANES), 1) < half, own, mate + LANES)
     pick = (iota((2 * LANES, LANES), 0) == row).astype(jnp.bfloat16)
-    out_ref[...] = interpolated((own_ref, mate_ref), pick, meta, *scratch)
-
-
-def group_kernel(group, cap, meta_ref, table_ref, out_ref, *scratch):
+    out_ref[...] = interpolated(table_ref, pick, meta, *scratch)
+
+
+def group_kernel(group, cap, meta_ref, table_ref, send_ref, out_ref, *scratch):
     holder = lax.axis_index("gy") * lax.axis_size("gz") + lax.axis_index("gz")
     slot = iota((LANES, LANES), 0)
     meta = jnp.zeros((META, LANES), jnp.float32)
     for r in range(LANES // cap):
         slots = jnp.where(slot // cap == r, holder * cap + slot - r * cap, -1)
         meta = meta + slot_meta(meta_ref[r], slots)
-    row = table_ref[VOXELS:, :].astype(jnp.float32)[group : group + 1].astype(jnp.int32)
-    pick = (iota((LANES, LANES), 0) == row).astype(jnp.bfloat16)
-    out_ref[...] = interpolated((table_ref,), pick, meta, *scratch)
+    pick = (iota((LANES, LANES), 0) == send_ref[group : group + 1, :]).astype(jnp.bfloat16)
+    out_ref[...] = interpolated(table_ref, pick, meta, *scratch)
 
 
 def sample_call(kernel, *operands):
@@ -184,7 +173,7 @@
         ],
         compiler_params=pltpu.CompilerParams(vmem_limit_bytes=24 << 20),
         cost_estimate=pl.CostEstimate(
-            flops=1300000000, bytes_accessed=1, transcendentals=0
+            flops=4000000000, bytes_accessed=1, transcendentals=0
         ),
         name="interpolate",
     )(*operands)
@@ -208,15 +197,22 @@
     rows = jnp.concatenate([piece[...] for piece in arrived], axis=0)
     samples = jnp.dot(hit, rows, preferred_element_type=jnp.float32)
     difference = image_ref[...].astype(jnp.float32) - samples
+    parts = []
+    for d in range(3):
+        weighted = slope_ref[d].astype(jnp.float32) * difference
+        coarse = weighted.astype(jnp.bfloat16)
+        parts += [coarse, (weighted - coarse.astype(jnp.float32)).astype(jnp.bfloat16)]
+    sums = jnp.dot(
+        jnp.concatenate(parts, axis=0), shape_ref[...], preferred_element_type=jnp.float32
+    )
+    columns = 0.0
+    for d in range(3):
+        both = sums[2 * LANES * d : 2 * LANES * d + LANES] + sums[2 * LANES * d + LANES : 2 * LANES * (d + 1)]
+        columns = columns + (pltpu.roll(both, 16 * d, 1) if d else both)
+    columns = columns.T
     _, _, at_k = axis_of_lane(8)
     for d in range(3):
-        weighted = slope_ref[d].astype(jnp.float32) * difference
-        corners = jnp.dot(
-            weighted,
-            shape_ref[...],
-            preferred_element_type=jnp.float32,
-            precision=lax.Precision.HIGHEST,
-        ).T[:8]
+        corners = columns[16 * d : 16 * d + 8] + columns[16 * d + 8 : 16 * d + 16]
         carried = pltpu.roll(corners, 4, 0)
         kept_ref[8 * d : 8 * d + 8, :] = corners + jnp.where(at_k > 0, pltpu.roll(carried, 1, 1), 0.0)
         sent_ref[8 * d : 8 * d + 8, :] = jnp.where(at_k == 0, pltpu.roll(carried, LANES - 7, 1), 0.0)
@@ -406,24 +402,31 @@
     peers = n_y * n_z
     cap = send_list.shape[0] // peers
     (shape_values,) = vmem_call(
-        shape_kernel, [((512, LANES), jnp.float32)], "shapes", cost=16 << 20, flops=1 << 33
-    )
-    packed, table = vmem_call(
-        prepare_kernel,
-        [((META, LANES), jnp.float32), ((TABLE, LANES), jnp.bfloat16)],
-        "prepare",
+        shape_kernel, [((512, LANES), jnp.bfloat16)], "shapes", cost=16 << 20, flops=1 << 33
+    )
+    (packed,) = small_call(
+        pack_kernel,
+        [(META, LANES)],
+        "pack",
         shape_values,
         fractions,
         displacement,
         offsets,
         recv_slot[None],
-        send_list.reshape(-1, LANES),
-        deformed_blocks,
-    )
+    )
+    send_rows = send_list.reshape(-1, LANES)
+    mate_rows = swapped(send_rows, "gz", 1)
+
+    def table_of(*blocks):
+        shape = (VOXELS, len(blocks) * LANES)
+        return vmem_call(
+            table_kernel, [(shape, jnp.bfloat16)], "table", packed, mate_rows, *blocks, flops=3 << 28
+        )[0]
+
     relative = n_z == 2 and n_y in (2, 4) and 2 * cap == LANES
     if relative:
         metas = [packed] + [ring(packed, "gy", -d) for d in range(1, n_y)]
-        mate = swapped(table, "gz", 1)
+        table = table_of(deformed_blocks, swapped(deformed_blocks, "gz", 1))
         arrived = [None] * n_y
         previous = []
         for d in ([3, 1, 2] if n_y == 4 else [1]) + [0]:
@@ -431,7 +434,8 @@
                 functools.partial(pair_kernel, d),
                 metas[d],
                 table,
-                mate,
+                send_rows,
+                mate_rows,
                 *previous,
             )
             arrived[d] = ring(samples, "gy", d) if d else samples
@@ -443,11 +447,13 @@
     else:
         gathered = lax.all_gather(packed, SLAB, axis=0)
         readers = LANES // cap
+        table = table_of(deformed_blocks)
         samples = [
             sample_call(
                 functools.partial(group_kernel, g, cap),
                 gathered[g * readers : (g + 1) * readers],
                 table,
+                send_rows,
             )
             for g in range(peers // readers)
         ]

time: 35.3 us -> 34.3 us (0.972)
  waiting for transfers between devices: 12 us -> 10.5 us
  starting transfers between devices: 14.7 us -> 15.9 us
  local copies, waits for them, and re-layouts: 1.19 us -> 0.46 us
    ppermute x10, waiting for transfers between devices: 7.36 us -> 5.84 us  [ring(): lax.ppermute(value, axes, [(i, (i + distance) % count) for i in range(cou...]
    ppermute x10, starting transfers between devices: 14.1 us -> 15.2 us  [ring(): lax.ppermute(value, axes, [(i, (i + distance) % count) for i in range(cou...]
    unnamed x16, local copies, waits for them, and re-layouts: 1.08 us -> 0.35 us
    pallas_call x7 -> x8, Pallas kernels: 2.64 us -> 2.6 us  [vmem_call(): pl.pallas_call(kernel, out_shape=[jax.ShapeDtypeStruct(shape, dtype) for...]
  transfers between devices with their start and end apart: 12 -> 13, of which waited for: 7 -> 5; matrix products, arithmetic and copies ran while one was open for 0% -> 0% of each run, Pallas kernels for 13% -> 16%
where the time goes in v5:
time: 34.3 us; the launch traced here: 34.1 us
  starting transfers between devices  15.9 us (46%)
  waiting for transfers between devices  10.5 us (31%)
  Pallas kernels  7.13 us (21%)
  local copies, waits for them, and re-layouts  0.46 us (1%)
    ppermute x10, starting transfers between devices, ring(): lax.ppermute(value, axes, [(i, (i + distance) % count) for i in range(cou...  15.2 us
    ppermute x10, waiting for transfers between devices, ring(): lax.ppermute(value, axes, [(i, (i + distance) % count) for i in range(cou...  5.84 us
    ppermute x1, waiting for transfers between devices, ring_2(): return lax.ppermute(value, ('gx', 'gy'), route)  4.68 us
    pallas_call x4, Pallas kernels, sample_call(): pl.pallas_call(kernel, out_shape=jax.ShapeDtypeStruct((LANES, 512), jnp.b...  4.52 us
    pallas_call x8, Pallas kernels, vmem_call(): pl.pallas_call(kernel, out_shape=[jax.ShapeDtypeStruct(shape, dtype) for...  2.6 us
  transfers between devices with their start and end apart: 13, of which 5 were waited for; matrix products, arithmetic and copies ran while one was open for 0% of the time, Pallas kernels for 16%

profile of v5, /device:TPU:0, one launch (start us, length us, event | category | flops | bytes accessed | tf_op | source)
XLA Modules:
  0.0 34.1 jit_solution(11667586878327663818)
XLA Ops:
  0.0 0.5 %collective-permute-start.2 = (bf16[128,4096]{1,0:T(8,128)(2,1)}, bf16[128,4096]{1,0:T(8,128)(2,1)S(1)}, u32[]{:S(2)}, u32[]{:S(2)}) collective-permute-start(bf16[128,4096]{1,0:T(8,128)(2,1)} %refs_0_.1), channel_id=1, source_target_pairs={{0,1},{1,0},{2,3},{3,2},{4,5},{5,4},{6,7},{7,6},{8,9},{9,8},{10,11... | collective-permute-start | bytes 3145736 | tf_op jit(solution)/shard_map/ppermute | solution.py:388
  0.5 0.0 copy-start.3
  0.5 0.0 copy-start
  0.5 0.1 collective-permute-start.1
  0.6 0.2 shapes.1.after_ref.shape_ref
  0.8 0.3 copy-done.3
  1.1 0.0 copy-done.4
  1.2 0.0 copy-done.5
  1.2 0.0 copy-done.6
  1.2 2.8 %collective-permute-start = (f32[32,128]{1,0:T(8,128)S(1)}, f32[32,128]{1,0:T(8,128)S(1)}, u32[]{:S(2)}, u32[]{:S(2)}) collective-permute-start(f32[32,128]{1,0:T(8,128)S(1)} %pack.1.after_ref.refs_0_.meta_ref), channel_id=1, source_target_pairs={{0,2},{2,4},{4,6},{6,0},{1,3},{3,5},{5,7},{7,1},{8,10},{10,12},{12... | collective-permute-start | bytes 49160 | tf_op jit(solution)/shard_map/ppermute | solution.py:376
  4.0 2.1 %collective-permute-start.4 = (f32[32,128]{1,0:T(8,128)S(1)}, f32[32,128]{1,0:T(8,128)S(1)}, u32[]{:S(2)}, u32[]{:S(2)}) collective-permute-start(f32[32,128]{1,0:T(8,128)S(1)} %pack.1.after_ref.refs_0_.meta_ref), channel_id=1, source_target_pairs={{0,6},{2,0},{4,2},{6,4},{1,7},{3,1},{5,3},{7,5},{8,14},{10,8},{12,... | collective-permute-start | bytes 49160 | tf_op jit(solution)/shard_map/ppermute | solution.py:376
  6.1 0.9 %collective-permute-start.5 = (f32[32,128]{1,0:T(8,128)S(1)}, f32[32,128]{1,0:T(8,128)S(1)}, u32[]{:S(2)}, u32[]{:S(2)}) collective-permute-start(f32[32,128]{1,0:T(8,128)S(1)} %pack.1.after_ref.refs_0_.meta_ref), channel_id=1, source_target_pairs={{0,4},{2,6},{4,0},{6,2},{1,5},{3,7},{5,1},{7,3},{8,12},{10,14},{12... | collective-permute-start | bytes 49160 | tf_op jit(solution)/shard_map/ppermute | solution.py:376
  7.0 0.1 copy.9.slot_ref
  7.1 0.0 collective-permute-done.1.later_ref.mate_ref
  7.1 0.0 collective-permute-done.2.refs_1_
  7.2 0.0 copy-done
  7.2 0.6 %table.1.table_ref = bf16[4096,256]{1,0:T(8,128)(2,1)S(1)} custom-call(f32[32,128]{1,0:T(8,128)S(1)} %pack.1.after_ref.refs_0_.meta_ref, s32[4,128]{1,0:T(4,128)S(1)} %collective-permute-done.1.later_ref.mate_ref, bf16[128,4096]{1,0:T(8,128)(2,1)S(1)} %copy-done, bf16[128,4096]{1,0:T(8,128)(2,1)S(1)} %collective-permute-done.2.refs_1_), custom_call_target="tpu_custom_call" | custom-call | flops 805306368 | bytes 1048576 | tf_op jit(solution)/shard_map/table/pallas_call | solution.py:77
  7.8 0.1 collective-permute-done.meta_ref.refs_3_
  7.8 0.0 copy-done.7
  7.8 1.1 %interpolate.4.rest_0_ = bf16[128,512]{1,0:T(8,128)(2,1)S(1)} custom-call(f32[32,128]{1,0:T(8,128)S(1)} %collective-permute-done.meta_ref.refs_3_, bf16[4096,256]{1,0:T(8,128)(2,1)S(1)} %table.1.table_ref, s32[4,128]{1,0:T(4,128)S(1)} %bitcast.6, s32[4,128]{1,0:T(4,128)S(1)} %collective-permute-done.1.later_ref.mate_ref), custom_call_target="tpu_custom_call" | custom-call | flops 4000000000 | bytes 1 | tf_op jit(solution)/shard_map/interpolate/pallas_call | solution.py:164
  9.0 2.0 %collective-permute-start.3 = (bf16[128,512]{1,0:T(8,128)(2,1)S(1)}, bf16[128,512]{1,0:T(8,128)(2,1)S(1)}, u32[]{:S(2)}, u32[]{:S(2)}) collective-permute-start(bf16[128,512]{1,0:T(8,128)(2,1)S(1)} %interpolate.4.rest_0_), channel_id=1, source_target_pairs={{0,6},{2,0},{4,2},{6,4},{1,7},{3,1},{5,3},{7,5},{8,14},{10,8},{12,... | collective-permute-start | bytes 393224 | tf_op jit(solution)/shard_map/ppermute | solution.py:376
  10.9 0.0 collective-permute-done.4.refs_1_.meta_ref
  10.9 1.1 %interpolate.5.rest_0_ = bf16[128,512]{1,0:T(8,128)(2,1)S(1)} custom-call(f32[32,128]{1,0:T(8,128)S(1)} %collective-permute-done.4.refs_1_.meta_ref, bf16[4096,256]{1,0:T(8,128)(2,1)S(1)} %table.1.table_ref, s32[4,128]{1,0:T(4,128)S(1)} %bitcast.7, s32[4,128]{1,0:T(4,128)S(1)} %collective-permute-done.1.later_ref.mate_ref, ...), custom_call_target="tpu_custom_call" | custom-call | flops 4000000000 | bytes 1 | tf_op jit(solution)/shard_map/interpolate/pallas_call | solution.py:164
  12.1 0.2 collective-permute-start.7
  12.2 0.0 collective-permute-done.5.refs_2_.meta_ref
  12.2 1.1 %interpolate.6.rest_0_ = bf16[128,512]{1,0:T(8,128)(2,1)S(1)} custom-call(f32[32,128]{1,0:T(8,128)S(1)} %collective-permute-done.5.refs_2_.meta_ref, bf16[4096,256]{1,0:T(8,128)(2,1)S(1)} %table.1.table_ref, s32[4,128]{1,0:T(4,128)S(1)} %bitcast.8, s32[4,128]{1,0:T(4,128)S(1)} %collective-permute-done.1.later_ref.mate_ref, ...), custom_call_target="tpu_custom_call" | custom-call | flops 4000000000 | bytes 1 | tf_op jit(solution)/shard_map/interpolate/pallas_call | solution.py:164
  13.4 2.0 %collective-permute-start.8 = (bf16[128,512]{1,0:T(8,128)(2,1)S(1)}, bf16[128,512]{1,0:T(8,128)(2,1)S(1)}, u32[]{:S(2)}, u32[]{:S(2)}) collective-permute-start(bf16[128,512]{1,0:T(8,128)(2,1)S(1)} %interpolate.6.rest_0_), channel_id=1, source_target_pairs={{0,4},{2,6},{4,0},{6,2},{1,5},{3,7},{5,1},{7,3},{8,12},{10,14},{12... | collective-permute-start | bytes 393224 | tf_op jit(solution)/shard_map/ppermute | solution.py:376
  15.4 0.0 collective-permute-done.3.after_ref.rest_3_
  15.4 0.0 copy-start.2
  15.4 2.7 %collective-permute-start.6 = (f32[4,8,128]{2,1,0:T(8,128)S(1)}, f32[4,8,128]{2,1,0:T(8,128)S(1)}, u32[]{:S(2)}, u32[]{:S(2)}) collective-permute-start(f32[4,8,128]{2,1,0:T(8,128)S(1)} %collect.1.own_ref), channel_id=1, source_target_pairs={{0,24},{8,0},{16,8},{24,16},{1,25},{9,1},{17,9},{25,17},{2,26},{10... | collective-permute-start | bytes 49160 | tf_op jit(solution)/shard_map/ppermute | solution.py:376
  18.1 1.1 %interpolate.7.rest_0_ = bf16[128,512]{1,0:T(8,128)(2,1)S(1)} custom-call(f32[32,128]{1,0:T(8,128)S(1)} %pack.1.after_ref.refs_0_.meta_ref, bf16[4096,256]{1,0:T(8,128)(2,1)S(1)} %table.1.table_ref, s32[4,128]{1,0:T(4,128)S(1)} %bitcast.9, s32[4,128]{1,0:T(4,128)S(1)} %collective-permute-done.1.later_ref.mate_ref, bf16[128,512]{1,0:T(8,128)(2,1)S(1)} %interpolate.6.rest_0_), custom_call_target="tpu_custom_call" | custom-call | flops 4000000000 | bytes 1 | tf_op jit(solution)/shard_map/interpolate/pallas_call | solution.py:164
  19.2 0.3 collective-permute-done.6.above_ref
  19.5 0.2 stiffness.1
  19.7 4.3 %collective-permute-done.8.rest_2_ = bf16[128,512]{1,0:T(8,128)(2,1)S(1)} collective-permute-done((bf16[128,512]{1,0:T(8,128)(2,1)S(1)}, bf16[128,512]{1,0:T(8,128)(2,1)S(1)}, u32[]{:S(2)}, u32[]{:S(2)}) %collective-permute-start.8) | collective-permute-done | bytes 131104 | tf_op jit(solution)/shard_map/ppermute | solution.py:376
  24.0 0.0 collective-permute-done.7.rest_1_
  24.0 0.0 copy-done.1
  24.0 0.0 copy-done.2
  24.0 0.8 %forces.1 = (f32[24,128]{1,0:T(8,128)S(1)}, f32[24,128]{1,0:T(8,128)S(1)}) custom-call(f32[8,128]{1,0:T(8,128)S(1)} %get-tuple-element.13.across_ref, s32[128,1]{1,0:T(8,128)S(1)} %copy.9.slot_ref, bf16[128,512]{1,0:T(8,128)(2,1)S(1)} %copy-done.2, bf16[3,128,512]{2,1,0:T(8,128)(2,1)S(1)} %copy-done.1, bf16[512,128]{1,0:T(8,128)(2,1)S(1)} %shapes.1.after_ref.shape_ref, ...), custom_call_target="tpu_custom_call" | custom-call | flops 1048576 | bytes 1048576 | tf_op jit(solution)/shard_map/forces/pallas_call | solution.py:77
  24.8 0.1 collective-permute-start.9
  24.9 1.2 %collective-permute-done.9.arrived_ref = f32[24,128]{1,0:T(8,128)S(1)} collective-permute-done((f32[24,128]{1,0:T(8,128)S(1)}, f32[24,128]{1,0:T(8,128)S(1)}, u32[]{:S(2)}, u32[]{:S(2)}) %collective-permute-start.9) | collective-permute-done | bytes 12320 | tf_op jit(solution)/shard_map/ppermute | solution.py:376
  26.1 0.2 layers.1
  26.2 0.0 collective-permute-start.10
  26.3 1.0 %collective-permute-start.11 = (f32[8,128]{1,0:T(8,128)S(1)}, f32[8,128]{1,0:T(8,128)S(1)}, u32[]{:S(2)}, u32[]{:S(2)}) collective-permute-start(f32[8,128]{1,0:T(8,128)S(1)} %get-tuple-element.19), channel_id=1, source_target_pairs={{0,2},{2,4},{4,6},{6,0},{1,3},{3,5},{5,7},{7,1},{8,10},{10,12},{12... | collective-permute-start | bytes 12296 | tf_op jit(solution)/shard_map/ppermute | solution.py:376
  27.3 1.5 %collective-permute-start.12 = (f32[8,128]{1,0:T(8,128)S(1)}, f32[8,128]{1,0:T(8,128)S(1)}, u32[]{:S(2)}, u32[]{:S(2)}) collective-permute-start(f32[8,128]{1,0:T(8,128)S(1)} %get-tuple-element.20), channel_id=1, source_target_pairs={{0,8},{8,16},{16,24},{24,0},{1,9},{9,17},{17,25},{25,1},{2,10},{10... | collective-permute-start | bytes 12296 | tf_op jit(solution)/shard_map/ppermute | solution.py:376
  28.8 4.7 %collective-permute-done.10.xy_ref = f32[8,128]{1,0:T(8,128)S(1)} collective-permute-done((f32[8,128]{1,0:T(8,128)S(1)}, f32[8,128]{1,0:T(8,128)S(1)}, u32[]{:S(2)}, u32[]{:S(2)}) %collective-permute-start.10) | collective-permute-done | bytes 4128 | tf_op jit(solution)/shard_map/ppermute | solution.py:384
  33.5 0.0 collective-permute-done.11.y_ref
  33.5 0.0 collective-permute-done.12.x_ref
  33.5 0.6 %total.1 = f32[3,128]{1,0:T(4,128)} custom-call(f32[8,128]{1,0:T(8,128)S(1)} %get-tuple-element.17.own_ref, f32[8,128]{1,0:T(8,128)S(1)} %collective-permute-done.10.xy_ref, f32[8,128]{1,0:T(8,128)S(1)} %collective-permute-done.11.y_ref, f32[8,128]{1,0:T(8,128)S(1)} %collective-permute-done.12.x_ref), custom_call_target="tpu_custom_call" | custom-call | flops 1048576 | bytes 1048576 | tf_op jit(solution)/shard_map/total/pallas_call | solution.py:77
  (7 shorter events, 0.0 us)
Async XLA Ops:
  0.0 7.1 %collective-permute-start.2 = (bf16[128,4096]{1,0:T(8,128)(2,1)}, bf16[128,4096]{1,0:T(8,128)(2,1)S(1)}, u32[]{:S(2)}, u32[]{:S(2)}) collective-permute-start(bf16[128,4096]{1,0:T(8,128)(2,1)} %refs_0_.1), channel_id=1, source_target_pairs={{0,1},{1,0},{2,3},{3,2},{4,5},{5,4},{6,7},{7,6},{8,9},{9,8},{10,11... | collective-permute-start | bytes 3145736 | tf_op jit(solution)/shard_map/ppermute | solution.py:388
  0.5 0.7 %copy-start.3 = (bf16[24,128]{1,0:T(8,128)(2,1)S(1)}, bf16[24,128]{1,0:T(8,128)(2,1)}, u32[]{:S(2)}) copy-start(bf16[24,128]{1,0:T(8,128)(2,1)} %fraction_ref.1) | copy-start | bytes 18436
  0.5 0.7 %copy-start.4 = (f32[3,128]{1,0:T(4,128)S(1)}, f32[3,128]{1,0:T(4,128)}, u32[]{:S(2)}) copy-start(f32[3,128]{1,0:T(4,128)} %displacement_ref.1) | copy-start | bytes 4612
  0.5 0.7 %copy-start.5 = (s32[3,128]{1,0:T(4,128)S(1)}, s32[3,128]{1,0:T(4,128)}, u32[]{:S(2)}) copy-start(s32[3,128]{1,0:T(4,128)} %offset_ref.1) | copy-start | bytes 4612
  0.5 0.7 %copy-start.6 = (s32[128]{0:T(128)S(1)}, s32[128]{0:T(128)}, u32[]{:S(2)}) copy-start(s32[128]{0:T(128)} %param.15) | copy-start | bytes 1540
  0.5 6.7 %copy-start = (bf16[128,4096]{1,0:T(8,128)(2,1)S(1)}, bf16[128,4096]{1,0:T(8,128)(2,1)}, u32[]{:S(2)}) copy-start(bf16[128,4096]{1,0:T(8,128)(2,1)} %refs_0_.1) | copy-start | bytes 3145732
  0.5 6.7 %collective-permute-start.1 = (s32[4,128]{1,0:T(4,128)}, s32[4,128]{1,0:T(4,128)S(1)}, u32[]{:S(2)}, u32[]{:S(2)}) collective-permute-start(s32[4,128]{1,0:T(4,128)} %bitcast.5), channel_id=1, source_target_pairs={{0,1},{1,0},{2,3},{3,2},{4,5},{5,4},{6,7},{7,6},{8,9},{9,8},{10,11... | collective-permute-start | bytes 6152 | tf_op jit(solution)/shard_map/ppermute | solution.py:388
  1.2 6.6 %collective-permute-start = (f32[32,128]{1,0:T(8,128)S(1)}, f32[32,128]{1,0:T(8,128)S(1)}, u32[]{:S(2)}, u32[]{:S(2)}) collective-permute-start(f32[32,128]{1,0:T(8,128)S(1)} %pack.1.after_ref.refs_0_.meta_ref), channel_id=1, source_target_pairs={{0,2},{2,4},{4,6},{6,0},{1,3},{3,5},{5,7},{7,1},{8,10},{10,12},{12... | collective-permute-start | bytes 49160 | tf_op jit(solution)/shard_map/ppermute | solution.py:376
  4.0 7.0 %collective-permute-start.4 = (f32[32,128]{1,0:T(8,128)S(1)}, f32[32,128]{1,0:T(8,128)S(1)}, u32[]{:S(2)}, u32[]{:S(2)}) collective-permute-start(f32[32,128]{1,0:T(8,128)S(1)} %pack.1.after_ref.refs_0_.meta_ref), channel_id=1, source_target_pairs={{0,6},{2,0},{4,2},{6,4},{1,7},{3,1},{5,3},{7,5},{8,14},{10,8},{12,... | collective-permute-start | bytes 49160 | tf_op jit(solution)/shard_map/ppermute | solution.py:376
  6.1 6.2 %collective-permute-start.5 = (f32[32,128]{1,0:T(8,128)S(1)}, f32[32,128]{1,0:T(8,128)S(1)}, u32[]{:S(2)}, u32[]{:S(2)}) collective-permute-start(f32[32,128]{1,0:T(8,128)S(1)} %pack.1.after_ref.refs_0_.meta_ref), channel_id=1, source_target_pairs={{0,4},{2,6},{4,0},{6,2},{1,5},{3,7},{5,1},{7,3},{8,12},{10,14},{12... | collective-permute-start | bytes 49160 | tf_op jit(solution)/shard_map/ppermute | solution.py:376
  7.1 0.7 %copy-start.7 = (s32[512]{0:T(512)S(1)}, s32[512]{0:T(512)}, u32[]{:S(2)}) copy-start(s32[512]{0:T(512)} %param.14) | copy-start | bytes 6148
  9.0 6.4 %collective-permute-start.3 = (bf16[128,512]{1,0:T(8,128)(2,1)S(1)}, bf16[128,512]{1,0:T(8,128)(2,1)S(1)}, u32[]{:S(2)}, u32[]{:S(2)}) collective-permute-start(bf16[128,512]{1,0:T(8,128)(2,1)S(1)} %interpolate.4.rest_0_), channel_id=1, source_target_pairs={{0,6},{2,0},{4,2},{6,4},{1,7},{3,1},{5,3},{7,5},{8,14},{10,8},{12,... | collective-permute-start | bytes 393224 | tf_op jit(solution)/shard_map/ppermute | solution.py:376
  12.1 11.9 %collective-permute-start.7 = (bf16[128,512]{1,0:T(8,128)(2,1)S(1)}, bf16[128,512]{1,0:T(8,128)(2,1)S(1)}, u32[]{:S(2)}, u32[]{:S(2)}) collective-permute-start(bf16[128,512]{1,0:T(8,128)(2,1)S(1)} %interpolate.5.rest_0_), channel_id=1, source_target_pairs={{0,2},{2,4},{4,6},{6,0},{1,3},{3,5},{5,7},{7,1},{8,10},{10,12},{12... | collective-permute-start | bytes 393224 | tf_op jit(solution)/shard_map/ppermute | solution.py:376
  13.4 10.6 %collective-permute-start.8 = (bf16[128,512]{1,0:T(8,128)(2,1)S(1)}, bf16[128,512]{1,0:T(8,128)(2,1)S(1)}, u32[]{:S(2)}, u32[]{:S(2)}) collective-permute-start(bf16[128,512]{1,0:T(8,128)(2,1)S(1)} %interpolate.6.rest_0_), channel_id=1, source_target_pairs={{0,4},{2,6},{4,0},{6,2},{1,5},{3,7},{5,1},{7,3},{8,12},{10,14},{12... | collective-permute-start | bytes 393224 | tf_op jit(solution)/shard_map/ppermute | solution.py:376
  15.4 8.6 %copy-start.1 = (bf16[3,128,512]{2,1,0:T(8,128)(2,1)S(1)}, bf16[3,128,512]{2,1,0:T(8,128)(2,1)}, u32[]{:S(2)}) copy-start(bf16[3,128,512]{2,1,0:T(8,128)(2,1)} %slope_ref.1) | copy-start | bytes 1179652
  15.4 8.6 %copy-start.2 = (bf16[128,512]{1,0:T(8,128)(2,1)S(1)}, bf16[128,512]{1,0:T(8,128)(2,1)}, u32[]{:S(2)}) copy-start(bf16[128,512]{1,0:T(8,128)(2,1)} %image_ref.1) | copy-start | bytes 393220
  15.4 4.1 %collective-permute-start.6 = (f32[4,8,128]{2,1,0:T(8,128)S(1)}, f32[4,8,128]{2,1,0:T(8,128)S(1)}, u32[]{:S(2)}, u32[]{:S(2)}) collective-permute-start(f32[4,8,128]{2,1,0:T(8,128)S(1)} %collect.1.own_ref), channel_id=1, source_target_pairs={{0,24},{8,0},{16,8},{24,16},{1,25},{9,1},{17,9},{25,17},{2,26},{10... | collective-permute-start | bytes 49160 | tf_op jit(solution)/shard_map/ppermute | solution.py:376
  24.8 1.2 %collective-permute-start.9 = (f32[24,128]{1,0:T(8,128)S(1)}, f32[24,128]{1,0:T(8,128)S(1)}, u32[]{:S(2)}, u32[]{:S(2)}) collective-permute-start(f32[24,128]{1,0:T(8,128)S(1)} %get-tuple-element.15), channel_id=1, source_target_pairs={{0,1},{1,0},{2,3},{3,2},{4,5},{5,4},{6,7},{7,6},{8,9},{9,8},{10,11... | collective-permute-start | bytes 36872 | tf_op jit(solution)/shard_map/ppermute | solution.py:376
  26.2 7.2 %collective-permute-start.10 = (f32[8,128]{1,0:T(8,128)S(1)}, f32[8,128]{1,0:T(8,128)S(1)}, u32[]{:S(2)}, u32[]{:S(2)}) collective-permute-start(f32[8,128]{1,0:T(8,128)S(1)} %get-tuple-element.18), channel_id=1, source_target_pairs={{0,10},{2,12},{4,14},{6,8},{8,18},{10,20},{12,22},{14,16},{16,26},... | collective-permute-start | bytes 12296 | tf_op jit(solution)/shard_map/ppermute | solution.py:384
  26.3 7.2 %collective-permute-start.11 = (f32[8,128]{1,0:T(8,128)S(1)}, f32[8,128]{1,0:T(8,128)S(1)}, u32[]{:S(2)}, u32[]{:S(2)}) collective-permute-start(f32[8,128]{1,0:T(8,128)S(1)} %get-tuple-element.19), channel_id=1, source_target_pairs={{0,2},{2,4},{4,6},{6,0},{1,3},{3,5},{5,7},{7,1},{8,10},{10,12},{12... | collective-permute-start | bytes 12296 | tf_op jit(solution)/shard_map/ppermute | solution.py:376
  27.3 6.2 %collective-permute-start.12 = (f32[8,128]{1,0:T(8,128)S(1)}, f32[8,128]{1,0:T(8,128)S(1)}, u32[]{:S(2)}, u32[]{:S(2)}) collective-permute-start(f32[8,128]{1,0:T(8,128)S(1)} %get-tuple-element.20), channel_id=1, source_target_pairs={{0,8},{8,16},{16,24},{24,0},{1,9},{9,17},{17,25},{25,1},{2,10},{10... | collective-permute-start | bytes 12296 | tf_op jit(solution)/shard_map/ppermute | solution.py:376

commit v6 on v5

--- a/solution.py
+++ b/solution.py
@@ -48,8 +48,8 @@
         centre = (index.astype(jnp.float32) + 0.5) * 0.125
         return jnp.where(upper == 1, centre, 1.0 - centre)
 
-    values = weight(voxel // 64, column // 2 % 2) * weight(voxel // 8 % 8, column % 2)
-    values = values * weight(voxel % 8, column // 4 % 2)
+    values = weight(voxel >> 6, (column >> 1) & 1) * weight((voxel >> 3) & 7, column & 1)
+    values = values * weight(voxel & 7, (column >> 2) & 1)
     coarse = values.astype(jnp.bfloat16).astype(jnp.float32)
     values = jnp.where(column < 8, coarse, jnp.where(column < 16, values - coarse, 0.0))
     out_ref[...] = values.astype(jnp.bfloat16)
@@ -135,7 +135,7 @@
     gy, gz = lax.axis_index("gy"), lax.axis_index("gz")
     half = LANES // 2
     slot = iota((LANES, LANES), 0)
-    slots = (((2 * gy + gz) ^ (slot // half)) * half) + slot % half
+    slots = ((2 * gy + gz) * half) ^ slot
     meta = slot_meta(meta_ref[...], slots)
     chip = lax.rem(gy + distance, lax.axis_size("gy"))
     chip = pl.ds(chip, 1)
@@ -181,22 +181,31 @@
 
 def axis_of_lane(rows):
     lane = iota((rows, LANES), 1)
-    return lane // (CY * CZ), lane // CZ % CY, lane % CZ
-
-
-def force_kernel(cap, relative, across_ref, slot_ref, image_ref, slope_ref, shape_ref, *rest):
+    return lane >> 6, (lane >> 3) & (CY - 1), lane & (CZ - 1)
+
+
+def remainder(cap, chips, slot_ref, base_ref, pieces):
+    total = sum(piece.shape[0] for piece in pieces)
+    number = iota((LANES, total), 1)
+    if chips is not None:
+        n_y = lax.axis_size("gy")
+        gy, gz = lax.axis_index("gy"), lax.axis_index("gz")
+        order = [2 * lax.rem(gy + n_y - d, n_y) + gz for d in chips]
+        lane = iota((1, LANES), 1)
+        number = jnp.concatenate([(holder * cap) ^ lane for holder in order], axis=1)
+    hit = (slot_ref[...] == number).astype(jnp.bfloat16)
+    rows = jnp.concatenate([piece[...] for piece in pieces], axis=0)
+    samples = jnp.dot(hit, rows, preferred_element_type=jnp.float32)
+    return base_ref[...].astype(jnp.float32) - samples
+
+
+def early_kernel(cap, chips, slot_ref, image_ref, *rest):
+    rest[-1][...] = remainder(cap, chips, slot_ref, image_ref, rest[:-1])
+
+
+def force_kernel(cap, chips, across_ref, slot_ref, base_ref, slope_ref, shape_ref, *rest):
     arrived, (kept_ref, sent_ref) = rest[:-2], rest[-2:]
-    total = sum(piece.shape[0] for piece in arrived)
-    number = iota((LANES, total), 1)
-    if relative:
-        n_y = lax.axis_size("gy")
-        chip = lax.rem(lax.axis_index("gy") + n_y - number // (2 * cap), n_y)
-        core = (number // cap % 2) ^ lax.axis_index("gz")
-        number = (2 * chip + core) * cap + number % cap
-    hit = (slot_ref[...] == number).astype(jnp.bfloat16)
-    rows = jnp.concatenate([piece[...] for piece in arrived], axis=0)
-    samples = jnp.dot(hit, rows, preferred_element_type=jnp.float32)
-    difference = image_ref[...].astype(jnp.float32) - samples
+    difference = remainder(cap, chips, slot_ref, base_ref, arrived)
     parts = []
     for d in range(3):
         weighted = slope_ref[d].astype(jnp.float32) * difference
@@ -243,7 +252,7 @@
         own_ref[row, :] = own[0:1] * data_weight + stiff[0:1]
 
 
-def final_kernel(own_ref, xy_ref, y_ref, x_ref, out_ref):
+def final_kernel(own_ref, y_ref, xy_ref, x_ref, out_ref):
     has_x = lax.axis_index("gx") > 0
     has_y = lax.axis_index("gy") > 0
     total = own_ref[0:3, :] + jnp.where(has_x, x_ref[0:3, :], 0.0)
@@ -429,7 +438,8 @@
         table = table_of(deformed_blocks, swapped(deformed_blocks, "gz", 1))
         arrived = [None] * n_y
         previous = []
-        for d in ([3, 1, 2] if n_y == 4 else [1]) + [0]:
+        order = [3, 2, 1] if n_y == 4 else [1]
+        for d in order + [0]:
             samples = sample_call(
                 functools.partial(pair_kernel, d),
                 metas[d],
@@ -464,13 +474,26 @@
             stiffness_kernel, [(8, LANES)], "stiffness", ring(slab, "gx", 1), slab, ring(slab, "gx", -1)
         )
         across = jnp.zeros((8, LANES), jnp.float32)
+    base, chips = reference_image, None
+    if relative:
+        chips = (0, order[0])[: n_y - 1]
+        (base,) = small_call(
+            functools.partial(early_kernel, cap, chips),
+            [(LANES, 512)],
+            "early",
+            recv_slot[:, None],
+            base,
+            *[arrived[d] for d in chips],
+        )
+        chips = tuple(order[1:]) or (order[0],)
+        arrived = [arrived[d] for d in chips]
     kept, sent = small_call(
-        functools.partial(force_kernel, cap, relative),
+        functools.partial(force_kernel, cap, chips),
         [(24, LANES)] * 2,
         "forces",
         across,
         recv_slot[:, None],
-        reference_image,
+        base,
         image_gradient,
         shape_values,
         *arrived,
@@ -479,7 +502,7 @@
         layer_kernel, [(8, LANES)] * 4, "layers", kept, ring(sent, "gz"), stiff
     )
     return small_call(
-        final_kernel, [(3, LANES)], "total", own, ring_2(xy), ring(y, "gy"), ring(x, "gx")
+        final_kernel, [(3, LANES)], "total", own, ring(y, "gy"), ring_2(xy), ring(x, "gx")
     )[0]
 
 

time: 34.3 us -> 33.9 us (0.988)
  waiting for transfers between devices: 10.5 us -> 9.02 us
  starting transfers between devices: 15.9 us -> 16.7 us
    ppermute x1, starting transfers between devices: 0.04 us -> 2.97 us  [ring_2(): return lax.ppermute(value, ('gx', 'gy'), route)]
    ppermute x1, waiting for transfers between devices: 4.68 us -> 1.92 us  [ring_2(): return lax.ppermute(value, ('gx', 'gy'), route)]
    ppermute x10, starting transfers between devices: 15.2 us -> 13.2 us  [ring(): lax.ppermute(value, axes, [(i, (i + distance) % count) for i in range(cou...]
    ppermute x10, waiting for transfers between devices: 5.84 us -> 7.1 us  [ring(): lax.ppermute(value, axes, [(i, (i + distance) % count) for i in range(cou...]
    pallas_call x8 -> x9, Pallas kernels: 2.6 us -> 2.75 us  [vmem_call(): pl.pallas_call(kernel, out_shape=[jax.ShapeDtypeStruct(shape, dtype) for...]
  transfers between devices with their start and end apart: 13 -> 13, of which waited for: 5 -> 8; matrix products, arithmetic and copies ran while one was open for 0% -> 0% of each run, Pallas kernels for 16% -> 17%
where the time goes in v6:
time: 33.9 us; the launch traced here: 33.7 us
  starting transfers between devices  16.7 us (49%)
  waiting for transfers between devices  9.02 us (27%)
  Pallas kernels  7.26 us (21%)
  local copies, waits for them, and re-layouts  0.5 us (1%)
    ppermute x10, starting transfers between devices, ring(): lax.ppermute(value, axes, [(i, (i + distance) % count) for i in range(cou...  13.2 us
    ppermute x10, waiting for transfers between devices, ring(): lax.ppermute(value, axes, [(i, (i + distance) % count) for i in range(cou...  7.1 us
    pallas_call x4, Pallas kernels, sample_call(): pl.pallas_call(kernel, out_shape=jax.ShapeDtypeStruct((LANES, 512), jnp.b...  4.52 us
    ppermute x1, starting transfers between devices, ring_2(): return lax.ppermute(value, ('gx', 'gy'), route)  2.97 us
    pallas_call x9, Pallas kernels, vmem_call(): pl.pallas_call(kernel, out_shape=[jax.ShapeDtypeStruct(shape, dtype) for...  2.75 us
    ppermute x1, waiting for transfers between devices, ring_2(): return lax.ppermute(value, ('gx', 'gy'), route)  1.92 us
  transfers between devices with their start and end apart: 13, of which 8 were waited for; matrix products, arithmetic and copies ran while one was open for 0% of the time, Pallas kernels for 17%

profile of v6, /device:TPU:0, one launch (start us, length us, event | category | flops | bytes accessed | tf_op | source)
XLA Modules:
  0.0 33.7 jit_solution(1884234722227518824)
XLA Ops:
  0.0 0.5 %collective-permute-start.2 = (bf16[128,4096]{1,0:T(8,128)(2,1)}, bf16[128,4096]{1,0:T(8,128)(2,1)S(1)}, u32[]{:S(2)}, u32[]{:S(2)}) collective-permute-start(bf16[128,4096]{1,0:T(8,128)(2,1)} %refs_0_.1), channel_id=1, source_target_pairs={{0,1},{1,0},{2,3},{3,2},{4,5},{5,4},{6,7},{7,6},{8,9},{9,8},{10,11... | collective-permute-start | bytes 3145736 | tf_op jit(solution)/shard_map/ppermute | solution.py:397
  0.5 0.0 copy-start.3
  0.5 0.0 copy-start
  0.5 0.1 collective-permute-start.1
  0.6 0.2 shapes.1.after_ref.shape_ref
  0.8 0.3 copy-done.3
  1.1 0.0 copy-done.4
  1.2 0.0 copy-done.5
  1.2 0.0 copy-done.6
  1.2 2.8 %collective-permute-start = (f32[32,128]{1,0:T(8,128)S(1)}, f32[32,128]{1,0:T(8,128)S(1)}, u32[]{:S(2)}, u32[]{:S(2)}) collective-permute-start(f32[32,128]{1,0:T(8,128)S(1)} %pack.1.after_ref.refs_0_.meta_ref), channel_id=1, source_target_pairs={{0,2},{2,4},{4,6},{6,0},{1,3},{3,5},{5,7},{7,1},{8,10},{10,12},{12... | collective-permute-start | bytes 49160 | tf_op jit(solution)/shard_map/ppermute | solution.py:385
  4.0 2.6 %collective-permute-start.5 = (f32[32,128]{1,0:T(8,128)S(1)}, f32[32,128]{1,0:T(8,128)S(1)}, u32[]{:S(2)}, u32[]{:S(2)}) collective-permute-start(f32[32,128]{1,0:T(8,128)S(1)} %pack.1.after_ref.refs_0_.meta_ref), channel_id=1, source_target_pairs={{0,4},{2,6},{4,0},{6,2},{1,5},{3,7},{5,1},{7,3},{8,12},{10,14},{12... | collective-permute-start | bytes 49160 | tf_op jit(solution)/shard_map/ppermute | solution.py:385
  6.6 1.3 %collective-permute-start.4 = (f32[32,128]{1,0:T(8,128)S(1)}, f32[32,128]{1,0:T(8,128)S(1)}, u32[]{:S(2)}, u32[]{:S(2)}) collective-permute-start(f32[32,128]{1,0:T(8,128)S(1)} %pack.1.after_ref.refs_0_.meta_ref), channel_id=1, source_target_pairs={{0,6},{2,0},{4,2},{6,4},{1,7},{3,1},{5,3},{7,5},{8,14},{10,8},{12,... | collective-permute-start | bytes 49160 | tf_op jit(solution)/shard_map/ppermute | solution.py:385
  7.9 0.1 copy.10.slot_ref
  8.0 0.0 collective-permute-done.1.later_ref.mate_ref
  8.0 0.0 collective-permute-done.2.refs_1_
  8.0 0.0 copy-done
  8.1 0.6 %table.1.table_ref = bf16[4096,256]{1,0:T(8,128)(2,1)S(1)} custom-call(f32[32,128]{1,0:T(8,128)S(1)} %pack.1.after_ref.refs_0_.meta_ref, s32[4,128]{1,0:T(4,128)S(1)} %collective-permute-done.1.later_ref.mate_ref, bf16[128,4096]{1,0:T(8,128)(2,1)S(1)} %copy-done, bf16[128,4096]{1,0:T(8,128)(2,1)S(1)} %collective-permute-done.2.refs_1_), custom_call_target="tpu_custom_call" | custom-call | flops 805306368 | bytes 1048576 | tf_op jit(solution)/shard_map/table/pallas_call | solution.py:77
  8.7 0.0 collective-permute-done.meta_ref.refs_3_
  8.7 0.0 copy-done.7
  8.7 1.1 %interpolate.4.rest_0_ = bf16[128,512]{1,0:T(8,128)(2,1)S(1)} custom-call(f32[32,128]{1,0:T(8,128)S(1)} %collective-permute-done.meta_ref.refs_3_, bf16[4096,256]{1,0:T(8,128)(2,1)S(1)} %table.1.table_ref, s32[4,128]{1,0:T(4,128)S(1)} %bitcast.6, s32[4,128]{1,0:T(4,128)S(1)} %collective-permute-done.1.later_ref.mate_ref), custom_call_target="tpu_custom_call" | custom-call | flops 4000000000 | bytes 1 | tf_op jit(solution)/shard_map/interpolate/pallas_call | solution.py:164
  9.8 1.1 %collective-permute-start.3 = (bf16[128,512]{1,0:T(8,128)(2,1)S(1)}, bf16[128,512]{1,0:T(8,128)(2,1)S(1)}, u32[]{:S(2)}, u32[]{:S(2)}) collective-permute-start(bf16[128,512]{1,0:T(8,128)(2,1)S(1)} %interpolate.4.rest_0_), channel_id=1, source_target_pairs={{0,6},{2,0},{4,2},{6,4},{1,7},{3,1},{5,3},{7,5},{8,14},{10,8},{12,... | collective-permute-start | bytes 393224 | tf_op jit(solution)/shard_map/ppermute | solution.py:385
  10.9 0.0 collective-permute-done.5.refs_2_.meta_ref
  10.9 1.1 %interpolate.5.rest_0_ = bf16[128,512]{1,0:T(8,128)(2,1)S(1)} custom-call(f32[32,128]{1,0:T(8,128)S(1)} %collective-permute-done.5.refs_2_.meta_ref, bf16[4096,256]{1,0:T(8,128)(2,1)S(1)} %table.1.table_ref, s32[4,128]{1,0:T(4,128)S(1)} %bitcast.7, s32[4,128]{1,0:T(4,128)S(1)} %collective-permute-done.1.later_ref.mate_ref, ...), custom_call_target="tpu_custom_call" | custom-call | flops 4000000000 | bytes 1 | tf_op jit(solution)/shard_map/interpolate/pallas_call | solution.py:164
  12.1 1.2 %collective-permute-start.7 = (bf16[128,512]{1,0:T(8,128)(2,1)S(1)}, bf16[128,512]{1,0:T(8,128)(2,1)S(1)}, u32[]{:S(2)}, u32[]{:S(2)}) collective-permute-start(bf16[128,512]{1,0:T(8,128)(2,1)S(1)} %interpolate.5.rest_0_), channel_id=1, source_target_pairs={{0,4},{2,6},{4,0},{6,2},{1,5},{3,7},{5,1},{7,3},{8,12},{10,14},{12... | collective-permute-start | bytes 393224 | tf_op jit(solution)/shard_map/ppermute | solution.py:385
  13.2 0.0 collective-permute-done.4.refs_1_.meta_ref
  13.2 1.1 %interpolate.6.rest_0_ = bf16[128,512]{1,0:T(8,128)(2,1)S(1)} custom-call(f32[32,128]{1,0:T(8,128)S(1)} %collective-permute-done.4.refs_1_.meta_ref, bf16[4096,256]{1,0:T(8,128)(2,1)S(1)} %table.1.table_ref, s32[4,128]{1,0:T(4,128)S(1)} %bitcast.8, s32[4,128]{1,0:T(4,128)S(1)} %collective-permute-done.1.later_ref.mate_ref, ...), custom_call_target="tpu_custom_call" | custom-call | flops 4000000000 | bytes 1 | tf_op jit(solution)/shard_map/interpolate/pallas_call | solution.py:164
  14.4 0.1 collective-permute-start.8
  14.5 0.7 %collective-permute-done.3.after_ref.rest_1_ = bf16[128,512]{1,0:T(8,128)(2,1)S(1)} collective-permute-done((bf16[128,512]{1,0:T(8,128)(2,1)S(1)}, bf16[128,512]{1,0:T(8,128)(2,1)S(1)}, u32[]{:S(2)}, u32[]{:S(2)}) %collective-permute-start.3) | collective-permute-done | bytes 131104 | tf_op jit(solution)/shard_map/ppermute | solution.py:385
  15.2 2.5 %collective-permute-start.6 = (f32[4,8,128]{2,1,0:T(8,128)S(1)}, f32[4,8,128]{2,1,0:T(8,128)S(1)}, u32[]{:S(2)}, u32[]{:S(2)}) collective-permute-start(f32[4,8,128]{2,1,0:T(8,128)S(1)} %collect.1.own_ref), channel_id=1, source_target_pairs={{0,24},{8,0},{16,8},{24,16},{1,25},{9,1},{17,9},{25,17},{2,26},{10... | collective-permute-start | bytes 49160 | tf_op jit(solution)/shard_map/ppermute | solution.py:385
  17.7 1.1 %interpolate.7.rest_0_ = bf16[128,512]{1,0:T(8,128)(2,1)S(1)} custom-call(f32[32,128]{1,0:T(8,128)S(1)} %pack.1.after_ref.refs_0_.meta_ref, bf16[4096,256]{1,0:T(8,128)(2,1)S(1)} %table.1.table_ref, s32[4,128]{1,0:T(4,128)S(1)} %bitcast.9, s32[4,128]{1,0:T(4,128)S(1)} %collective-permute-done.1.later_ref.mate_ref, bf16[128,512]{1,0:T(8,128)(2,1)S(1)} %interpolate.6.rest_0_), custom_call_target="tpu_custom_call" | custom-call | flops 4000000000 | bytes 1 | tf_op jit(solution)/shard_map/interpolate/pallas_call | solution.py:164
  18.8 0.0 copy-done.2
  18.8 0.2 early.1.base_ref
  19.1 0.1 collective-permute-done.6.above_ref
  19.1 0.2 stiffness.1
  19.3 1.9 %collective-permute-done.8.rest_1_ = bf16[128,512]{1,0:T(8,128)(2,1)S(1)} collective-permute-done((bf16[128,512]{1,0:T(8,128)(2,1)S(1)}, bf16[128,512]{1,0:T(8,128)(2,1)S(1)}, u32[]{:S(2)}, u32[]{:S(2)}) %collective-permute-start.8) | collective-permute-done | bytes 131104 | tf_op jit(solution)/shard_map/ppermute | solution.py:385
  21.2 2.2 %collective-permute-done.7.rest_0_ = bf16[128,512]{1,0:T(8,128)(2,1)S(1)} collective-permute-done((bf16[128,512]{1,0:T(8,128)(2,1)S(1)}, bf16[128,512]{1,0:T(8,128)(2,1)S(1)}, u32[]{:S(2)}, u32[]{:S(2)}) %collective-permute-start.7) | collective-permute-done | bytes 131104 | tf_op jit(solution)/shard_map/ppermute | solution.py:385
  23.4 0.0 copy-done.1
  23.4 0.8 %forces.1 = (f32[24,128]{1,0:T(8,128)S(1)}, f32[24,128]{1,0:T(8,128)S(1)}) custom-call(f32[8,128]{1,0:T(8,128)S(1)} %get-tuple-element.13.across_ref, s32[128,1]{1,0:T(8,128)S(1)} %copy.10.slot_ref, f32[128,512]{1,0:T(8,128)S(1)} %early.1.base_ref, bf16[3,128,512]{2,1,0:T(8,128)(2,1)S(1)} %copy-done.1, bf16[512,128]{1,0:T(8,128)(2,1)S(1)} %shapes.1.after_ref.shape_ref, ...), custom_call_target="tpu_custom_call" | custom-call | flops 1048576 | bytes 1048576 | tf_op jit(solution)/shard_map/forces/pallas_call | solution.py:77
  24.2 0.1 collective-permute-start.9
  24.2 1.2 %collective-permute-done.9.arrived_ref = f32[24,128]{1,0:T(8,128)S(1)} collective-permute-done((f32[24,128]{1,0:T(8,128)S(1)}, f32[24,128]{1,0:T(8,128)S(1)}, u32[]{:S(2)}, u32[]{:S(2)}) %collective-permute-start.9) | collective-permute-done | bytes 12320 | tf_op jit(solution)/shard_map/ppermute | solution.py:385
  25.4 0.1 layers.1
  25.6 0.0 collective-permute-start.10
  25.6 3.0 %collective-permute-start.11 = (f32[8,128]{1,0:T(8,128)S(1)}, f32[8,128]{1,0:T(8,128)S(1)}, u32[]{:S(2)}, u32[]{:S(2)}) collective-permute-start(f32[8,128]{1,0:T(8,128)S(1)} %get-tuple-element.19), channel_id=1, source_target_pairs={{0,10},{2,12},{4,14},{6,8},{8,18},{10,20},{12,22},{14,16},{16,26},... | collective-permute-start | bytes 12296 | tf_op jit(solution)/shard_map/ppermute | solution.py:393
  28.6 1.5 %collective-permute-start.12 = (f32[8,128]{1,0:T(8,128)S(1)}, f32[8,128]{1,0:T(8,128)S(1)}, u32[]{:S(2)}, u32[]{:S(2)}) collective-permute-start(f32[8,128]{1,0:T(8,128)S(1)} %get-tuple-element.20), channel_id=1, source_target_pairs={{0,8},{8,16},{16,24},{24,0},{1,9},{9,17},{17,25},{25,1},{2,10},{10... | collective-permute-start | bytes 12296 | tf_op jit(solution)/shard_map/ppermute | solution.py:385
  30.1 0.9 %collective-permute-done.10.y_ref = f32[8,128]{1,0:T(8,128)S(1)} collective-permute-done((f32[8,128]{1,0:T(8,128)S(1)}, f32[8,128]{1,0:T(8,128)S(1)}, u32[]{:S(2)}, u32[]{:S(2)}) %collective-permute-start.10) | collective-permute-done | bytes 4128 | tf_op jit(solution)/shard_map/ppermute | solution.py:385
  31.0 1.9 %collective-permute-done.11.xy_ref = f32[8,128]{1,0:T(8,128)S(1)} collective-permute-done((f32[8,128]{1,0:T(8,128)S(1)}, f32[8,128]{1,0:T(8,128)S(1)}, u32[]{:S(2)}, u32[]{:S(2)}) %collective-permute-start.11) | collective-permute-done | bytes 4128 | tf_op jit(solution)/shard_map/ppermute | solution.py:393
  32.9 0.2 collective-permute-done.12.x_ref
  33.1 0.6 %total.1 = f32[3,128]{1,0:T(4,128)} custom-call(f32[8,128]{1,0:T(8,128)S(1)} %get-tuple-element.17.own_ref, f32[8,128]{1,0:T(8,128)S(1)} %collective-permute-done.10.y_ref, f32[8,128]{1,0:T(8,128)S(1)} %collective-permute-done.11.xy_ref, f32[8,128]{1,0:T(8,128)S(1)} %collective-permute-done.12.x_ref), custom_call_target="tpu_custom_call" | custom-call | flops 1048576 | bytes 1048576 | tf_op jit(solution)/shard_map/total/pallas_call | solution.py:77
  (8 shorter events, 0.0 us)
Async XLA Ops:
  0.0 8.0 %collective-permute-start.2 = (bf16[128,4096]{1,0:T(8,128)(2,1)}, bf16[128,4096]{1,0:T(8,128)(2,1)S(1)}, u32[]{:S(2)}, u32[]{:S(2)}) collective-permute-start(bf16[128,4096]{1,0:T(8,128)(2,1)} %refs_0_.1), channel_id=1, source_target_pairs={{0,1},{1,0},{2,3},{3,2},{4,5},{5,4},{6,7},{7,6},{8,9},{9,8},{10,11... | collective-permute-start | bytes 3145736 | tf_op jit(solution)/shard_map/ppermute | solution.py:397
  0.5 0.7 %copy-start.3 = (bf16[24,128]{1,0:T(8,128)(2,1)S(1)}, bf16[24,128]{1,0:T(8,128)(2,1)}, u32[]{:S(2)}) copy-start(bf16[24,128]{1,0:T(8,128)(2,1)} %fraction_ref.1) | copy-start | bytes 18436
  0.5 0.7 %copy-start.4 = (f32[3,128]{1,0:T(4,128)S(1)}, f32[3,128]{1,0:T(4,128)}, u32[]{:S(2)}) copy-start(f32[3,128]{1,0:T(4,128)} %displacement_ref.1) | copy-start | bytes 4612
  0.5 0.7 %copy-start.5 = (s32[3,128]{1,0:T(4,128)S(1)}, s32[3,128]{1,0:T(4,128)}, u32[]{:S(2)}) copy-start(s32[3,128]{1,0:T(4,128)} %offset_ref.1) | copy-start | bytes 4612
  0.5 0.7 %copy-start.6 = (s32[128]{0:T(128)S(1)}, s32[128]{0:T(128)}, u32[]{:S(2)}) copy-start(s32[128]{0:T(128)} %param.15) | copy-start | bytes 1540
  0.5 7.6 %copy-start = (bf16[128,4096]{1,0:T(8,128)(2,1)S(1)}, bf16[128,4096]{1,0:T(8,128)(2,1)}, u32[]{:S(2)}) copy-start(bf16[128,4096]{1,0:T(8,128)(2,1)} %refs_0_.1) | copy-start | bytes 3145732
  0.5 7.6 %collective-permute-start.1 = (s32[4,128]{1,0:T(4,128)}, s32[4,128]{1,0:T(4,128)S(1)}, u32[]{:S(2)}, u32[]{:S(2)}) collective-permute-start(s32[4,128]{1,0:T(4,128)} %bitcast.5), channel_id=1, source_target_pairs={{0,1},{1,0},{2,3},{3,2},{4,5},{5,4},{6,7},{7,6},{8,9},{9,8},{10,11... | collective-permute-start | bytes 6152 | tf_op jit(solution)/shard_map/ppermute | solution.py:397
  1.2 7.5 %collective-permute-start = (f32[32,128]{1,0:T(8,128)S(1)}, f32[32,128]{1,0:T(8,128)S(1)}, u32[]{:S(2)}, u32[]{:S(2)}) collective-permute-start(f32[32,128]{1,0:T(8,128)S(1)} %pack.1.after_ref.refs_0_.meta_ref), channel_id=1, source_target_pairs={{0,2},{2,4},{4,6},{6,0},{1,3},{3,5},{5,7},{7,1},{8,10},{10,12},{12... | collective-permute-start | bytes 49160 | tf_op jit(solution)/shard_map/ppermute | solution.py:385
  4.0 7.0 %collective-permute-start.5 = (f32[32,128]{1,0:T(8,128)S(1)}, f32[32,128]{1,0:T(8,128)S(1)}, u32[]{:S(2)}, u32[]{:S(2)}) collective-permute-start(f32[32,128]{1,0:T(8,128)S(1)} %pack.1.after_ref.refs_0_.meta_ref), channel_id=1, source_target_pairs={{0,4},{2,6},{4,0},{6,2},{1,5},{3,7},{5,1},{7,3},{8,12},{10,14},{12... | collective-permute-start | bytes 49160 | tf_op jit(solution)/shard_map/ppermute | solution.py:385
  6.6 6.7 %collective-permute-start.4 = (f32[32,128]{1,0:T(8,128)S(1)}, f32[32,128]{1,0:T(8,128)S(1)}, u32[]{:S(2)}, u32[]{:S(2)}) collective-permute-start(f32[32,128]{1,0:T(8,128)S(1)} %pack.1.after_ref.refs_0_.meta_ref), channel_id=1, source_target_pairs={{0,6},{2,0},{4,2},{6,4},{1,7},{3,1},{5,3},{7,5},{8,14},{10,8},{12,... | collective-permute-start | bytes 49160 | tf_op jit(solution)/shard_map/ppermute | solution.py:385
  8.0 0.7 %copy-start.7 = (s32[512]{0:T(512)S(1)}, s32[512]{0:T(512)}, u32[]{:S(2)}) copy-start(s32[512]{0:T(512)} %param.14) | copy-start | bytes 6148
  9.8 5.4 %collective-permute-start.3 = (bf16[128,512]{1,0:T(8,128)(2,1)S(1)}, bf16[128,512]{1,0:T(8,128)(2,1)S(1)}, u32[]{:S(2)}, u32[]{:S(2)}) collective-permute-start(bf16[128,512]{1,0:T(8,128)(2,1)S(1)} %interpolate.4.rest_0_), channel_id=1, source_target_pairs={{0,6},{2,0},{4,2},{6,4},{1,7},{3,1},{5,3},{7,5},{8,14},{10,8},{12,... | collective-permute-start | bytes 393224 | tf_op jit(solution)/shard_map/ppermute | solution.py:385
  12.1 11.3 %collective-permute-start.7 = (bf16[128,512]{1,0:T(8,128)(2,1)S(1)}, bf16[128,512]{1,0:T(8,128)(2,1)S(1)}, u32[]{:S(2)}, u32[]{:S(2)}) collective-permute-start(bf16[128,512]{1,0:T(8,128)(2,1)S(1)} %interpolate.5.rest_0_), channel_id=1, source_target_pairs={{0,4},{2,6},{4,0},{6,2},{1,5},{3,7},{5,1},{7,3},{8,12},{10,14},{12... | collective-permute-start | bytes 393224 | tf_op jit(solution)/shard_map/ppermute | solution.py:385
  14.4 6.8 %collective-permute-start.8 = (bf16[128,512]{1,0:T(8,128)(2,1)S(1)}, bf16[128,512]{1,0:T(8,128)(2,1)S(1)}, u32[]{:S(2)}, u32[]{:S(2)}) collective-permute-start(bf16[128,512]{1,0:T(8,128)(2,1)S(1)} %interpolate.6.rest_0_), channel_id=1, source_target_pairs={{0,2},{2,4},{4,6},{6,0},{1,3},{3,5},{5,7},{7,1},{8,10},{10,12},{12... | collective-permute-start | bytes 393224 | tf_op jit(solution)/shard_map/ppermute | solution.py:385
  15.2 3.6 %copy-start.2 = (bf16[128,512]{1,0:T(8,128)(2,1)S(1)}, bf16[128,512]{1,0:T(8,128)(2,1)}, u32[]{:S(2)}) copy-start(bf16[128,512]{1,0:T(8,128)(2,1)} %image_ref.1) | copy-start | bytes 393220
  15.2 8.2 %copy-start.1 = (bf16[3,128,512]{2,1,0:T(8,128)(2,1)S(1)}, bf16[3,128,512]{2,1,0:T(8,128)(2,1)}, u32[]{:S(2)}) copy-start(bf16[3,128,512]{2,1,0:T(8,128)(2,1)} %slope_ref.1) | copy-start | bytes 1179652
  15.2 3.9 %collective-permute-start.6 = (f32[4,8,128]{2,1,0:T(8,128)S(1)}, f32[4,8,128]{2,1,0:T(8,128)S(1)}, u32[]{:S(2)}, u32[]{:S(2)}) collective-permute-start(f32[4,8,128]{2,1,0:T(8,128)S(1)} %collect.1.own_ref), channel_id=1, source_target_pairs={{0,24},{8,0},{16,8},{24,16},{1,25},{9,1},{17,9},{25,17},{2,26},{10... | collective-permute-start | bytes 49160 | tf_op jit(solution)/shard_map/ppermute | solution.py:385
  24.2 1.2 %collective-permute-start.9 = (f32[24,128]{1,0:T(8,128)S(1)}, f32[24,128]{1,0:T(8,128)S(1)}, u32[]{:S(2)}, u32[]{:S(2)}) collective-permute-start(f32[24,128]{1,0:T(8,128)S(1)} %get-tuple-element.15), channel_id=1, source_target_pairs={{0,1},{1,0},{2,3},{3,2},{4,5},{5,4},{6,7},{7,6},{8,9},{9,8},{10,11... | collective-permute-start | bytes 36872 | tf_op jit(solution)/shard_map/ppermute | solution.py:385
  25.6 5.4 %collective-permute-start.10 = (f32[8,128]{1,0:T(8,128)S(1)}, f32[8,128]{1,0:T(8,128)S(1)}, u32[]{:S(2)}, u32[]{:S(2)}) collective-permute-start(f32[8,128]{1,0:T(8,128)S(1)} %get-tuple-element.18), channel_id=1, source_target_pairs={{0,2},{2,4},{4,6},{6,0},{1,3},{3,5},{5,7},{7,1},{8,10},{10,12},{12... | collective-permute-start | bytes 12296 | tf_op jit(solution)/shard_map/ppermute | solution.py:385
  25.6 7.3 %collective-permute-start.11 = (f32[8,128]{1,0:T(8,128)S(1)}, f32[8,128]{1,0:T(8,128)S(1)}, u32[]{:S(2)}, u32[]{:S(2)}) collective-permute-start(f32[8,128]{1,0:T(8,128)S(1)} %get-tuple-element.19), channel_id=1, source_target_pairs={{0,10},{2,12},{4,14},{6,8},{8,18},{10,20},{12,22},{14,16},{16,26},... | collective-permute-start | bytes 12296 | tf_op jit(solution)/shard_map/ppermute | solution.py:393
  28.6 4.5 %collective-permute-start.12 = (f32[8,128]{1,0:T(8,128)S(1)}, f32[8,128]{1,0:T(8,128)S(1)}, u32[]{:S(2)}, u32[]{:S(2)}) collective-permute-start(f32[8,128]{1,0:T(8,128)S(1)} %get-tuple-element.20), channel_id=1, source_target_pairs={{0,8},{8,16},{16,24},{24,0},{1,9},{9,17},{17,25},{25,1},{2,10},{10... | collective-permute-start | bytes 12296 | tf_op jit(solution)/shard_map/ppermute | solution.py:385

commit v7 on v6

--- a/solution.py
+++ b/solution.py
@@ -23,6 +23,7 @@
 META = 32
 
 VOXELS = 4096
+SENT = 24
 
 
 def iota(shape, dim):
@@ -204,7 +205,7 @@
 
 
 def force_kernel(cap, chips, across_ref, slot_ref, base_ref, slope_ref, shape_ref, *rest):
-    arrived, (kept_ref, sent_ref) = rest[:-2], rest[-2:]
+    arrived, out_ref = rest[:-1], rest[-1]
     difference = remainder(cap, chips, slot_ref, base_ref, arrived)
     parts = []
     for d in range(3):
@@ -223,33 +224,66 @@
     for d in range(3):
         corners = columns[16 * d : 16 * d + 8] + columns[16 * d + 8 : 16 * d + 16]
         carried = pltpu.roll(corners, 4, 0)
-        kept_ref[8 * d : 8 * d + 8, :] = corners + jnp.where(at_k > 0, pltpu.roll(carried, 1, 1), 0.0)
-        sent_ref[8 * d : 8 * d + 8, :] = jnp.where(at_k == 0, pltpu.roll(carried, LANES - 7, 1), 0.0)
-        sent_ref[8 * d + 4 : 8 * d + 6, :] = across_ref[2 * d : 2 * d + 2, :]
-
-
-def layer_kernel(kept_ref, arrived_ref, stiff_ref, xy_ref, y_ref, x_ref, own_ref):
+        kept, sent = 8 * d, SENT + 8 * d
+        out_ref[kept : kept + 8, :] = corners + jnp.where(at_k > 0, pltpu.roll(carried, 1, 1), 0.0)
+        out_ref[sent : sent + 8, :] = jnp.where(at_k == 0, pltpu.roll(carried, LANES - 7, 1), 0.0)
+        out_ref[sent + 4 : sent + 6, :] = across_ref[2 * d : 2 * d + 2, :]
+
+
+def layers(d, z):
     at_i, at_j, _ = axis_of_lane(8)
-    behind = lax.axis_index("gz") > 0
 
     def along_x(lower_half, upper_half):
         moved = pltpu.roll(upper_half, CY * CZ, 1)
         return lower_half + jnp.where(at_i > 0, moved, 0.0), jnp.where(at_i == 0, moved, 0.0)
 
+    carried = pltpu.roll(z, 7, 0)
+    stay = z + jnp.where(at_j > 0, pltpu.roll(carried, CZ, 1), 0.0)
+    leave = jnp.where(at_j == 0, pltpu.roll(carried, LANES - CZ * (CY - 1), 1), 0.0)
+    own, x = along_x(stay, pltpu.roll(stay, 6, 0))
+    y, xy = along_x(leave, pltpu.roll(leave, 6, 0))
+    return [value[0:1] * data_weight for value in (own, x, y, xy)]
+
+
+def layer_kernel(kept_ref, arrived_ref, stiff_ref, xy_ref, y_ref, x_ref, own_ref):
+    behind = lax.axis_index("gz") > 0
     for d in range(3):
-        part = slice(8 * d, 8 * d + 8)
-        z = kept_ref[part, :] + jnp.where(behind, arrived_ref[part, :], 0.0)
-        carried = pltpu.roll(z, 7, 0)
-        stay = z + jnp.where(at_j > 0, pltpu.roll(carried, CZ, 1), 0.0)
-        leave = jnp.where(at_j == 0, pltpu.roll(carried, LANES - CZ * (CY - 1), 1), 0.0)
-        own, x = along_x(stay, pltpu.roll(stay, 6, 0))
-        y, xy = along_x(leave, pltpu.roll(leave, 6, 0))
-        stiff = stiff_ref[2 * d : 2 * d + 2, :] + arrived_ref[8 * d + 4 : 8 * d + 6, :]
+        part, sent = slice(8 * d, 8 * d + 8), slice(SENT + 8 * d, SENT + 8 * d + 8)
+        z = kept_ref[part, :] + jnp.where(behind, arrived_ref[sent, :], 0.0)
+        own, x, y, xy = layers(d, z)
+        stiff = stiff_ref[2 * d : 2 * d + 2, :]
         row = slice(d, d + 1)
-        xy_ref[row, :] = xy[0:1] * data_weight
-        y_ref[row, :] = y[0:1] * data_weight
-        x_ref[row, :] = x[0:1] * data_weight + stiff[1:2]
-        own_ref[row, :] = own[0:1] * data_weight + stiff[0:1]
+        xy_ref[row, :] = xy
+        y_ref[row, :] = y
+        x_ref[row, :] = x + stiff[1:2]
+        own_ref[row, :] = own + stiff[0:1]
+
+
+def chip_kernel(here_ref, mate_ref, stiff_ref, turn_ref, x_ref, own_ref):
+    first = lax.axis_index("gz") == 0
+    turn_ref[...] = jnp.zeros((8, LANES), jnp.float32)
+    for d in range(3):
+        part, sent = slice(8 * d, 8 * d + 8), slice(SENT + 8 * d, SENT + 8 * d + 8)
+        z = here_ref[part, :] + jnp.where(first, 0.0, mate_ref[sent, :])
+        own, x, y, xy = layers(d, z)
+        row = slice(d, d + 1)
+        turn_ref[row, :] = jnp.where(first, y, xy)
+        stiff = stiff_ref[2 * d : 2 * d + 2, :] + mate_ref[SENT + 8 * d + 4 : SENT + 8 * d + 6, :]
+        x_ref[row, :] = x + stiff[1:2]
+        own_ref[row, :] = own + stiff[0:1]
+        z = mate_ref[part, :] + jnp.where(first, here_ref[sent, :], 0.0)
+        _, _, y, xy = layers(d, z)
+        turn_ref[d + 3 : d + 4, :] = jnp.where(first, y, xy)
+
+
+def chip_total_kernel(own_ref, turned_ref, mate_ref, x_ref, out_ref):
+    has_x, has_y = lax.axis_index("gx") > 0, lax.axis_index("gy") > 0
+    first = lax.axis_index("gz") == 0
+    total = own_ref[0:3, :] + jnp.where(has_x, x_ref[0:3, :], 0.0)
+    has = has_y & (first | has_x)
+    total = total + jnp.where(has, turned_ref[0:3, :], 0.0)
+    has = has_y & (jnp.logical_not(first) | has_x)
+    out_ref[...] = total + jnp.where(has, mate_ref[3:6, :], 0.0)
 
 
 def final_kernel(own_ref, y_ref, xy_ref, x_ref, out_ref):
@@ -391,6 +425,17 @@
         (x * ny + y, (x + 1) % nx * ny + (y + 1) % ny) for x in range(nx) for y in range(ny)
     ]
     return lax.ppermute(value, ("gx", "gy"), route)
+
+
+def turned_ring(value):
+    nx, ny = lax.axis_size("gx"), lax.axis_size("gy")
+    route = [
+        ((x * ny + y) * 2 + core, ((x + core) % nx * ny + (y + 1) % ny) * 2 + core)
+        for x in range(nx)
+        for y in range(ny)
+        for core in range(2)
+    ]
+    return lax.ppermute(value, ("gx", "gy", "gz"), route)
 
 
 def swapped(value, axes, mask):
@@ -487,9 +532,9 @@
         )
         chips = tuple(order[1:]) or (order[0],)
         arrived = [arrived[d] for d in chips]
-    kept, sent = small_call(
+    (force,) = small_call(
         functools.partial(force_kernel, cap, chips),
-        [(24, LANES)] * 2,
+        [(2 * SENT, LANES)],
         "forces",
         across,
         recv_slot[:, None],
@@ -498,9 +543,14 @@
         shape_values,
         *arrived,
     )
-    xy, y, x, own = small_call(
-        layer_kernel, [(8, LANES)] * 4, "layers", kept, ring(sent, "gz"), stiff
-    )
+    came = ring(force, "gz")
+    if relative:
+        turn, x, own = small_call(chip_kernel, [(8, LANES)] * 3, "layers", force, came, stiff)
+        turned = turned_ring(turn)
+        return small_call(
+            chip_total_kernel, [(3, LANES)], "total", own, turned, ring(turned, "gz"), ring(x, "gx")
+        )[0]
+    xy, y, x, own = small_call(layer_kernel, [(8, LANES)] * 4, "layers", force, came, stiff)
     return small_call(
         final_kernel, [(3, LANES)], "total", own, ring(y, "gy"), ring_2(xy), ring(x, "gx")
     )[0]

time: 33.9 us -> 33.5 us (0.988)
  starting transfers between devices: 16.7 us -> 14.7 us
  waiting for transfers between devices: 9.02 us -> 10.7 us
    ppermute x1, starting transfers between devices: 2.97 us -> 0.06 us  [turned_ring(): return lax.ppermute(value, ('gx', 'gy', 'gz'), route)]
    ppermute x1, waiting for transfers between devices: 1.92 us -> 3.85 us  [turned_ring(): return lax.ppermute(value, ('gx', 'gy', 'gz'), route)]
    ppermute x10, starting transfers between devices: 13.2 us -> 14 us  [ring(): lax.ppermute(value, axes, [(i, (i + distance) % count) for i in range(cou...]
  transfers between devices with their start and end apart: 13 -> 13, of which waited for: 8 -> 7; matrix products, arithmetic and copies ran while one was open for 0% -> 0% of each run, Pallas kernels for 17% -> 17%
where the time goes in v7:
time: 33.5 us; the launch traced here: 33.3 us
  starting transfers between devices  14.7 us (44%)
  waiting for transfers between devices  10.7 us (32%)
  Pallas kernels  7.27 us (22%)
  local copies, waits for them, and re-layouts  0.5 us (1%)
    ppermute x10, starting transfers between devices, ring(): lax.ppermute(value, axes, [(i, (i + distance) % count) for i in range(cou...  14 us
    ppermute x10, waiting for transfers between devices, ring(): lax.ppermute(value, axes, [(i, (i + distance) % count) for i in range(cou...  6.84 us
    pallas_call x4, Pallas kernels, sample_call(): pl.pallas_call(kernel, out_shape=jax.ShapeDtypeStruct((LANES, 512), jnp.b...  4.52 us
    ppermute x1, waiting for transfers between devices, turned_ring(): return lax.ppermute(value, ('gx', 'gy', 'gz'), route)  3.85 us
    pallas_call x9, Pallas kernels, vmem_call(): pl.pallas_call(kernel, out_shape=[jax.ShapeDtypeStruct(shape, dtype) for...  2.75 us
  transfers between devices with their start and end apart: 13, of which 7 were waited for; matrix products, arithmetic and copies ran while one was open for 0% of the time, Pallas kernels for 17%

profile of v7, /device:TPU:0, one launch (start us, length us, event | category | flops | bytes accessed | tf_op | source)
XLA Modules:
  0.0 33.3 jit_solution(5002254953265705438)
XLA Ops:
  0.0 0.5 %collective-permute-start.2 = (bf16[128,4096]{1,0:T(8,128)(2,1)}, bf16[128,4096]{1,0:T(8,128)(2,1)S(1)}, u32[]{:S(2)}, u32[]{:S(2)}) collective-permute-start(bf16[128,4096]{1,0:T(8,128)(2,1)} %refs_0_.1), channel_id=1, source_target_pairs={{0,1},{1,0},{2,3},{3,2},{4,5},{5,4},{6,7},{7,6},{8,9},{9,8},{10,11... | collective-permute-start | bytes 3145736 | tf_op jit(solution)/shard_map/ppermute | solution.py:442
  0.5 0.0 copy-start.3
  0.5 0.0 copy-start
  0.5 0.1 collective-permute-start.1
  0.6 0.2 shapes.1.after_ref.shape_ref
  0.8 0.3 copy-done.3
  1.1 0.0 copy-done.4
  1.2 0.0 copy-done.5
  1.2 0.0 copy-done.6
  1.2 2.8 %collective-permute-start = (f32[32,128]{1,0:T(8,128)S(1)}, f32[32,128]{1,0:T(8,128)S(1)}, u32[]{:S(2)}, u32[]{:S(2)}) collective-permute-start(f32[32,128]{1,0:T(8,128)S(1)} %pack.1.after_ref.refs_0_.meta_ref), channel_id=1, source_target_pairs={{0,2},{2,4},{4,6},{6,0},{1,3},{3,5},{5,7},{7,1},{8,10},{10,12},{12... | collective-permute-start | bytes 49160 | tf_op jit(solution)/shard_map/ppermute | solution.py:419
  4.0 2.6 %collective-permute-start.5 = (f32[32,128]{1,0:T(8,128)S(1)}, f32[32,128]{1,0:T(8,128)S(1)}, u32[]{:S(2)}, u32[]{:S(2)}) collective-permute-start(f32[32,128]{1,0:T(8,128)S(1)} %pack.1.after_ref.refs_0_.meta_ref), channel_id=1, source_target_pairs={{0,4},{2,6},{4,0},{6,2},{1,5},{3,7},{5,1},{7,3},{8,12},{10,14},{12... | collective-permute-start | bytes 49160 | tf_op jit(solution)/shard_map/ppermute | solution.py:419
  6.6 1.3 %collective-permute-start.4 = (f32[32,128]{1,0:T(8,128)S(1)}, f32[32,128]{1,0:T(8,128)S(1)}, u32[]{:S(2)}, u32[]{:S(2)}) collective-permute-start(f32[32,128]{1,0:T(8,128)S(1)} %pack.1.after_ref.refs_0_.meta_ref), channel_id=1, source_target_pairs={{0,6},{2,0},{4,2},{6,4},{1,7},{3,1},{5,3},{7,5},{8,14},{10,8},{12,... | collective-permute-start | bytes 49160 | tf_op jit(solution)/shard_map/ppermute | solution.py:419
  7.9 0.1 copy.10.slot_ref
  8.0 0.0 collective-permute-done.1.later_ref.mate_ref
  8.0 0.0 collective-permute-done.2.refs_1_
  8.0 0.0 copy-done
  8.1 0.6 %table.1.table_ref = bf16[4096,256]{1,0:T(8,128)(2,1)S(1)} custom-call(f32[32,128]{1,0:T(8,128)S(1)} %pack.1.after_ref.refs_0_.meta_ref, s32[4,128]{1,0:T(4,128)S(1)} %collective-permute-done.1.later_ref.mate_ref, bf16[128,4096]{1,0:T(8,128)(2,1)S(1)} %copy-done, bf16[128,4096]{1,0:T(8,128)(2,1)S(1)} %collective-permute-done.2.refs_1_), custom_call_target="tpu_custom_call" | custom-call | flops 805306368 | bytes 1048576 | tf_op jit(solution)/shard_map/table/pallas_call | solution.py:78
  8.7 0.0 collective-permute-done.meta_ref.refs_3_
  8.7 0.0 copy-done.7
  8.7 1.1 %interpolate.4.rest_0_ = bf16[128,512]{1,0:T(8,128)(2,1)S(1)} custom-call(f32[32,128]{1,0:T(8,128)S(1)} %collective-permute-done.meta_ref.refs_3_, bf16[4096,256]{1,0:T(8,128)(2,1)S(1)} %table.1.table_ref, s32[4,128]{1,0:T(4,128)S(1)} %bitcast.6, s32[4,128]{1,0:T(4,128)S(1)} %collective-permute-done.1.later_ref.mate_ref), custom_call_target="tpu_custom_call" | custom-call | flops 4000000000 | bytes 1 | tf_op jit(solution)/shard_map/interpolate/pallas_call | solution.py:165
  9.8 1.1 %collective-permute-start.3 = (bf16[128,512]{1,0:T(8,128)(2,1)S(1)}, bf16[128,512]{1,0:T(8,128)(2,1)S(1)}, u32[]{:S(2)}, u32[]{:S(2)}) collective-permute-start(bf16[128,512]{1,0:T(8,128)(2,1)S(1)} %interpolate.4.rest_0_), channel_id=1, source_target_pairs={{0,6},{2,0},{4,2},{6,4},{1,7},{3,1},{5,3},{7,5},{8,14},{10,8},{12,... | collective-permute-start | bytes 393224 | tf_op jit(solution)/shard_map/ppermute | solution.py:419
  10.9 0.0 collective-permute-done.5.refs_2_.meta_ref
  10.9 1.1 %interpolate.5.rest_0_ = bf16[128,512]{1,0:T(8,128)(2,1)S(1)} custom-call(f32[32,128]{1,0:T(8,128)S(1)} %collective-permute-done.5.refs_2_.meta_ref, bf16[4096,256]{1,0:T(8,128)(2,1)S(1)} %table.1.table_ref, s32[4,128]{1,0:T(4,128)S(1)} %bitcast.7, s32[4,128]{1,0:T(4,128)S(1)} %collective-permute-done.1.later_ref.mate_ref, ...), custom_call_target="tpu_custom_call" | custom-call | flops 4000000000 | bytes 1 | tf_op jit(solution)/shard_map/interpolate/pallas_call | solution.py:165
  12.1 1.2 %collective-permute-start.7 = (bf16[128,512]{1,0:T(8,128)(2,1)S(1)}, bf16[128,512]{1,0:T(8,128)(2,1)S(1)}, u32[]{:S(2)}, u32[]{:S(2)}) collective-permute-start(bf16[128,512]{1,0:T(8,128)(2,1)S(1)} %interpolate.5.rest_0_), channel_id=1, source_target_pairs={{0,4},{2,6},{4,0},{6,2},{1,5},{3,7},{5,1},{7,3},{8,12},{10,14},{12... | collective-permute-start | bytes 393224 | tf_op jit(solution)/shard_map/ppermute | solution.py:419
  13.2 0.0 collective-permute-done.4.refs_1_.meta_ref
  13.2 1.1 %interpolate.6.rest_0_ = bf16[128,512]{1,0:T(8,128)(2,1)S(1)} custom-call(f32[32,128]{1,0:T(8,128)S(1)} %collective-permute-done.4.refs_1_.meta_ref, bf16[4096,256]{1,0:T(8,128)(2,1)S(1)} %table.1.table_ref, s32[4,128]{1,0:T(4,128)S(1)} %bitcast.8, s32[4,128]{1,0:T(4,128)S(1)} %collective-permute-done.1.later_ref.mate_ref, ...), custom_call_target="tpu_custom_call" | custom-call | flops 4000000000 | bytes 1 | tf_op jit(solution)/shard_map/interpolate/pallas_call | solution.py:165
  14.4 0.1 collective-permute-start.8
  14.5 0.7 %collective-permute-done.3.after_ref.rest_1_ = bf16[128,512]{1,0:T(8,128)(2,1)S(1)} collective-permute-done((bf16[128,512]{1,0:T(8,128)(2,1)S(1)}, bf16[128,512]{1,0:T(8,128)(2,1)S(1)}, u32[]{:S(2)}, u32[]{:S(2)}) %collective-permute-start.3) | collective-permute-done | bytes 131104 | tf_op jit(solution)/shard_map/ppermute | solution.py:419
  15.2 2.5 %collective-permute-start.6 = (f32[4,8,128]{2,1,0:T(8,128)S(1)}, f32[4,8,128]{2,1,0:T(8,128)S(1)}, u32[]{:S(2)}, u32[]{:S(2)}) collective-permute-start(f32[4,8,128]{2,1,0:T(8,128)S(1)} %collect.1.own_ref), channel_id=1, source_target_pairs={{0,24},{8,0},{16,8},{24,16},{1,25},{9,1},{17,9},{25,17},{2,26},{10... | collective-permute-start | bytes 49160 | tf_op jit(solution)/shard_map/ppermute | solution.py:419
  17.7 1.1 %interpolate.7.rest_0_ = bf16[128,512]{1,0:T(8,128)(2,1)S(1)} custom-call(f32[32,128]{1,0:T(8,128)S(1)} %pack.1.after_ref.refs_0_.meta_ref, bf16[4096,256]{1,0:T(8,128)(2,1)S(1)} %table.1.table_ref, s32[4,128]{1,0:T(4,128)S(1)} %bitcast.9, s32[4,128]{1,0:T(4,128)S(1)} %collective-permute-done.1.later_ref.mate_ref, bf16[128,512]{1,0:T(8,128)(2,1)S(1)} %interpolate.6.rest_0_), custom_call_target="tpu_custom_call" | custom-call | flops 4000000000 | bytes 1 | tf_op jit(solution)/shard_map/interpolate/pallas_call | solution.py:165
  18.8 0.0 copy-done.2
  18.8 0.2 early.1.base_ref
  19.1 0.1 collective-permute-done.6.above_ref
  19.1 0.2 stiffness.1
  19.3 1.9 %collective-permute-done.8.rest_1_ = bf16[128,512]{1,0:T(8,128)(2,1)S(1)} collective-permute-done((bf16[128,512]{1,0:T(8,128)(2,1)S(1)}, bf16[128,512]{1,0:T(8,128)(2,1)S(1)}, u32[]{:S(2)}, u32[]{:S(2)}) %collective-permute-start.8) | collective-permute-done | bytes 131104 | tf_op jit(solution)/shard_map/ppermute | solution.py:419
  21.2 2.2 %collective-permute-done.7.rest_0_ = bf16[128,512]{1,0:T(8,128)(2,1)S(1)} collective-permute-done((bf16[128,512]{1,0:T(8,128)(2,1)S(1)}, bf16[128,512]{1,0:T(8,128)(2,1)S(1)}, u32[]{:S(2)}, u32[]{:S(2)}) %collective-permute-start.7) | collective-permute-done | bytes 131104 | tf_op jit(solution)/shard_map/ppermute | solution.py:419
  23.4 0.0 copy-done.1
  23.4 0.8 %forces.1.here_ref = f32[48,128]{1,0:T(8,128)S(1)} custom-call(f32[8,128]{1,0:T(8,128)S(1)} %get-tuple-element.10.across_ref, s32[128,1]{1,0:T(8,128)S(1)} %copy.10.slot_ref, f32[128,512]{1,0:T(8,128)S(1)} %early.1.base_ref, bf16[3,128,512]{2,1,0:T(8,128)(2,1)S(1)} %copy-done.1, bf16[512,128]{1,0:T(8,128)(2,1)S(1)} %shapes.1.after_ref.shape_ref, ...), custom_call_target="tpu_custom_call" | custom-call | flops 1048576 | bytes 1048576 | tf_op jit(solution)/shard_map/forces/pallas_call | solution.py:78
  24.2 0.1 collective-permute-start.9
  24.2 1.2 %collective-permute-done.9.mate_ref = f32[48,128]{1,0:T(8,128)S(1)} collective-permute-done((f32[48,128]{1,0:T(8,128)S(1)}, f32[48,128]{1,0:T(8,128)S(1)}, u32[]{:S(2)}, u32[]{:S(2)}) %collective-permute-start.9) | collective-permute-done | bytes 24608 | tf_op jit(solution)/shard_map/ppermute | solution.py:419
  25.4 0.2 layers.1
  25.6 0.1 collective-permute-start.10
  25.7 1.5 %collective-permute-start.12 = (f32[8,128]{1,0:T(8,128)S(1)}, f32[8,128]{1,0:T(8,128)S(1)}, u32[]{:S(2)}, u32[]{:S(2)}) collective-permute-start(f32[8,128]{1,0:T(8,128)S(1)} %get-tuple-element.14), channel_id=1, source_target_pairs={{0,8},{8,16},{16,24},{24,0},{1,9},{9,17},{17,25},{25,1},{2,10},{10... | collective-permute-start | bytes 12296 | tf_op jit(solution)/shard_map/ppermute | solution.py:419
  27.2 3.9 %collective-permute-done.10.turned_ref = f32[8,128]{1,0:T(8,128)S(1)} collective-permute-done((f32[8,128]{1,0:T(8,128)S(1)}, f32[8,128]{1,0:T(8,128)S(1)}, u32[]{:S(2)}, u32[]{:S(2)}) %collective-permute-start.10) | collective-permute-done | bytes 4128 | tf_op jit(solution)/shard_map/ppermute | solution.py:438
  31.1 0.8 %collective-permute-start.11 = (f32[8,128]{1,0:T(8,128)S(1)}, f32[8,128]{1,0:T(8,128)S(1)}, u32[]{:S(2)}, u32[]{:S(2)}) collective-permute-start(f32[8,128]{1,0:T(8,128)S(1)} %collective-permute-done.10.turned_ref), channel_id=1, source_target_pairs={{0,1},{1,0},{2,3},{3,2},{4,5},{5,4},{6,7},{7,6},{8,9},{9,8},{10,11... | collective-permute-start | bytes 12296 | tf_op jit(solution)/shard_map/ppermute | solution.py:419
  31.9 0.0 collective-permute-done.12.x_ref
  31.9 0.8 %collective-permute-done.11.mate_ref = f32[8,128]{1,0:T(8,128)S(1)} collective-permute-done((f32[8,128]{1,0:T(8,128)S(1)}, f32[8,128]{1,0:T(8,128)S(1)}, u32[]{:S(2)}, u32[]{:S(2)}) %collective-permute-start.11) | collective-permute-done | bytes 4128 | tf_op jit(solution)/shard_map/ppermute | solution.py:419
  32.7 0.6 %total.1 = f32[3,128]{1,0:T(4,128)} custom-call(f32[8,128]{1,0:T(8,128)S(1)} %get-tuple-element.12.own_ref, f32[8,128]{1,0:T(8,128)S(1)} %collective-permute-done.10.turned_ref, f32[8,128]{1,0:T(8,128)S(1)} %collective-permute-done.11.mate_ref, f32[8,128]{1,0:T(8,128)S(1)} %collective-permute-done.12.x_ref), custom_call_target="tpu_custom_call" | custom-call | flops 1048576 | bytes 1048576 | tf_op jit(solution)/shard_map/total/pallas_call | solution.py:78
  (8 shorter events, 0.0 us)
Async XLA Ops:
  0.0 8.0 %collective-permute-start.2 = (bf16[128,4096]{1,0:T(8,128)(2,1)}, bf16[128,4096]{1,0:T(8,128)(2,1)S(1)}, u32[]{:S(2)}, u32[]{:S(2)}) collective-permute-start(bf16[128,4096]{1,0:T(8,128)(2,1)} %refs_0_.1), channel_id=1, source_target_pairs={{0,1},{1,0},{2,3},{3,2},{4,5},{5,4},{6,7},{7,6},{8,9},{9,8},{10,11... | collective-permute-start | bytes 3145736 | tf_op jit(solution)/shard_map/ppermute | solution.py:442
  0.5 0.7 %copy-start.3 = (bf16[24,128]{1,0:T(8,128)(2,1)S(1)}, bf16[24,128]{1,0:T(8,128)(2,1)}, u32[]{:S(2)}) copy-start(bf16[24,128]{1,0:T(8,128)(2,1)} %fraction_ref.1) | copy-start | bytes 18436
  0.5 0.7 %copy-start.4 = (f32[3,128]{1,0:T(4,128)S(1)}, f32[3,128]{1,0:T(4,128)}, u32[]{:S(2)}) copy-start(f32[3,128]{1,0:T(4,128)} %displacement_ref.1) | copy-start | bytes 4612
  0.5 0.7 %copy-start.5 = (s32[3,128]{1,0:T(4,128)S(1)}, s32[3,128]{1,0:T(4,128)}, u32[]{:S(2)}) copy-start(s32[3,128]{1,0:T(4,128)} %offset_ref.1) | copy-start | bytes 4612
  0.5 0.7 %copy-start.6 = (s32[128]{0:T(128)S(1)}, s32[128]{0:T(128)}, u32[]{:S(2)}) copy-start(s32[128]{0:T(128)} %param.15) | copy-start | bytes 1540
  0.5 7.6 %copy-start = (bf16[128,4096]{1,0:T(8,128)(2,1)S(1)}, bf16[128,4096]{1,0:T(8,128)(2,1)}, u32[]{:S(2)}) copy-start(bf16[128,4096]{1,0:T(8,128)(2,1)} %refs_0_.1) | copy-start | bytes 3145732
  0.5 7.6 %collective-permute-start.1 = (s32[4,128]{1,0:T(4,128)}, s32[4,128]{1,0:T(4,128)S(1)}, u32[]{:S(2)}, u32[]{:S(2)}) collective-permute-start(s32[4,128]{1,0:T(4,128)} %bitcast.5), channel_id=1, source_target_pairs={{0,1},{1,0},{2,3},{3,2},{4,5},{5,4},{6,7},{7,6},{8,9},{9,8},{10,11... | collective-permute-start | bytes 6152 | tf_op jit(solution)/shard_map/ppermute | solution.py:442
  1.2 7.5 %collective-permute-start = (f32[32,128]{1,0:T(8,128)S(1)}, f32[32,128]{1,0:T(8,128)S(1)}, u32[]{:S(2)}, u32[]{:S(2)}) collective-permute-start(f32[32,128]{1,0:T(8,128)S(1)} %pack.1.after_ref.refs_0_.meta_ref), channel_id=1, source_target_pairs={{0,2},{2,4},{4,6},{6,0},{1,3},{3,5},{5,7},{7,1},{8,10},{10,12},{12... | collective-permute-start | bytes 49160 | tf_op jit(solution)/shard_map/ppermute | solution.py:419
  4.0 7.0 %collective-permute-start.5 = (f32[32,128]{1,0:T(8,128)S(1)}, f32[32,128]{1,0:T(8,128)S(1)}, u32[]{:S(2)}, u32[]{:S(2)}) collective-permute-start(f32[32,128]{1,0:T(8,128)S(1)} %pack.1.after_ref.refs_0_.meta_ref), channel_id=1, source_target_pairs={{0,4},{2,6},{4,0},{6,2},{1,5},{3,7},{5,1},{7,3},{8,12},{10,14},{12... | collective-permute-start | bytes 49160 | tf_op jit(solution)/shard_map/ppermute | solution.py:419
  6.6 6.7 %collective-permute-start.4 = (f32[32,128]{1,0:T(8,128)S(1)}, f32[32,128]{1,0:T(8,128)S(1)}, u32[]{:S(2)}, u32[]{:S(2)}) collective-permute-start(f32[32,128]{1,0:T(8,128)S(1)} %pack.1.after_ref.refs_0_.meta_ref), channel_id=1, source_target_pairs={{0,6},{2,0},{4,2},{6,4},{1,7},{3,1},{5,3},{7,5},{8,14},{10,8},{12,... | collective-permute-start | bytes 49160 | tf_op jit(solution)/shard_map/ppermute | solution.py:419
  8.0 0.7 %copy-start.7 = (s32[512]{0:T(512)S(1)}, s32[512]{0:T(512)}, u32[]{:S(2)}) copy-start(s32[512]{0:T(512)} %param.14) | copy-start | bytes 6148
  9.8 5.4 %collective-permute-start.3 = (bf16[128,512]{1,0:T(8,128)(2,1)S(1)}, bf16[128,512]{1,0:T(8,128)(2,1)S(1)}, u32[]{:S(2)}, u32[]{:S(2)}) collective-permute-start(bf16[128,512]{1,0:T(8,128)(2,1)S(1)} %interpolate.4.rest_0_), channel_id=1, source_target_pairs={{0,6},{2,0},{4,2},{6,4},{1,7},{3,1},{5,3},{7,5},{8,14},{10,8},{12,... | collective-permute-start | bytes 393224 | tf_op jit(solution)/shard_map/ppermute | solution.py:419
  12.1 11.3 %collective-permute-start.7 = (bf16[128,512]{1,0:T(8,128)(2,1)S(1)}, bf16[128,512]{1,0:T(8,128)(2,1)S(1)}, u32[]{:S(2)}, u32[]{:S(2)}) collective-permute-start(bf16[128,512]{1,0:T(8,128)(2,1)S(1)} %interpolate.5.rest_0_), channel_id=1, source_target_pairs={{0,4},{2,6},{4,0},{6,2},{1,5},{3,7},{5,1},{7,3},{8,12},{10,14},{12... | collective-permute-start | bytes 393224 | tf_op jit(solution)/shard_map/ppermute | solution.py:419
  14.4 6.8 %collective-permute-start.8 = (bf16[128,512]{1,0:T(8,128)(2,1)S(1)}, bf16[128,512]{1,0:T(8,128)(2,1)S(1)}, u32[]{:S(2)}, u32[]{:S(2)}) collective-permute-start(bf16[128,512]{1,0:T(8,128)(2,1)S(1)} %interpolate.6.rest_0_), channel_id=1, source_target_pairs={{0,2},{2,4},{4,6},{6,0},{1,3},{3,5},{5,7},{7,1},{8,10},{10,12},{12... | collective-permute-start | bytes 393224 | tf_op jit(solution)/shard_map/ppermute | solution.py:419
  15.2 3.6 %copy-start.2 = (bf16[128,512]{1,0:T(8,128)(2,1)S(1)}, bf16[128,512]{1,0:T(8,128)(2,1)}, u32[]{:S(2)}) copy-start(bf16[128,512]{1,0:T(8,128)(2,1)} %image_ref.1) | copy-start | bytes 393220
  15.2 8.2 %copy-start.1 = (bf16[3,128,512]{2,1,0:T(8,128)(2,1)S(1)}, bf16[3,128,512]{2,1,0:T(8,128)(2,1)}, u32[]{:S(2)}) copy-start(bf16[3,128,512]{2,1,0:T(8,128)(2,1)} %slope_ref.1) | copy-start | bytes 1179652
  15.2 3.9 %collective-permute-start.6 = (f32[4,8,128]{2,1,0:T(8,128)S(1)}, f32[4,8,128]{2,1,0:T(8,128)S(1)}, u32[]{:S(2)}, u32[]{:S(2)}) collective-permute-start(f32[4,8,128]{2,1,0:T(8,128)S(1)} %collect.1.own_ref), channel_id=1, source_target_pairs={{0,24},{8,0},{16,8},{24,16},{1,25},{9,1},{17,9},{25,17},{2,26},{10... | collective-permute-start | bytes 49160 | tf_op jit(solution)/shard_map/ppermute | solution.py:419
  24.2 1.3 %collective-permute-start.9 = (f32[48,128]{1,0:T(8,128)S(1)}, f32[48,128]{1,0:T(8,128)S(1)}, u32[]{:S(2)}, u32[]{:S(2)}) collective-permute-start(f32[48,128]{1,0:T(8,128)S(1)} %forces.1.here_ref), channel_id=1, source_target_pairs={{0,1},{1,0},{2,3},{3,2},{4,5},{5,4},{6,7},{7,6},{8,9},{9,8},{10,11... | collective-permute-start | bytes 73736 | tf_op jit(solution)/shard_map/ppermute | solution.py:419
  25.6 5.5 %collective-permute-start.10 = (f32[8,128]{1,0:T(8,128)S(1)}, f32[8,128]{1,0:T(8,128)S(1)}, u32[]{:S(2)}, u32[]{:S(2)}) collective-permute-start(f32[8,128]{1,0:T(8,128)S(1)} %get-tuple-element.13), channel_id=1, source_target_pairs={{0,2},{1,11},{2,4},{3,13},{4,6},{5,15},{6,0},{7,9},{8,10},{9,19},{... | collective-permute-start | bytes 12296 | tf_op jit(solution)/shard_map/ppermute | solution.py:438
  25.7 6.2 %collective-permute-start.12 = (f32[8,128]{1,0:T(8,128)S(1)}, f32[8,128]{1,0:T(8,128)S(1)}, u32[]{:S(2)}, u32[]{:S(2)}) collective-permute-start(f32[8,128]{1,0:T(8,128)S(1)} %get-tuple-element.14), channel_id=1, source_target_pairs={{0,8},{8,16},{16,24},{24,0},{1,9},{9,17},{17,25},{25,1},{2,10},{10... | collective-permute-start | bytes 12296 | tf_op jit(solution)/shard_map/ppermute | solution.py:419
  31.1 1.6 %collective-permute-start.11 = (f32[8,128]{1,0:T(8,128)S(1)}, f32[8,128]{1,0:T(8,128)S(1)}, u32[]{:S(2)}, u32[]{:S(2)}) collective-permute-start(f32[8,128]{1,0:T(8,128)S(1)} %collective-permute-done.10.turned_ref), channel_id=1, source_target_pairs={{0,1},{1,0},{2,3},{3,2},{4,5},{5,4},{6,7},{7,6},{8,9},{9,8},{10,11... | collective-permute-start | bytes 12296 | tf_op jit(solution)/shard_map/ppermute | solution.py:419

commit v8 on v7

--- a/solution.py
+++ b/solution.py
@@ -429,13 +429,27 @@
 
 def turned_ring(value):
     nx, ny = lax.axis_size("gx"), lax.axis_size("gy")
-    route = [
-        ((x * ny + y) * 2 + core, ((x + core) % nx * ny + (y + 1) % ny) * 2 + core)
+    place = {
+        (x * ny + y) * 2 + core: (x, y, core)
         for x in range(nx)
         for y in range(ny)
         for core in range(2)
-    ]
-    return lax.ppermute(value, ("gx", "gy", "gz"), route)
+    }
+    number = {where: i for i, where in place.items()}
+    route = [(i, number.get((x + core, y + 1, core))) for i, (x, y, core) in place.items()]
+    route = [pair for pair in route if pair[1] is not None]
+
+    def from_order(i):
+        x, y, core = place[i]
+        return y, -core, x > 0, -x
+
+    def to_order(i):
+        x, y, core = place[i]
+        return x > 0, y, -core if x else core, -x
+
+    sources = sorted(set(place) - {pair[0] for pair in route}, key=from_order)
+    targets = sorted(set(place) - {pair[1] for pair in route}, key=to_order)
+    return lax.ppermute(value, ("gx", "gy", "gz"), route + list(zip(sources, targets)))
 
 
 def swapped(value, axes, mask):

time: 33.5 us -> 32.5 us (0.970)
  the two profiles are of different devices: /device:TPU:0 before, /device:TPU:5 now
where the time goes in v8:
time: 32.5 us; the launch traced here: 32.3 us
  waiting for transfers between devices  13.2 us (41%)
  starting transfers between devices  11.2 us (34%)
  Pallas kernels  7.25 us (22%)
  local copies, waits for them, and re-layouts  0.54 us (2%)
    ppermute x10, starting transfers between devices, ring(): lax.ppermute(value, axes, [(i, (i + distance) % count) for i in range(cou...  10.1 us
    ppermute x10, waiting for transfers between devices, ring(): lax.ppermute(value, axes, [(i, (i + distance) % count) for i in range(cou...  8.84 us
    pallas_call x4, Pallas kernels, sample_call(): pl.pallas_call(kernel, out_shape=jax.ShapeDtypeStruct((LANES, 512), jnp.b...  4.5 us
    ppermute x1, waiting for transfers between devices, turned_ring(): lax.ppermute(value, ('gx', 'gy', 'gz'), route + list(zip(sources, targets)))  4.39 us
    pallas_call x9, Pallas kernels, vmem_call(): pl.pallas_call(kernel, out_shape=[jax.ShapeDtypeStruct(shape, dtype) for...  2.75 us
    ppermute x2, starting transfers between devices, swapped(): lax.ppermute(value, axes, [(i, i ^ mask) for i in range(lax.axis_size(axe...  0.76 us
  transfers between devices with their start and end apart: 13, of which 6 were waited for; matrix products, arithmetic and copies ran while one was open for 0% of the time, Pallas kernels for 18%

profile of v8, /device:TPU:5, one launch (start us, length us, event | category | flops | bytes accessed | tf_op | source)
XLA Modules:
  0.0 32.3 jit_solution(18146863235292229333)
XLA Ops:
  0.0 0.7 %collective-permute-start.2 = (bf16[128,4096]{1,0:T(8,128)(2,1)}, bf16[128,4096]{1,0:T(8,128)(2,1)S(1)}, u32[]{:S(2)}, u32[]{:S(2)}) collective-permute-start(bf16[128,4096]{1,0:T(8,128)(2,1)} %refs_0_.1), channel_id=1, source_target_pairs={{0,1},{1,0},{2,3},{3,2},{4,5},{5,4},{6,7},{7,6},{8,9},{9,8},{10,11... | collective-permute-start | bytes 3145736 | tf_op jit(solution)/shard_map/ppermute | solution.py:456
  0.7 0.0 copy-start
  0.7 0.1 collective-permute-start.1
  0.8 0.2 shapes.1.after_ref.shape_ref
  1.0 0.3 %copy-done.3 = bf16[24,128]{1,0:T(8,128)(2,1)S(1)} copy-done((bf16[24,128]{1,0:T(8,128)(2,1)S(1)}, bf16[24,128]{1,0:T(8,128)(2,1)}, u32[]{:S(2)}) %copy-start.3) | copy-done | bytes 6168
  1.4 0.0 copy-done.4
  1.4 0.0 copy-done.5
  1.4 0.0 copy-done.6
  1.4 1.3 %collective-permute-start = (f32[32,128]{1,0:T(8,128)S(1)}, f32[32,128]{1,0:T(8,128)S(1)}, u32[]{:S(2)}, u32[]{:S(2)}) collective-permute-start(f32[32,128]{1,0:T(8,128)S(1)} %pack.1.after_ref.refs_0_.meta_ref), channel_id=1, source_target_pairs={{0,2},{2,4},{4,6},{6,0},{1,3},{3,5},{5,7},{7,1},{8,10},{10,12},{12... | collective-permute-start | bytes 49160 | tf_op jit(solution)/shard_map/ppermute | solution.py:419
  2.7 2.3 %collective-permute-start.5 = (f32[32,128]{1,0:T(8,128)S(1)}, f32[32,128]{1,0:T(8,128)S(1)}, u32[]{:S(2)}, u32[]{:S(2)}) collective-permute-start(f32[32,128]{1,0:T(8,128)S(1)} %pack.1.after_ref.refs_0_.meta_ref), channel_id=1, source_target_pairs={{0,4},{2,6},{4,0},{6,2},{1,5},{3,7},{5,1},{7,3},{8,12},{10,14},{12... | collective-permute-start | bytes 49160 | tf_op jit(solution)/shard_map/ppermute | solution.py:419
  5.1 1.1 %collective-permute-start.4 = (f32[32,128]{1,0:T(8,128)S(1)}, f32[32,128]{1,0:T(8,128)S(1)}, u32[]{:S(2)}, u32[]{:S(2)}) collective-permute-start(f32[32,128]{1,0:T(8,128)S(1)} %pack.1.after_ref.refs_0_.meta_ref), channel_id=1, source_target_pairs={{0,6},{2,0},{4,2},{6,4},{1,7},{3,1},{5,3},{7,5},{8,14},{10,8},{12,... | collective-permute-start | bytes 49160 | tf_op jit(solution)/shard_map/ppermute | solution.py:419
  6.1 0.1 copy.10.slot_ref
  6.2 0.0 collective-permute-done.1.later_ref.mate_ref
  6.2 0.0 collective-permute-done.2.refs_1_
  6.3 0.0 copy-done
  6.3 0.6 %table.1.table_ref = bf16[4096,256]{1,0:T(8,128)(2,1)S(1)} custom-call(f32[32,128]{1,0:T(8,128)S(1)} %pack.1.after_ref.refs_0_.meta_ref, s32[4,128]{1,0:T(4,128)S(1)} %collective-permute-done.1.later_ref.mate_ref, bf16[128,4096]{1,0:T(8,128)(2,1)S(1)} %copy-done, bf16[128,4096]{1,0:T(8,128)(2,1)S(1)} %collective-permute-done.2.refs_1_), custom_call_target="tpu_custom_call" | custom-call | flops 805306368 | bytes 1048576 | tf_op jit(solution)/shard_map/table/pallas_call | solution.py:78
  6.9 0.0 collective-permute-done.meta_ref.refs_3_
  6.9 0.0 copy-done.7
  6.9 1.1 %interpolate.4.rest_0_ = bf16[128,512]{1,0:T(8,128)(2,1)S(1)} custom-call(f32[32,128]{1,0:T(8,128)S(1)} %collective-permute-done.meta_ref.refs_3_, bf16[4096,256]{1,0:T(8,128)(2,1)S(1)} %table.1.table_ref, s32[4,128]{1,0:T(4,128)S(1)} %bitcast.6, s32[4,128]{1,0:T(4,128)S(1)} %collective-permute-done.1.later_ref.mate_ref), custom_call_target="tpu_custom_call" | custom-call | flops 4000000000 | bytes 1 | tf_op jit(solution)/shard_map/interpolate/pallas_call | solution.py:165
  8.0 0.5 %collective-permute-start.3 = (bf16[128,512]{1,0:T(8,128)(2,1)S(1)}, bf16[128,512]{1,0:T(8,128)(2,1)S(1)}, u32[]{:S(2)}, u32[]{:S(2)}) collective-permute-start(bf16[128,512]{1,0:T(8,128)(2,1)S(1)} %interpolate.4.rest_0_), channel_id=1, source_target_pairs={{0,6},{2,0},{4,2},{6,4},{1,7},{3,1},{5,3},{7,5},{8,14},{10,8},{12,... | collective-permute-start | bytes 393224 | tf_op jit(solution)/shard_map/ppermute | solution.py:419
  8.5 0.0 collective-permute-done.5.refs_2_.meta_ref
  8.5 1.1 %interpolate.5.rest_0_ = bf16[128,512]{1,0:T(8,128)(2,1)S(1)} custom-call(f32[32,128]{1,0:T(8,128)S(1)} %collective-permute-done.5.refs_2_.meta_ref, bf16[4096,256]{1,0:T(8,128)(2,1)S(1)} %table.1.table_ref, s32[4,128]{1,0:T(4,128)S(1)} %bitcast.7, s32[4,128]{1,0:T(4,128)S(1)} %collective-permute-done.1.later_ref.mate_ref, ...), custom_call_target="tpu_custom_call" | custom-call | flops 4000000000 | bytes 1 | tf_op jit(solution)/shard_map/interpolate/pallas_call | solution.py:165
  9.7 1.2 %collective-permute-start.7 = (bf16[128,512]{1,0:T(8,128)(2,1)S(1)}, bf16[128,512]{1,0:T(8,128)(2,1)S(1)}, u32[]{:S(2)}, u32[]{:S(2)}) collective-permute-start(bf16[128,512]{1,0:T(8,128)(2,1)S(1)} %interpolate.5.rest_0_), channel_id=1, source_target_pairs={{0,4},{2,6},{4,0},{6,2},{1,5},{3,7},{5,1},{7,3},{8,12},{10,14},{12... | collective-permute-start | bytes 393224 | tf_op jit(solution)/shard_map/ppermute | solution.py:419
  10.9 0.0 collective-permute-done.4.refs_1_.meta_ref
  10.9 1.1 %interpolate.6.rest_0_ = bf16[128,512]{1,0:T(8,128)(2,1)S(1)} custom-call(f32[32,128]{1,0:T(8,128)S(1)} %collective-permute-done.4.refs_1_.meta_ref, bf16[4096,256]{1,0:T(8,128)(2,1)S(1)} %table.1.table_ref, s32[4,128]{1,0:T(4,128)S(1)} %bitcast.8, s32[4,128]{1,0:T(4,128)S(1)} %collective-permute-done.1.later_ref.mate_ref, ...), custom_call_target="tpu_custom_call" | custom-call | flops 4000000000 | bytes 1 | tf_op jit(solution)/shard_map/interpolate/pallas_call | solution.py:165
  12.0 0.1 collective-permute-start.8
  12.2 0.0 collective-permute-done.3.after_ref.rest_1_
  12.2 0.0 copy-start.1
  12.2 1.2 %collective-permute-start.6 = (f32[4,8,128]{2,1,0:T(8,128)S(1)}, f32[4,8,128]{2,1,0:T(8,128)S(1)}, u32[]{:S(2)}, u32[]{:S(2)}) collective-permute-start(f32[4,8,128]{2,1,0:T(8,128)S(1)} %collect.1.own_ref), channel_id=1, source_target_pairs={{0,24},{8,0},{16,8},{24,16},{1,25},{9,1},{17,9},{25,17},{2,26},{10... | collective-permute-start | bytes 49160 | tf_op jit(solution)/shard_map/ppermute | solution.py:419
  13.4 1.1 %interpolate.7.rest_0_ = bf16[128,512]{1,0:T(8,128)(2,1)S(1)} custom-call(f32[32,128]{1,0:T(8,128)S(1)} %pack.1.after_ref.refs_0_.meta_ref, bf16[4096,256]{1,0:T(8,128)(2,1)S(1)} %table.1.table_ref, s32[4,128]{1,0:T(4,128)S(1)} %bitcast.9, s32[4,128]{1,0:T(4,128)S(1)} %collective-permute-done.1.later_ref.mate_ref, bf16[128,512]{1,0:T(8,128)(2,1)S(1)} %interpolate.6.rest_0_), custom_call_target="tpu_custom_call" | custom-call | flops 4000000000 | bytes 1 | tf_op jit(solution)/shard_map/interpolate/pallas_call | solution.py:165
  14.5 0.0 copy-done.2
  14.5 0.2 early.1.base_ref
  14.8 0.1 collective-permute-done.6.above_ref
  14.8 0.2 stiffness.1
  15.0 3.4 %collective-permute-done.8.rest_1_ = bf16[128,512]{1,0:T(8,128)(2,1)S(1)} collective-permute-done((bf16[128,512]{1,0:T(8,128)(2,1)S(1)}, bf16[128,512]{1,0:T(8,128)(2,1)S(1)}, u32[]{:S(2)}, u32[]{:S(2)}) %collective-permute-start.8) | collective-permute-done | bytes 131104 | tf_op jit(solution)/shard_map/ppermute | solution.py:419
  18.4 3.4 %collective-permute-done.7.rest_0_ = bf16[128,512]{1,0:T(8,128)(2,1)S(1)} collective-permute-done((bf16[128,512]{1,0:T(8,128)(2,1)S(1)}, bf16[128,512]{1,0:T(8,128)(2,1)S(1)}, u32[]{:S(2)}, u32[]{:S(2)}) %collective-permute-start.7) | collective-permute-done | bytes 131104 | tf_op jit(solution)/shard_map/ppermute | solution.py:419
  21.8 0.0 copy-done.1
  21.8 0.8 %forces.1.here_ref = f32[48,128]{1,0:T(8,128)S(1)} custom-call(f32[8,128]{1,0:T(8,128)S(1)} %get-tuple-element.10.across_ref, s32[128,1]{1,0:T(8,128)S(1)} %copy.10.slot_ref, f32[128,512]{1,0:T(8,128)S(1)} %early.1.base_ref, bf16[3,128,512]{2,1,0:T(8,128)(2,1)S(1)} %copy-done.1, bf16[512,128]{1,0:T(8,128)(2,1)S(1)} %shapes.1.after_ref.shape_ref, ...), custom_call_target="tpu_custom_call" | custom-call | flops 1048576 | bytes 1048576 | tf_op jit(solution)/shard_map/forces/pallas_call | solution.py:78
  22.5 0.9 %collective-permute-start.9 = (f32[48,128]{1,0:T(8,128)S(1)}, f32[48,128]{1,0:T(8,128)S(1)}, u32[]{:S(2)}, u32[]{:S(2)}) collective-permute-start(f32[48,128]{1,0:T(8,128)S(1)} %forces.1.here_ref), channel_id=1, source_target_pairs={{0,1},{1,0},{2,3},{3,2},{4,5},{5,4},{6,7},{7,6},{8,9},{9,8},{10,11... | collective-permute-start | bytes 73736 | tf_op jit(solution)/shard_map/ppermute | solution.py:419
  23.5 0.8 %collective-permute-done.9.mate_ref = f32[48,128]{1,0:T(8,128)S(1)} collective-permute-done((f32[48,128]{1,0:T(8,128)S(1)}, f32[48,128]{1,0:T(8,128)S(1)}, u32[]{:S(2)}, u32[]{:S(2)}) %collective-permute-start.9) | collective-permute-done | bytes 24608 | tf_op jit(solution)/shard_map/ppermute | solution.py:419
  24.3 0.2 layers.1
  24.5 0.3 collective-permute-start.10
  24.8 1.4 %collective-permute-start.12 = (f32[8,128]{1,0:T(8,128)S(1)}, f32[8,128]{1,0:T(8,128)S(1)}, u32[]{:S(2)}, u32[]{:S(2)}) collective-permute-start(f32[8,128]{1,0:T(8,128)S(1)} %get-tuple-element.14), channel_id=1, source_target_pairs={{0,8},{8,16},{16,24},{24,0},{1,9},{9,17},{17,25},{25,1},{2,10},{10... | collective-permute-start | bytes 12296 | tf_op jit(solution)/shard_map/ppermute | solution.py:419
  26.2 4.4 %collective-permute-done.10.turned_ref = f32[8,128]{1,0:T(8,128)S(1)} collective-permute-done((f32[8,128]{1,0:T(8,128)S(1)}, f32[8,128]{1,0:T(8,128)S(1)}, u32[]{:S(2)}, u32[]{:S(2)}) %collective-permute-start.10) | collective-permute-done | bytes 4128 | tf_op jit(solution)/shard_map/ppermute | solution.py:452
  30.6 0.0 collective-permute-start.11
  30.6 0.0 collective-permute-done.12.x_ref
  30.6 1.2 %collective-permute-done.11.mate_ref = f32[8,128]{1,0:T(8,128)S(1)} collective-permute-done((f32[8,128]{1,0:T(8,128)S(1)}, f32[8,128]{1,0:T(8,128)S(1)}, u32[]{:S(2)}, u32[]{:S(2)}) %collective-permute-start.11) | collective-permute-done | bytes 4128 | tf_op jit(solution)/shard_map/ppermute | solution.py:419
  31.8 0.6 %total.1 = f32[3,128]{1,0:T(4,128)} custom-call(f32[8,128]{1,0:T(8,128)S(1)} %get-tuple-element.12.own_ref, f32[8,128]{1,0:T(8,128)S(1)} %collective-permute-done.10.turned_ref, f32[8,128]{1,0:T(8,128)S(1)} %collective-permute-done.11.mate_ref, f32[8,128]{1,0:T(8,128)S(1)} %collective-permute-done.12.x_ref), custom_call_target="tpu_custom_call" | custom-call | flops 1048576 | bytes 1048576 | tf_op jit(solution)/shard_map/total/pallas_call | solution.py:78
  (8 shorter events, 0.0 us)
Async XLA Ops:
  0.0 6.3 %collective-permute-start.2 = (bf16[128,4096]{1,0:T(8,128)(2,1)}, bf16[128,4096]{1,0:T(8,128)(2,1)S(1)}, u32[]{:S(2)}, u32[]{:S(2)}) collective-permute-start(bf16[128,4096]{1,0:T(8,128)(2,1)} %refs_0_.1), channel_id=1, source_target_pairs={{0,1},{1,0},{2,3},{3,2},{4,5},{5,4},{6,7},{7,6},{8,9},{9,8},{10,11... | collective-permute-start | bytes 3145736 | tf_op jit(solution)/shard_map/ppermute | solution.py:456
  0.7 0.7 %copy-start.3 = (bf16[24,128]{1,0:T(8,128)(2,1)S(1)}, bf16[24,128]{1,0:T(8,128)(2,1)}, u32[]{:S(2)}) copy-start(bf16[24,128]{1,0:T(8,128)(2,1)} %fraction_ref.1) | copy-start | bytes 18436
  0.7 0.7 %copy-start.4 = (f32[3,128]{1,0:T(4,128)S(1)}, f32[3,128]{1,0:T(4,128)}, u32[]{:S(2)}) copy-start(f32[3,128]{1,0:T(4,128)} %displacement_ref.1) | copy-start | bytes 4612
  0.7 0.7 %copy-start.5 = (s32[3,128]{1,0:T(4,128)S(1)}, s32[3,128]{1,0:T(4,128)}, u32[]{:S(2)}) copy-start(s32[3,128]{1,0:T(4,128)} %offset_ref.1) | copy-start | bytes 4612
  0.7 0.7 %copy-start.6 = (s32[128]{0:T(128)S(1)}, s32[128]{0:T(128)}, u32[]{:S(2)}) copy-start(s32[128]{0:T(128)} %param.15) | copy-start | bytes 1540
  0.7 5.6 %copy-start = (bf16[128,4096]{1,0:T(8,128)(2,1)S(1)}, bf16[128,4096]{1,0:T(8,128)(2,1)}, u32[]{:S(2)}) copy-start(bf16[128,4096]{1,0:T(8,128)(2,1)} %refs_0_.1) | copy-start | bytes 3145732
  0.7 5.5 %collective-permute-start.1 = (s32[4,128]{1,0:T(4,128)}, s32[4,128]{1,0:T(4,128)S(1)}, u32[]{:S(2)}, u32[]{:S(2)}) collective-permute-start(s32[4,128]{1,0:T(4,128)} %bitcast.5), channel_id=1, source_target_pairs={{0,1},{1,0},{2,3},{3,2},{4,5},{5,4},{6,7},{7,6},{8,9},{9,8},{10,11... | collective-permute-start | bytes 6152 | tf_op jit(solution)/shard_map/ppermute | solution.py:456
  1.4 5.5 %collective-permute-start = (f32[32,128]{1,0:T(8,128)S(1)}, f32[32,128]{1,0:T(8,128)S(1)}, u32[]{:S(2)}, u32[]{:S(2)}) collective-permute-start(f32[32,128]{1,0:T(8,128)S(1)} %pack.1.after_ref.refs_0_.meta_ref), channel_id=1, source_target_pairs={{0,2},{2,4},{4,6},{6,0},{1,3},{3,5},{5,7},{7,1},{8,10},{10,12},{12... | collective-permute-start | bytes 49160 | tf_op jit(solution)/shard_map/ppermute | solution.py:419
  2.7 5.8 %collective-permute-start.5 = (f32[32,128]{1,0:T(8,128)S(1)}, f32[32,128]{1,0:T(8,128)S(1)}, u32[]{:S(2)}, u32[]{:S(2)}) collective-permute-start(f32[32,128]{1,0:T(8,128)S(1)} %pack.1.after_ref.refs_0_.meta_ref), channel_id=1, source_target_pairs={{0,4},{2,6},{4,0},{6,2},{1,5},{3,7},{5,1},{7,3},{8,12},{10,14},{12... | collective-permute-start | bytes 49160 | tf_op jit(solution)/shard_map/ppermute | solution.py:419
  5.1 5.8 %collective-permute-start.4 = (f32[32,128]{1,0:T(8,128)S(1)}, f32[32,128]{1,0:T(8,128)S(1)}, u32[]{:S(2)}, u32[]{:S(2)}) collective-permute-start(f32[32,128]{1,0:T(8,128)S(1)} %pack.1.after_ref.refs_0_.meta_ref), channel_id=1, source_target_pairs={{0,6},{2,0},{4,2},{6,4},{1,7},{3,1},{5,3},{7,5},{8,14},{10,8},{12,... | collective-permute-start | bytes 49160 | tf_op jit(solution)/shard_map/ppermute | solution.py:419
  6.2 0.7 %copy-start.7 = (s32[512]{0:T(512)S(1)}, s32[512]{0:T(512)}, u32[]{:S(2)}) copy-start(s32[512]{0:T(512)} %param.14) | copy-start | bytes 6148
  8.0 4.1 %collective-permute-start.3 = (bf16[128,512]{1,0:T(8,128)(2,1)S(1)}, bf16[128,512]{1,0:T(8,128)(2,1)S(1)}, u32[]{:S(2)}, u32[]{:S(2)}) collective-permute-start(bf16[128,512]{1,0:T(8,128)(2,1)S(1)} %interpolate.4.rest_0_), channel_id=1, source_target_pairs={{0,6},{2,0},{4,2},{6,4},{1,7},{3,1},{5,3},{7,5},{8,14},{10,8},{12,... | collective-permute-start | bytes 393224 | tf_op jit(solution)/shard_map/ppermute | solution.py:419
  9.7 12.1 %collective-permute-start.7 = (bf16[128,512]{1,0:T(8,128)(2,1)S(1)}, bf16[128,512]{1,0:T(8,128)(2,1)S(1)}, u32[]{:S(2)}, u32[]{:S(2)}) collective-permute-start(bf16[128,512]{1,0:T(8,128)(2,1)S(1)} %interpolate.5.rest_0_), channel_id=1, source_target_pairs={{0,4},{2,6},{4,0},{6,2},{1,5},{3,7},{5,1},{7,3},{8,12},{10,14},{12... | collective-permute-start | bytes 393224 | tf_op jit(solution)/shard_map/ppermute | solution.py:419
  12.0 6.4 %collective-permute-start.8 = (bf16[128,512]{1,0:T(8,128)(2,1)S(1)}, bf16[128,512]{1,0:T(8,128)(2,1)S(1)}, u32[]{:S(2)}, u32[]{:S(2)}) collective-permute-start(bf16[128,512]{1,0:T(8,128)(2,1)S(1)} %interpolate.6.rest_0_), channel_id=1, source_target_pairs={{0,2},{2,4},{4,6},{6,0},{1,3},{3,5},{5,7},{7,1},{8,10},{10,12},{12... | collective-permute-start | bytes 393224 | tf_op jit(solution)/shard_map/ppermute | solution.py:419
  12.2 2.4 %copy-start.2 = (bf16[128,512]{1,0:T(8,128)(2,1)S(1)}, bf16[128,512]{1,0:T(8,128)(2,1)}, u32[]{:S(2)}) copy-start(bf16[128,512]{1,0:T(8,128)(2,1)} %image_ref.1) | copy-start | bytes 393220
  12.2 9.6 %copy-start.1 = (bf16[3,128,512]{2,1,0:T(8,128)(2,1)S(1)}, bf16[3,128,512]{2,1,0:T(8,128)(2,1)}, u32[]{:S(2)}) copy-start(bf16[3,128,512]{2,1,0:T(8,128)(2,1)} %slope_ref.1) | copy-start | bytes 1179652
  12.2 2.6 %collective-permute-start.6 = (f32[4,8,128]{2,1,0:T(8,128)S(1)}, f32[4,8,128]{2,1,0:T(8,128)S(1)}, u32[]{:S(2)}, u32[]{:S(2)}) collective-permute-start(f32[4,8,128]{2,1,0:T(8,128)S(1)} %collect.1.own_ref), channel_id=1, source_target_pairs={{0,24},{8,0},{16,8},{24,16},{1,25},{9,1},{17,9},{25,17},{2,26},{10... | collective-permute-start | bytes 49160 | tf_op jit(solution)/shard_map/ppermute | solution.py:419
  22.5 1.8 %collective-permute-start.9 = (f32[48,128]{1,0:T(8,128)S(1)}, f32[48,128]{1,0:T(8,128)S(1)}, u32[]{:S(2)}, u32[]{:S(2)}) collective-permute-start(f32[48,128]{1,0:T(8,128)S(1)} %forces.1.here_ref), channel_id=1, source_target_pairs={{0,1},{1,0},{2,3},{3,2},{4,5},{5,4},{6,7},{7,6},{8,9},{9,8},{10,11... | collective-permute-start | bytes 73736 | tf_op jit(solution)/shard_map/ppermute | solution.py:419
  24.5 6.1 %collective-permute-start.10 = (f32[8,128]{1,0:T(8,128)S(1)}, f32[8,128]{1,0:T(8,128)S(1)}, u32[]{:S(2)}, u32[]{:S(2)}) collective-permute-start(f32[8,128]{1,0:T(8,128)S(1)} %get-tuple-element.13), channel_id=1, source_target_pairs={{0,2},{1,11},{2,4},{3,13},{4,6},{5,15},{8,10},{9,19},{10,12},{11,2... | collective-permute-start | bytes 12296 | tf_op jit(solution)/shard_map/ppermute | solution.py:452
  24.8 5.8 %collective-permute-start.12 = (f32[8,128]{1,0:T(8,128)S(1)}, f32[8,128]{1,0:T(8,128)S(1)}, u32[]{:S(2)}, u32[]{:S(2)}) collective-permute-start(f32[8,128]{1,0:T(8,128)S(1)} %get-tuple-element.14), channel_id=1, source_target_pairs={{0,8},{8,16},{16,24},{24,0},{1,9},{9,17},{17,25},{25,1},{2,10},{10... | collective-permute-start | bytes 12296 | tf_op jit(solution)/shard_map/ppermute | solution.py:419
  30.6 1.2 %collective-permute-start.11 = (f32[8,128]{1,0:T(8,128)S(1)}, f32[8,128]{1,0:T(8,128)S(1)}, u32[]{:S(2)}, u32[]{:S(2)}) collective-permute-start(f32[8,128]{1,0:T(8,128)S(1)} %collective-permute-done.10.turned_ref), channel_id=1, source_target_pairs={{0,1},{1,0},{2,3},{3,2},{4,5},{5,4},{6,7},{7,6},{8,9},{9,8},{10,11... | collective-permute-start | bytes 12296 | tf_op jit(solution)/shard_map/ppermute | solution.py:419

commit v9 on v8

--- a/solution.py
+++ b/solution.py
@@ -509,7 +509,7 @@
             )
             arrived[d] = ring(samples, "gy", d) if d else samples
             previous = [samples]
-        (column,) = small_call(collect_kernel, [(n_y, 8, LANES)], "collect", arrived[n_y - 1], *metas)
+        (column,) = small_call(collect_kernel, [(n_y, 8, LANES)], "collect", previous[0], *metas)
         stiff, across = small_call(
             column_kernel, [(8, LANES)] * 2, "stiffness", column, ring(column, "gx", -1)
         )

time: 32.5 us -> 32.4 us (level)
    ppermute x10, starting transfers between devices: 10.1 us -> 9.78 us  [ring(): lax.ppermute(value, axes, [(i, (i + distance) % count) for i in range(cou...]
    ppermute x1, starting transfers between devices: 0.28 us -> 0.61 us  [turned_ring(): lax.ppermute(value, ('gx', 'gy', 'gz'), route + list(zip(sources, targets)))]
where the time goes in v9:
time: 32.4 us; the launch traced here: 32.2 us
  waiting for transfers between devices  13.1 us (40%)
  starting transfers between devices  11.1 us (34%)
  Pallas kernels  7.27 us (22%)
  local copies, waits for them, and re-layouts  0.51 us (2%)
    ppermute x10, starting transfers between devices, ring(): lax.ppermute(value, axes, [(i, (i + distance) % count) for i in range(cou...  9.78 us
    ppermute x10, waiting for transfers between devices, ring(): lax.ppermute(value, axes, [(i, (i + distance) % count) for i in range(cou...  8.69 us
    pallas_call x4, Pallas kernels, sample_call(): pl.pallas_call(kernel, out_shape=jax.ShapeDtypeStruct((LANES, 512), jnp.b...  4.52 us
    ppermute x1, waiting for transfers between devices, turned_ring(): lax.ppermute(value, ('gx', 'gy', 'gz'), route + list(zip(sources, targets)))  4.41 us
    pallas_call x9, Pallas kernels, vmem_call(): pl.pallas_call(kernel, out_shape=[jax.ShapeDtypeStruct(shape, dtype) for...  2.75 us
    ppermute x2, starting transfers between devices, swapped(): lax.ppermute(value, axes, [(i, i ^ mask) for i in range(lax.axis_size(axe...  0.76 us
  transfers between devices with their start and end apart: 13, of which 6 were waited for; matrix products, arithmetic and copies ran while one was open for 0% of the time, Pallas kernels for 18%

profile of v9, /device:TPU:5, one launch (start us, length us, event | category | flops | bytes accessed | tf_op | source)
XLA Modules:
  0.0 32.2 jit_solution(15277630406356462206)
XLA Ops:
  0.0 0.7 %collective-permute-start.1 = (bf16[128,4096]{1,0:T(8,128)(2,1)}, bf16[128,4096]{1,0:T(8,128)(2,1)S(1)}, u32[]{:S(2)}, u32[]{:S(2)}) collective-permute-start(bf16[128,4096]{1,0:T(8,128)(2,1)} %refs_0_.1), channel_id=1, source_target_pairs={{0,1},{1,0},{2,3},{3,2},{4,5},{5,4},{6,7},{7,6},{8,9},{9,8},{10,11... | collective-permute-start | bytes 3145736 | tf_op jit(solution)/shard_map/ppermute | solution.py:456
  0.7 0.0 copy-start
  0.7 0.1 collective-permute-start
  0.8 0.2 shapes.1.after_ref.shape_ref
  1.0 0.3 %copy-done.3 = bf16[24,128]{1,0:T(8,128)(2,1)S(1)} copy-done((bf16[24,128]{1,0:T(8,128)(2,1)S(1)}, bf16[24,128]{1,0:T(8,128)(2,1)}, u32[]{:S(2)}) %copy-start.3) | copy-done | bytes 6168
  1.4 0.0 copy-done.4
  1.4 0.0 copy-done.5
  1.4 0.0 copy-done.6
  1.4 1.3 %collective-permute-start.4 = (f32[32,128]{1,0:T(8,128)S(1)}, f32[32,128]{1,0:T(8,128)S(1)}, u32[]{:S(2)}, u32[]{:S(2)}) collective-permute-start(f32[32,128]{1,0:T(8,128)S(1)} %pack.1.after_ref.meta_ref.refs_0_), channel_id=1, source_target_pairs={{0,2},{2,4},{4,6},{6,0},{1,3},{3,5},{5,7},{7,1},{8,10},{10,12},{12... | collective-permute-start | bytes 49160 | tf_op jit(solution)/shard_map/ppermute | solution.py:419
  2.8 2.3 %collective-permute-start.3 = (f32[32,128]{1,0:T(8,128)S(1)}, f32[32,128]{1,0:T(8,128)S(1)}, u32[]{:S(2)}, u32[]{:S(2)}) collective-permute-start(f32[32,128]{1,0:T(8,128)S(1)} %pack.1.after_ref.meta_ref.refs_0_), channel_id=1, source_target_pairs={{0,4},{2,6},{4,0},{6,2},{1,5},{3,7},{5,1},{7,3},{8,12},{10,14},{12... | collective-permute-start | bytes 49160 | tf_op jit(solution)/shard_map/ppermute | solution.py:419
  5.1 1.1 %collective-permute-start.2 = (f32[32,128]{1,0:T(8,128)S(1)}, f32[32,128]{1,0:T(8,128)S(1)}, u32[]{:S(2)}, u32[]{:S(2)}) collective-permute-start(f32[32,128]{1,0:T(8,128)S(1)} %pack.1.after_ref.meta_ref.refs_0_), channel_id=1, source_target_pairs={{0,6},{2,0},{4,2},{6,4},{1,7},{3,1},{5,3},{7,5},{8,14},{10,8},{12,... | collective-permute-start | bytes 49160 | tf_op jit(solution)/shard_map/ppermute | solution.py:419
  6.1 0.0 collective-permute-done.later_ref.mate_ref
  6.1 0.0 collective-permute-done.1.refs_1_
  6.1 0.0 copy-done
  6.1 0.6 %table.1.table_ref = bf16[4096,256]{1,0:T(8,128)(2,1)S(1)} custom-call(f32[32,128]{1,0:T(8,128)S(1)} %pack.1.after_ref.meta_ref.refs_0_, s32[4,128]{1,0:T(4,128)S(1)} %collective-permute-done.later_ref.mate_ref, bf16[128,4096]{1,0:T(8,128)(2,1)S(1)} %copy-done, bf16[128,4096]{1,0:T(8,128)(2,1)S(1)} %collective-permute-done.1.refs_1_), custom_call_target="tpu_custom_call" | custom-call | flops 805306368 | bytes 1048576 | tf_op jit(solution)/shard_map/table/pallas_call | solution.py:78
  6.7 0.0 collective-permute-done.4.meta_ref.refs_3_
  6.8 0.0 copy-done.7
  6.8 1.1 %interpolate.4.rest_0_ = bf16[128,512]{1,0:T(8,128)(2,1)S(1)} custom-call(f32[32,128]{1,0:T(8,128)S(1)} %collective-permute-done.4.meta_ref.refs_3_, bf16[4096,256]{1,0:T(8,128)(2,1)S(1)} %table.1.table_ref, s32[4,128]{1,0:T(4,128)S(1)} %bitcast.6, s32[4,128]{1,0:T(4,128)S(1)} %collective-permute-done.later_ref.mate_ref), custom_call_target="tpu_custom_call" | custom-call | flops 4000000000 | bytes 1 | tf_op jit(solution)/shard_map/interpolate/pallas_call | solution.py:165
  7.9 0.7 %collective-permute-start.6 = (bf16[128,512]{1,0:T(8,128)(2,1)S(1)}, bf16[128,512]{1,0:T(8,128)(2,1)S(1)}, u32[]{:S(2)}, u32[]{:S(2)}) collective-permute-start(bf16[128,512]{1,0:T(8,128)(2,1)S(1)} %interpolate.4.rest_0_), channel_id=1, source_target_pairs={{0,6},{2,0},{4,2},{6,4},{1,7},{3,1},{5,3},{7,5},{8,14},{10,8},{12,... | collective-permute-start | bytes 393224 | tf_op jit(solution)/shard_map/ppermute | solution.py:419
  8.6 0.0 collective-permute-done.3.meta_ref.refs_2_
  8.6 1.1 %interpolate.5.rest_0_ = bf16[128,512]{1,0:T(8,128)(2,1)S(1)} custom-call(f32[32,128]{1,0:T(8,128)S(1)} %collective-permute-done.3.meta_ref.refs_2_, bf16[4096,256]{1,0:T(8,128)(2,1)S(1)} %table.1.table_ref, s32[4,128]{1,0:T(4,128)S(1)} %bitcast.7, s32[4,128]{1,0:T(4,128)S(1)} %collective-permute-done.later_ref.mate_ref, bf16[128,512]{1,0:T(8,128)(2,1)S(1)} %interpolate.4.rest_0_), custom_call_target="tpu_custom_call" | custom-call | flops 4000000000 | bytes 1 | tf_op jit(solution)/shard_map/interpolate/pallas_call | solution.py:165
  9.7 1.0 %collective-permute-start.7 = (bf16[128,512]{1,0:T(8,128)(2,1)S(1)}, bf16[128,512]{1,0:T(8,128)(2,1)S(1)}, u32[]{:S(2)}, u32[]{:S(2)}) collective-permute-start(bf16[128,512]{1,0:T(8,128)(2,1)S(1)} %interpolate.5.rest_0_), channel_id=1, source_target_pairs={{0,4},{2,6},{4,0},{6,2},{1,5},{3,7},{5,1},{7,3},{8,12},{10,14},{12... | collective-permute-start | bytes 393224 | tf_op jit(solution)/shard_map/ppermute | solution.py:419
  10.7 0.0 collective-permute-done.2.meta_ref.refs_1_
  10.7 1.1 %interpolate.6.rest_0_ = bf16[128,512]{1,0:T(8,128)(2,1)S(1)} custom-call(f32[32,128]{1,0:T(8,128)S(1)} %collective-permute-done.2.meta_ref.refs_1_, bf16[4096,256]{1,0:T(8,128)(2,1)S(1)} %table.1.table_ref, s32[4,128]{1,0:T(4,128)S(1)} %bitcast.8, s32[4,128]{1,0:T(4,128)S(1)} %collective-permute-done.later_ref.mate_ref, bf16[128,512]{1,0:T(8,128)(2,1)S(1)} %interpolate.5.rest_0_), custom_call_target="tpu_custom_call" | custom-call | flops 4000000000 | bytes 1 | tf_op jit(solution)/shard_map/interpolate/pallas_call | solution.py:165
  11.9 0.0 copy-start.2
  11.9 0.0 copy-start.1
  11.9 0.1 collective-permute-start.8
  12.0 1.1 %interpolate.7.after_ref.rest_0_ = bf16[128,512]{1,0:T(8,128)(2,1)S(1)} custom-call(f32[32,128]{1,0:T(8,128)S(1)} %pack.1.after_ref.meta_ref.refs_0_, bf16[4096,256]{1,0:T(8,128)(2,1)S(1)} %table.1.table_ref, s32[4,128]{1,0:T(4,128)S(1)} %bitcast.9, s32[4,128]{1,0:T(4,128)S(1)} %collective-permute-done.later_ref.mate_ref, ...), custom_call_target="tpu_custom_call" | custom-call | flops 4000000000 | bytes 1 | tf_op jit(solution)/shard_map/interpolate/pallas_call | solution.py:165
  13.2 1.2 %collective-permute-start.5 = (f32[4,8,128]{2,1,0:T(8,128)S(1)}, f32[4,8,128]{2,1,0:T(8,128)S(1)}, u32[]{:S(2)}, u32[]{:S(2)}) collective-permute-start(f32[4,8,128]{2,1,0:T(8,128)S(1)} %collect.1.own_ref), channel_id=1, source_target_pairs={{0,24},{8,0},{16,8},{24,16},{1,25},{9,1},{17,9},{25,17},{2,26},{10... | collective-permute-start | bytes 49160 | tf_op jit(solution)/shard_map/ppermute | solution.py:419
  14.4 0.1 copy.10.slot_ref
  14.5 1.6 %collective-permute-done.5.above_ref = f32[4,8,128]{2,1,0:T(8,128)S(1)} collective-permute-done((f32[4,8,128]{2,1,0:T(8,128)S(1)}, f32[4,8,128]{2,1,0:T(8,128)S(1)}, u32[]{:S(2)}, u32[]{:S(2)}) %collective-permute-start.5) | collective-permute-done | bytes 16416 | tf_op jit(solution)/shard_map/ppermute | solution.py:419
  16.1 0.2 stiffness.1
  16.3 0.0 collective-permute-done.6.rest_1_
  16.3 0.0 copy-done.2
  16.3 0.2 early.1.base_ref
  16.6 1.7 %collective-permute-done.8.rest_1_ = bf16[128,512]{1,0:T(8,128)(2,1)S(1)} collective-permute-done((bf16[128,512]{1,0:T(8,128)(2,1)S(1)}, bf16[128,512]{1,0:T(8,128)(2,1)S(1)}, u32[]{:S(2)}, u32[]{:S(2)}) %collective-permute-start.8) | collective-permute-done | bytes 131104 | tf_op jit(solution)/shard_map/ppermute | solution.py:419
  18.2 3.4 %collective-permute-done.7.rest_0_ = bf16[128,512]{1,0:T(8,128)(2,1)S(1)} collective-permute-done((bf16[128,512]{1,0:T(8,128)(2,1)S(1)}, bf16[128,512]{1,0:T(8,128)(2,1)S(1)}, u32[]{:S(2)}, u32[]{:S(2)}) %collective-permute-start.7) | collective-permute-done | bytes 131104 | tf_op jit(solution)/shard_map/ppermute | solution.py:419
  21.6 0.8 %forces.1.here_ref = f32[48,128]{1,0:T(8,128)S(1)} custom-call(f32[8,128]{1,0:T(8,128)S(1)} %get-tuple-element.10.across_ref, s32[128,1]{1,0:T(8,128)S(1)} %copy.10.slot_ref, f32[128,512]{1,0:T(8,128)S(1)} %early.1.base_ref, bf16[3,128,512]{2,1,0:T(8,128)(2,1)S(1)} %copy-done.1, bf16[512,128]{1,0:T(8,128)(2,1)S(1)} %shapes.1.after_ref.shape_ref, ...), custom_call_target="tpu_custom_call" | custom-call | flops 1048576 | bytes 1048576 | tf_op jit(solution)/shard_map/forces/pallas_call | solution.py:78
  22.4 0.9 %collective-permute-start.9 = (f32[48,128]{1,0:T(8,128)S(1)}, f32[48,128]{1,0:T(8,128)S(1)}, u32[]{:S(2)}, u32[]{:S(2)}) collective-permute-start(f32[48,128]{1,0:T(8,128)S(1)} %forces.1.here_ref), channel_id=1, source_target_pairs={{0,1},{1,0},{2,3},{3,2},{4,5},{5,4},{6,7},{7,6},{8,9},{9,8},{10,11... | collective-permute-start | bytes 73736 | tf_op jit(solution)/shard_map/ppermute | solution.py:419
  23.3 0.8 %collective-permute-done.9.mate_ref = f32[48,128]{1,0:T(8,128)S(1)} collective-permute-done((f32[48,128]{1,0:T(8,128)S(1)}, f32[48,128]{1,0:T(8,128)S(1)}, u32[]{:S(2)}, u32[]{:S(2)}) %collective-permute-start.9) | collective-permute-done | bytes 24608 | tf_op jit(solution)/shard_map/ppermute | solution.py:419
  24.2 0.2 layers.1
  24.3 0.6 %collective-permute-start.10 = (f32[8,128]{1,0:T(8,128)S(1)}, f32[8,128]{1,0:T(8,128)S(1)}, u32[]{:S(2)}, u32[]{:S(2)}) collective-permute-start(f32[8,128]{1,0:T(8,128)S(1)} %get-tuple-element.13), channel_id=1, source_target_pairs={{0,2},{1,11},{2,4},{3,13},{4,6},{5,15},{8,10},{9,19},{10,12},{11,2... | collective-permute-start | bytes 12296 | tf_op jit(solution)/shard_map/ppermute | solution.py:452
  24.9 1.1 %collective-permute-start.12 = (f32[8,128]{1,0:T(8,128)S(1)}, f32[8,128]{1,0:T(8,128)S(1)}, u32[]{:S(2)}, u32[]{:S(2)}) collective-permute-start(f32[8,128]{1,0:T(8,128)S(1)} %get-tuple-element.14), channel_id=1, source_target_pairs={{0,8},{8,16},{16,24},{24,0},{1,9},{9,17},{17,25},{25,1},{2,10},{10... | collective-permute-start | bytes 12296 | tf_op jit(solution)/shard_map/ppermute | solution.py:419
  26.0 4.4 %collective-permute-done.10.turned_ref = f32[8,128]{1,0:T(8,128)S(1)} collective-permute-done((f32[8,128]{1,0:T(8,128)S(1)}, f32[8,128]{1,0:T(8,128)S(1)}, u32[]{:S(2)}, u32[]{:S(2)}) %collective-permute-start.10) | collective-permute-done | bytes 4128 | tf_op jit(solution)/shard_map/ppermute | solution.py:452
  30.4 0.0 collective-permute-start.11
  30.4 0.0 collective-permute-done.12.x_ref
  30.4 1.2 %collective-permute-done.11.mate_ref = f32[8,128]{1,0:T(8,128)S(1)} collective-permute-done((f32[8,128]{1,0:T(8,128)S(1)}, f32[8,128]{1,0:T(8,128)S(1)}, u32[]{:S(2)}, u32[]{:S(2)}) %collective-permute-start.11) | collective-permute-done | bytes 4128 | tf_op jit(solution)/shard_map/ppermute | solution.py:419
  31.6 0.6 %total.1 = f32[3,128]{1,0:T(4,128)} custom-call(f32[8,128]{1,0:T(8,128)S(1)} %get-tuple-element.12.own_ref, f32[8,128]{1,0:T(8,128)S(1)} %collective-permute-done.10.turned_ref, f32[8,128]{1,0:T(8,128)S(1)} %collective-permute-done.11.mate_ref, f32[8,128]{1,0:T(8,128)S(1)} %collective-permute-done.12.x_ref), custom_call_target="tpu_custom_call" | custom-call | flops 1048576 | bytes 1048576 | tf_op jit(solution)/shard_map/total/pallas_call | solution.py:78
  (8 shorter events, 0.0 us)
Async XLA Ops:
  0.0 6.1 %collective-permute-start.1 = (bf16[128,4096]{1,0:T(8,128)(2,1)}, bf16[128,4096]{1,0:T(8,128)(2,1)S(1)}, u32[]{:S(2)}, u32[]{:S(2)}) collective-permute-start(bf16[128,4096]{1,0:T(8,128)(2,1)} %refs_0_.1), channel_id=1, source_target_pairs={{0,1},{1,0},{2,3},{3,2},{4,5},{5,4},{6,7},{7,6},{8,9},{9,8},{10,11... | collective-permute-start | bytes 3145736 | tf_op jit(solution)/shard_map/ppermute | solution.py:456
  0.7 0.7 %copy-start.3 = (bf16[24,128]{1,0:T(8,128)(2,1)S(1)}, bf16[24,128]{1,0:T(8,128)(2,1)}, u32[]{:S(2)}) copy-start(bf16[24,128]{1,0:T(8,128)(2,1)} %fraction_ref.1) | copy-start | bytes 18436
  0.7 0.7 %copy-start.4 = (f32[3,128]{1,0:T(4,128)S(1)}, f32[3,128]{1,0:T(4,128)}, u32[]{:S(2)}) copy-start(f32[3,128]{1,0:T(4,128)} %displacement_ref.1) | copy-start | bytes 4612
  0.7 0.7 %copy-start.5 = (s32[3,128]{1,0:T(4,128)S(1)}, s32[3,128]{1,0:T(4,128)}, u32[]{:S(2)}) copy-start(s32[3,128]{1,0:T(4,128)} %offset_ref.1) | copy-start | bytes 4612
  0.7 0.7 %copy-start.6 = (s32[128]{0:T(128)S(1)}, s32[128]{0:T(128)}, u32[]{:S(2)}) copy-start(s32[128]{0:T(128)} %param.15) | copy-start | bytes 1540
  0.7 5.5 %copy-start = (bf16[128,4096]{1,0:T(8,128)(2,1)S(1)}, bf16[128,4096]{1,0:T(8,128)(2,1)}, u32[]{:S(2)}) copy-start(bf16[128,4096]{1,0:T(8,128)(2,1)} %refs_0_.1) | copy-start | bytes 3145732
  0.7 5.4 %collective-permute-start = (s32[4,128]{1,0:T(4,128)}, s32[4,128]{1,0:T(4,128)S(1)}, u32[]{:S(2)}, u32[]{:S(2)}) collective-permute-start(s32[4,128]{1,0:T(4,128)} %bitcast.5), channel_id=1, source_target_pairs={{0,1},{1,0},{2,3},{3,2},{4,5},{5,4},{6,7},{7,6},{8,9},{9,8},{10,11... | collective-permute-start | bytes 6152 | tf_op jit(solution)/shard_map/ppermute | solution.py:456
  1.4 5.4 %copy-start.7 = (s32[512]{0:T(512)S(1)}, s32[512]{0:T(512)}, u32[]{:S(2)}) copy-start(s32[512]{0:T(512)} %param.14) | copy-start | bytes 6148
  1.4 5.3 %collective-permute-start.4 = (f32[32,128]{1,0:T(8,128)S(1)}, f32[32,128]{1,0:T(8,128)S(1)}, u32[]{:S(2)}, u32[]{:S(2)}) collective-permute-start(f32[32,128]{1,0:T(8,128)S(1)} %pack.1.after_ref.meta_ref.refs_0_), channel_id=1, source_target_pairs={{0,2},{2,4},{4,6},{6,0},{1,3},{3,5},{5,7},{7,1},{8,10},{10,12},{12... | collective-permute-start | bytes 49160 | tf_op jit(solution)/shard_map/ppermute | solution.py:419
  2.8 5.8 %collective-permute-start.3 = (f32[32,128]{1,0:T(8,128)S(1)}, f32[32,128]{1,0:T(8,128)S(1)}, u32[]{:S(2)}, u32[]{:S(2)}) collective-permute-start(f32[32,128]{1,0:T(8,128)S(1)} %pack.1.after_ref.meta_ref.refs_0_), channel_id=1, source_target_pairs={{0,4},{2,6},{4,0},{6,2},{1,5},{3,7},{5,1},{7,3},{8,12},{10,14},{12... | collective-permute-start | bytes 49160 | tf_op jit(solution)/shard_map/ppermute | solution.py:419
  5.1 5.7 %collective-permute-start.2 = (f32[32,128]{1,0:T(8,128)S(1)}, f32[32,128]{1,0:T(8,128)S(1)}, u32[]{:S(2)}, u32[]{:S(2)}) collective-permute-start(f32[32,128]{1,0:T(8,128)S(1)} %pack.1.after_ref.meta_ref.refs_0_), channel_id=1, source_target_pairs={{0,6},{2,0},{4,2},{6,4},{1,7},{3,1},{5,3},{7,5},{8,14},{10,8},{12,... | collective-permute-start | bytes 49160 | tf_op jit(solution)/shard_map/ppermute | solution.py:419
  7.9 8.4 %collective-permute-start.6 = (bf16[128,512]{1,0:T(8,128)(2,1)S(1)}, bf16[128,512]{1,0:T(8,128)(2,1)S(1)}, u32[]{:S(2)}, u32[]{:S(2)}) collective-permute-start(bf16[128,512]{1,0:T(8,128)(2,1)S(1)} %interpolate.4.rest_0_), channel_id=1, source_target_pairs={{0,6},{2,0},{4,2},{6,4},{1,7},{3,1},{5,3},{7,5},{8,14},{10,8},{12,... | collective-permute-start | bytes 393224 | tf_op jit(solution)/shard_map/ppermute | solution.py:419
  9.7 11.9 %collective-permute-start.7 = (bf16[128,512]{1,0:T(8,128)(2,1)S(1)}, bf16[128,512]{1,0:T(8,128)(2,1)S(1)}, u32[]{:S(2)}, u32[]{:S(2)}) collective-permute-start(bf16[128,512]{1,0:T(8,128)(2,1)S(1)} %interpolate.5.rest_0_), channel_id=1, source_target_pairs={{0,4},{2,6},{4,0},{6,2},{1,5},{3,7},{5,1},{7,3},{8,12},{10,14},{12... | collective-permute-start | bytes 393224 | tf_op jit(solution)/shard_map/ppermute | solution.py:419
  11.9 4.5 %copy-start.2 = (bf16[128,512]{1,0:T(8,128)(2,1)S(1)}, bf16[128,512]{1,0:T(8,128)(2,1)}, u32[]{:S(2)}) copy-start(bf16[128,512]{1,0:T(8,128)(2,1)} %image_ref.1) | copy-start | bytes 393220
  11.9 9.7 %copy-start.1 = (bf16[3,128,512]{2,1,0:T(8,128)(2,1)S(1)}, bf16[3,128,512]{2,1,0:T(8,128)(2,1)}, u32[]{:S(2)}) copy-start(bf16[3,128,512]{2,1,0:T(8,128)(2,1)} %slope_ref.1) | copy-start | bytes 1179652
  11.9 6.3 %collective-permute-start.8 = (bf16[128,512]{1,0:T(8,128)(2,1)S(1)}, bf16[128,512]{1,0:T(8,128)(2,1)S(1)}, u32[]{:S(2)}, u32[]{:S(2)}) collective-permute-start(bf16[128,512]{1,0:T(8,128)(2,1)S(1)} %interpolate.6.rest_0_), channel_id=1, source_target_pairs={{0,2},{2,4},{4,6},{6,0},{1,3},{3,5},{5,7},{7,1},{8,10},{10,12},{12... | collective-permute-start | bytes 393224 | tf_op jit(solution)/shard_map/ppermute | solution.py:419
  13.2 2.9 %collective-permute-start.5 = (f32[4,8,128]{2,1,0:T(8,128)S(1)}, f32[4,8,128]{2,1,0:T(8,128)S(1)}, u32[]{:S(2)}, u32[]{:S(2)}) collective-permute-start(f32[4,8,128]{2,1,0:T(8,128)S(1)} %collect.1.own_ref), channel_id=1, source_target_pairs={{0,24},{8,0},{16,8},{24,16},{1,25},{9,1},{17,9},{25,17},{2,26},{10... | collective-permute-start | bytes 49160 | tf_op jit(solution)/shard_map/ppermute | solution.py:419
  22.4 1.8 %collective-permute-start.9 = (f32[48,128]{1,0:T(8,128)S(1)}, f32[48,128]{1,0:T(8,128)S(1)}, u32[]{:S(2)}, u32[]{:S(2)}) collective-permute-start(f32[48,128]{1,0:T(8,128)S(1)} %forces.1.here_ref), channel_id=1, source_target_pairs={{0,1},{1,0},{2,3},{3,2},{4,5},{5,4},{6,7},{7,6},{8,9},{9,8},{10,11... | collective-permute-start | bytes 73736 | tf_op jit(solution)/shard_map/ppermute | solution.py:419
  24.3 6.1 %collective-permute-start.10 = (f32[8,128]{1,0:T(8,128)S(1)}, f32[8,128]{1,0:T(8,128)S(1)}, u32[]{:S(2)}, u32[]{:S(2)}) collective-permute-start(f32[8,128]{1,0:T(8,128)S(1)} %get-tuple-element.13), channel_id=1, source_target_pairs={{0,2},{1,11},{2,4},{3,13},{4,6},{5,15},{8,10},{9,19},{10,12},{11,2... | collective-permute-start | bytes 12296 | tf_op jit(solution)/shard_map/ppermute | solution.py:452
  24.9 5.5 %collective-permute-start.12 = (f32[8,128]{1,0:T(8,128)S(1)}, f32[8,128]{1,0:T(8,128)S(1)}, u32[]{:S(2)}, u32[]{:S(2)}) collective-permute-start(f32[8,128]{1,0:T(8,128)S(1)} %get-tuple-element.14), channel_id=1, source_target_pairs={{0,8},{8,16},{16,24},{24,0},{1,9},{9,17},{17,25},{25,1},{2,10},{10... | collective-permute-start | bytes 12296 | tf_op jit(solution)/shard_map/ppermute | solution.py:419
  30.4 1.2 %collective-permute-start.11 = (f32[8,128]{1,0:T(8,128)S(1)}, f32[8,128]{1,0:T(8,128)S(1)}, u32[]{:S(2)}, u32[]{:S(2)}) collective-permute-start(f32[8,128]{1,0:T(8,128)S(1)} %collective-permute-done.10.turned_ref), channel_id=1, source_target_pairs={{0,1},{1,0},{2,3},{3,2},{4,5},{5,4},{6,7},{7,6},{8,9},{9,8},{10,11... | collective-permute-start | bytes 12296 | tf_op jit(solution)/shard_map/ppermute | solution.py:419
